TPU v7x, 32 devices: a whole 2x2x4 slice. The times are simulated.
32 devices in a mesh: dp: 8 (over z, x), seq: 4 (over y, core).
Axes of the slice: x: 2, y: 2, z: 4, core: 2. Of those that a mesh axis runs over, the one named last changes fastest.
Arguments:
- latents: float32 [2, 16, 320, 16], P(None, 'dp', 'seq'), may hold values from -6 to 6
- noise_draw: float32 [2, 16, 320, 16], P(None, 'dp', 'seq'), may hold values from -6 to 6
- heights: int32 [2, 16], P(None, 'dp'), may hold values from 8 to 16, as said below
- widths: int32 [2, 16], P(None, 'dp'), may hold values from 1 to 20, as said below
- labels: int32 [2, 16], P(None, 'dp'), may hold values from 0 to 1000
- timesteps: int32 [2, 16], P(None, 'dp'), may hold values from 0 to 999
- bias_tiles: bfloat16 [2, 16, 16, 320, 320], P(None, 'dp', 'seq'), may hold values from -4 to 4
- param_embed: float32 [272, 1152], P(None, ('dp', 'seq')), may hold values from -0.75 to 0.75
- param_square: float32 [2, 1152, 1152], P(None, None, ('dp', 'seq')), may hold values from -0.375 to 0.375
- param_table: float32 [1001, 1152], P(None, ('dp', 'seq')), may hold values from -0.1875 to 0.1875
- param_shift: float32 [1152, 9216], P(None, ('dp', 'seq')), may hold values from -0.1875 to 0.1875
- param_attend: float32 [1152, 3456], P(None, ('dp', 'seq')), may hold values from -0.1875 to 0.1875
- param_expand: float32 [1152, 4608], P(None, ('dp', 'seq')), may hold values from -0.1875 to 0.1875
- param_reduce: float32 [4608, 1152], P(('dp', 'seq')), may hold values from -0.09375 to 0.09375
- param_final: float32 [1152, 16], P(('dp', 'seq')), may hold values from -0.1875 to 0.1875
- param_biases: float32 [21888], P(('dp', 'seq')), may hold values from -0.3125 to 0.3125
- first_embed: float32 [272, 1152], P(None, ('dp', 'seq')), may hold values from -0.00012207031 to 0.00012207031
- first_square: float32 [2, 1152, 1152], P(None, None, ('dp', 'seq')), may hold values from -0.00012207031 to 0.00012207031
- first_table: float32 [1001, 1152], P(None, ('dp', 'seq')), may hold values from -1.1444092e-05 to 1.1444092e-05
- first_shift: float32 [1152, 9216], P(None, ('dp', 'seq')), may hold values from -0.00012207031 to 0.00012207031
- first_attend: float32 [1152, 3456], P(None, ('dp', 'seq')), may hold values from -0.00012207031 to 0.00012207031
- first_expand: float32 [1152, 4608], P(None, ('dp', 'seq')), may hold values from -0.00012207031 to 0.00012207031
- first_reduce: float32 [4608, 1152], P(('dp', 'seq')), may hold values from -0.00012207031 to 0.00012207031
- first_final: float32 [1152, 16], P(('dp', 'seq')), may hold values from -0.00012207031 to 0.00012207031
- first_biases: float32 [21888], P(('dp', 'seq')), may hold values from -0.00036621094 to 0.00036621094
- second_embed: float32 [272, 1152], P(None, ('dp', 'seq')), may hold values from 8.8507623e-10 to 1.42973855e-08
- second_square: float32 [2, 1152, 1152], P(None, None, ('dp', 'seq')), may hold values from 8.8507623e-10 to 1.42973855e-08
- second_table: float32 [1001, 1152], P(None, ('dp', 'seq')), may hold values from 8.850762e-12 to 1.4297385e-10
- second_shift: float32 [1152, 9216], P(None, ('dp', 'seq')), may hold values from 8.8507623e-10 to 1.42973855e-08
- second_attend: float32 [1152, 3456], P(None, ('dp', 'seq')), may hold values from 8.8507623e-10 to 1.42973855e-08
- second_expand: float32 [1152, 4608], P(None, ('dp', 'seq')), may hold values from 8.8507623e-10 to 1.42973855e-08
- second_reduce: float32 [4608, 1152], P(('dp', 'seq')), may hold values from 8.8507623e-10 to 1.42973855e-08
- second_final: float32 [1152, 16], P(('dp', 'seq')), may hold values from 8.8507623e-10 to 1.42973855e-08
- second_biases: float32 [21888], P(('dp', 'seq')), may hold values from 8.169935e-09 to 1.293573e-07
Outputs:
- loss_total: float32 [], replicated
- value_count: float32 [], replicated
- grad_norm: float32 [], replicated
- new_param_embed: float32 [272, 1152], P(None, ('dp', 'seq'))
- new_param_square: float32 [2, 1152, 1152], P(None, None, ('dp', 'seq'))
- new_param_table: float32 [1001, 1152], P(None, ('dp', 'seq'))
- new_param_shift: float32 [1152, 9216], P(None, ('dp', 'seq'))
- new_param_attend: float32 [1152, 3456], P(None, ('dp', 'seq'))
- new_param_expand: float32 [1152, 4608], P(None, ('dp', 'seq'))
- new_param_reduce: float32 [4608, 1152], P(('dp', 'seq'))
- new_param_final: float32 [1152, 16], P(('dp', 'seq'))
- new_param_biases: float32 [21888], P(('dp', 'seq'))
- new_first_embed: float32 [272, 1152], P(None, ('dp', 'seq'))
- new_first_square: float32 [2, 1152, 1152], P(None, None, ('dp', 'seq'))
- new_first_table: float32 [1001, 1152], P(None, ('dp', 'seq'))
- new_first_shift: float32 [1152, 9216], P(None, ('dp', 'seq'))
- new_first_attend: float32 [1152, 3456], P(None, ('dp', 'seq'))
- new_first_expand: float32 [1152, 4608], P(None, ('dp', 'seq'))
- new_first_reduce: float32 [4608, 1152], P(('dp', 'seq'))
- new_first_final: float32 [1152, 16], P(('dp', 'seq'))
- new_first_biases: float32 [21888], P(('dp', 'seq'))
- new_second_embed: float32 [272, 1152], P(None, ('dp', 'seq'))
- new_second_square: float32 [2, 1152, 1152], P(None, None, ('dp', 'seq'))
- new_second_table: float32 [1001, 1152], P(None, ('dp', 'seq'))
- new_second_shift: float32 [1152, 9216], P(None, ('dp', 'seq'))
- new_second_attend: float32 [1152, 3456], P(None, ('dp', 'seq'))
- new_second_expand: float32 [1152, 4608], P(None, ('dp', 'seq'))
- new_second_reduce: float32 [4608, 1152], P(('dp', 'seq'))
- new_second_final: float32 [1152, 16], P(('dp', 'seq'))
- new_second_biases: float32 [21888], P(('dp', 'seq'))
Inputs may be any that keep to these rules, and one draw needn't show every extreme that they name: `heights`: in every micro-batch, one image of each aligned block of 2 images is 16 patches high and 20 wide. `widths`: height times width is at most 320.
All inputs are finite; a program needn't handle non-finite values.
Results may differ from a plain program's by a relative error of at most 0.011.
The roundings to bfloat16 on the way count: a program that leaves them out, or rounds other values in their place, can miss the bound.
Values may be sent and summed in bfloat16 or wider, within the bound.
No kernel may reach another device: no remote copies, remote signals or barrier semaphores. Data moves between devices by JAX's collectives and lax.ppermute only.
A program may use at most 384 MiB of HBM per device.

v0:
```python
import math

import jax
import jax.numpy as jnp
from jax import lax
from jax.sharding import PartitionSpec as P

D = 1152
HEADS = 16
HEAD = 72
FF = 4608
FREQ = 256
PIN = 16
MICRO = 2
TSTEPS = 1000
STEP = 10


BETA_ONE = 0.9
BETA_TWO = 0.95
EPSILON = 1e-08
DECAY = 0.1
RATE = 0.03
LIMIT = 1.0


def smooth_gate(values_in):
    return values_in * jax.nn.sigmoid(values_in)


def gaussian_unit(values_in):
    return (
        0.5
        * values_in
        * (
            1.0
            + jnp.tanh(
                0.7978845608028654 * (values_in + 0.044715 * values_in * values_in * values_in)
            )
        )
    )


def modnorm(stream, offset, stretch):
    centred = stream - jnp.mean(stream, -1, keepdims=True)
    spread = jnp.mean(centred * centred, -1, keepdims=True)
    return centred * lax.rsqrt(spread + 1e-06) * (1.0 + stretch[:, None, :]) + offset[:, None, :]


def time_freq(steps_in):
    half_freq = FREQ // 2
    rate_table = jnp.exp(-math.log(10000.0) * jnp.arange(half_freq).astype(jnp.float32) / half_freq)
    angles = steps_in.astype(jnp.float32)[:, None] * rate_table[None, :]
    return jnp.concatenate([jnp.cos(angles), jnp.sin(angles)], -1)


def signal_level(steps_in):
    angles = (steps_in.astype(jnp.float32) / TSTEPS + 0.008) / 1.008 * (math.pi / 2)
    return jnp.cos(angles) * jnp.cos(angles)


def place_embed(across, first_slot, slots):
    slot_ids = first_slot + jnp.arange(slots, dtype=jnp.int32)
    row_pos = (slot_ids[None, :] // across[:, None]).astype(jnp.float32)
    col_pos = (slot_ids[None, :] % across[:, None]).astype(jnp.float32)
    quarter = D // 4
    rate_table = jnp.exp(-math.log(10000.0) * jnp.arange(quarter).astype(jnp.float32) / quarter)
    rows_angle = row_pos[..., None] * rate_table
    cols_angle = col_pos[..., None] * rate_table
    return jnp.concatenate(
        [jnp.sin(rows_angle), jnp.cos(rows_angle), jnp.sin(cols_angle), jnp.cos(cols_angle)], -1
    )


def bias_parts(bias_vector):
    marks = [0, D, 2 * D, 3 * D, 11 * D, 12 * D, 13 * D, 14 * D, 14 * D + FF, 15 * D + FF]
    return [bias_vector[marks[number] : marks[number + 1]] for number in range(9)]


def matmul_rows(left, right):
    return jnp.dot(left, right, preferred_element_type=jnp.float32)


def outer_rows(left, right):
    return lax.dot_general(
        left, right, (((0,), (0,)), ((), ())), preferred_element_type=jnp.float32
    )


def inner_cols(left, right):
    return lax.dot_general(
        left, right, (((1,), (1,)), ((), ())), preferred_element_type=jnp.float32
    )


def to_low(values_in):
    return values_in.astype(jnp.bfloat16)


def row_sums(values_in):
    return jnp.sum(values_in.astype(jnp.float32), 0)


def attend_scores(queries, key_rows, bias_tile, usable):
    raw_scores = jnp.einsum(
        "iqhd,ikhd->ihqk", queries, key_rows, preferred_element_type=jnp.float32
    ) * HEAD ** (-0.5)
    raw_scores = raw_scores + bias_tile.astype(jnp.float32)
    return jnp.where(usable[:, None, None, :], raw_scores, -1e30)


def attend_backward(heads, bias_tile, usable, log_total, grad_context):
    queries, key_rows, values = (heads[:, :, 0], heads[:, :, 1], heads[:, :, 2])
    attention = jnp.exp(attend_scores(queries, key_rows, bias_tile, usable) - log_total)
    grad_values = jnp.einsum(
        "ihqk,iqhd->ikhd", to_low(attention), grad_context, preferred_element_type=jnp.float32
    )
    grad_attention = jnp.einsum(
        "iqhd,ikhd->ihqk", grad_context, values, preferred_element_type=jnp.float32
    )
    grad_scores = to_low(
        attention * (grad_attention - jnp.sum(attention * grad_attention, -1, keepdims=True))
    )
    grad_queries = jnp.einsum(
        "ihqk,ikhd->iqhd", grad_scores, key_rows, preferred_element_type=jnp.float32
    ) * HEAD ** (-0.5)
    grad_keys = jnp.einsum(
        "ihqk,iqhd->ikhd", grad_scores, queries, preferred_element_type=jnp.float32
    ) * HEAD ** (-0.5)
    return to_low(jnp.stack([grad_queries, grad_keys, grad_values], 2))


def layer_forward(weights, batch, seq_index):
    (
        embed_weight,
        square_weight,
        class_table,
        shift_weight,
        attend_weight,
        expand_weight,
        reduce_weight,
        final_weight,
        bias_vector,
    ) = weights
    latent, noise_in, height, across, labels_in, steps_in, bias_tile = batch
    images, local_slots = (latent.shape[0], latent.shape[1])
    total_rows = images * local_slots
    biases = [piece.astype(jnp.float32) for piece in bias_parts(bias_vector)]
    freq_in = to_low(time_freq(steps_in))
    pre_time = matmul_rows(freq_in, embed_weight[PIN:]) + biases[1]
    hid_time = to_low(smooth_gate(pre_time))
    onehot = to_low(
        (labels_in[:, None] == jnp.arange(class_table.shape[0])[None, :]).astype(jnp.float32)
    )
    condition = (
        matmul_rows(hid_time, square_weight[0]) + biases[2] + matmul_rows(onehot, class_table)
    )
    cond_act = to_low(smooth_gate(condition))
    modulation = matmul_rows(cond_act, shift_weight) + biases[3]
    pieces = [modulation[:, number * D : (number + 1) * D] for number in range(8)]
    signal = signal_level(steps_in)[:, None, None]
    noisy_input = to_low(jnp.sqrt(signal) * latent + jnp.sqrt(1.0 - signal) * noise_in)
    first_slot = seq_index * local_slots
    stream_in = matmul_rows(noisy_input.reshape(total_rows, PIN), embed_weight[:PIN]).reshape(
        images, local_slots, D
    )
    stream_in = stream_in + biases[0] + place_embed(across, first_slot, local_slots)
    normed_one = to_low(modnorm(stream_in, pieces[0], pieces[1])).reshape(total_rows, D)
    triple = matmul_rows(normed_one, attend_weight) + jnp.concatenate(
        [biases[4], jnp.zeros_like(biases[4]), biases[5]]
    )
    triple = to_low(triple).reshape(images, local_slots, 3, HEADS, HEAD)
    heads = lax.all_to_all(triple, "seq", split_axis=3, concat_axis=1, tiled=True)
    usable = jnp.arange(heads.shape[1])[None, :] < (height * across)[:, None]
    scores = attend_scores(heads[:, :, 0], heads[:, :, 1], bias_tile, usable)
    row_max = jnp.max(scores, -1, keepdims=True)
    log_total = row_max + jnp.log(jnp.sum(jnp.exp(scores - row_max), -1, keepdims=True))
    attention = to_low(jnp.exp(scores - log_total))
    context = to_low(
        jnp.einsum("ihqk,ikhd->iqhd", attention, heads[:, :, 2], preferred_element_type=jnp.float32)
    )
    merged = lax.all_to_all(context, "seq", split_axis=1, concat_axis=2, tiled=True).reshape(
        total_rows, D
    )
    attended = (matmul_rows(merged, square_weight[1]) + biases[6]).reshape(images, local_slots, D)
    stream_mid = stream_in + pieces[2][:, None, :] * attended
    normed_two = to_low(modnorm(stream_mid, pieces[3], pieces[4])).reshape(total_rows, D)
    upward = matmul_rows(normed_two, expand_weight) + biases[7]
    active = to_low(gaussian_unit(upward))
    downward = (matmul_rows(active, reduce_weight) + biases[8]).reshape(images, local_slots, D)
    stream_out = stream_mid + pieces[5][:, None, :] * downward
    normed_end = to_low(modnorm(stream_out, pieces[6], pieces[7])).reshape(total_rows, D)
    predicted = matmul_rows(normed_end, final_weight).reshape(images, local_slots, PIN)
    errors = predicted - noise_in
    kept_rows = (first_slot + jnp.arange(local_slots))[None, :] < (height * across)[:, None]
    kept_rows = kept_rows[:, :, None].astype(jnp.float32)
    loss_part = jnp.sum(kept_rows * errors * errors)
    count_part = jnp.sum(kept_rows) * PIN
    saved = dict(
        pieces=pieces,
        freq_in=freq_in,
        pre_time=pre_time,
        hid_time=hid_time,
        onehot=onehot,
        condition=condition,
        cond_act=cond_act,
        noisy_input=noisy_input,
        stream_in=stream_in,
        normed_one=normed_one,
        heads=heads,
        usable=usable,
        log_total=log_total,
        merged=merged,
        attended=attended,
        stream_mid=stream_mid,
        normed_two=normed_two,
        upward=upward,
        active=active,
        downward=downward,
        stream_out=stream_out,
        normed_end=normed_end,
        errors=errors,
        kept_rows=kept_rows,
    )
    return (loss_part, count_part, saved)


def layer_backward(weights, batch, saved, seq_index):
    (
        embed_weight,
        square_weight,
        class_table,
        shift_weight,
        attend_weight,
        expand_weight,
        reduce_weight,
        final_weight,
        bias_vector,
    ) = weights
    bias_tile = batch[6]
    pieces = saved["pieces"]
    images, local_slots = (saved["errors"].shape[0], saved["errors"].shape[1])
    total_rows = images * local_slots
    grad_pred = to_low(2.0 * saved["kept_rows"] * saved["errors"]).reshape(total_rows, PIN)
    grad_final = outer_rows(saved["normed_end"], grad_pred)
    grad_end = inner_cols(grad_pred, final_weight).reshape(images, local_slots, D)
    grad_out, grad_offset_end, grad_stretch_end = jax.vjp(
        modnorm, saved["stream_out"], pieces[6], pieces[7]
    )[1](grad_end)
    grad_gate_two = jnp.sum(grad_out * saved["downward"], 1)
    grad_down = to_low(grad_out * pieces[5][:, None, :]).reshape(total_rows, D)
    grad_reduce = outer_rows(saved["active"], grad_down)
    grad_active = inner_cols(grad_down, reduce_weight)
    grad_up = to_low(jax.vjp(gaussian_unit, saved["upward"])[1](grad_active)[0])
    grad_expand = outer_rows(saved["normed_two"], grad_up)
    grad_two = inner_cols(grad_up, expand_weight).reshape(images, local_slots, D)
    grad_mid_norm, grad_offset_two, grad_stretch_two = jax.vjp(
        modnorm, saved["stream_mid"], pieces[3], pieces[4]
    )[1](grad_two)
    grad_mid = grad_out + grad_mid_norm
    grad_gate_one = jnp.sum(grad_mid * saved["attended"], 1)
    grad_att = to_low(grad_mid * pieces[2][:, None, :]).reshape(total_rows, D)
    grad_proj = outer_rows(saved["merged"], grad_att)
    grad_merged = to_low(inner_cols(grad_att, square_weight[1])).reshape(
        images, local_slots, HEADS, HEAD
    )
    grad_context = lax.all_to_all(grad_merged, "seq", split_axis=2, concat_axis=1, tiled=True)
    grad_heads = attend_backward(
        saved["heads"], bias_tile, saved["usable"], saved["log_total"], grad_context
    )
    grad_triple = lax.all_to_all(
        grad_heads, "seq", split_axis=1, concat_axis=3, tiled=True
    ).reshape(total_rows, 3 * D)
    grad_attend = outer_rows(saved["normed_one"], grad_triple)
    triple_sums = row_sums(grad_triple)
    grad_one = inner_cols(grad_triple, attend_weight).reshape(images, local_slots, D)
    grad_in_norm, grad_offset_one, grad_stretch_one = jax.vjp(
        modnorm, saved["stream_in"], pieces[0], pieces[1]
    )[1](grad_one)
    grad_in = to_low(grad_mid + grad_in_norm).reshape(total_rows, D)
    grad_patch = outer_rows(saved["noisy_input"].reshape(total_rows, PIN), grad_in)
    grad_mod = jnp.concatenate(
        [
            grad_offset_one,
            grad_stretch_one,
            grad_gate_one,
            grad_offset_two,
            grad_stretch_two,
            grad_gate_two,
            grad_offset_end,
            grad_stretch_end,
        ],
        -1,
    )
    grad_mod = lax.psum(grad_mod.astype(jnp.bfloat16), "seq").astype(jnp.float32)
    owned = (jnp.arange(images) % lax.axis_size("seq") == seq_index).astype(jnp.float32)
    grad_mod = to_low(grad_mod * owned[:, None])
    grad_cond = to_low(
        jax.vjp(smooth_gate, saved["condition"])[1](inner_cols(grad_mod, shift_weight))[0]
    )
    grad_pre = to_low(
        jax.vjp(smooth_gate, saved["pre_time"])[1](inner_cols(grad_cond, square_weight[0]))[0]
    )
    grad_bias = jnp.concatenate(
        [
            row_sums(grad_in),
            row_sums(grad_pre),
            row_sums(grad_cond),
            row_sums(grad_mod),
            triple_sums[:D],
            triple_sums[2 * D :],
            row_sums(grad_att),
            row_sums(grad_up),
            row_sums(grad_down),
        ]
    )
    parts = (
        saved["freq_in"],
        saved["hid_time"],
        saved["onehot"],
        saved["cond_act"],
        grad_pre,
        grad_cond,
        grad_mod,
    )
    grad_shift = outer_rows(saved["cond_act"], grad_mod)
    grad_table = outer_rows(saved["onehot"], grad_cond)
    grad_time_two = outer_rows(saved["hid_time"], grad_cond)
    grad_time_one = outer_rows(saved["freq_in"], grad_pre)
    weight_grads = (
        jnp.concatenate([grad_patch, grad_time_one], 0),
        jnp.stack([grad_time_two, grad_proj]),
        grad_table,
        grad_shift,
        grad_attend,
        grad_expand,
        grad_reduce,
        grad_final,
        grad_bias,
    )
    return (weight_grads, parts)


def adam_step(weight, moment, second, gradient, factor):
    clipped = gradient * factor
    moment = BETA_ONE * moment + (1.0 - BETA_ONE) * clipped
    second = BETA_TWO * second + (1.0 - BETA_TWO) * clipped * clipped
    fixed_one = moment / (1.0 - BETA_ONE**STEP)
    fixed_two = second / (1.0 - BETA_TWO**STEP)
    weight = weight - RATE * (fixed_one / (jnp.sqrt(fixed_two) + EPSILON) + DECAY * weight)
    return (weight, moment, second)


def on_device(
    latents,
    noise_draw,
    heights,
    widths,
    labels,
    timesteps,
    bias_tiles,
    param_embed,
    param_square,
    param_table,
    param_shift,
    param_attend,
    param_expand,
    param_reduce,
    param_final,
    param_biases,
    first_embed,
    first_square,
    first_table,
    first_shift,
    first_attend,
    first_expand,
    first_reduce,
    first_final,
    first_biases,
    second_embed,
    second_square,
    second_table,
    second_shift,
    second_attend,
    second_expand,
    second_reduce,
    second_final,
    second_biases,
):
    weights = (
        lax.all_gather(to_low(param_embed), ("dp", "seq"), axis=1, tiled=True),
        lax.all_gather(to_low(param_square), ("dp", "seq"), axis=2, tiled=True),
        lax.all_gather(to_low(param_table), ("dp", "seq"), axis=1, tiled=True),
        lax.all_gather(to_low(param_shift), ("dp", "seq"), axis=1, tiled=True),
        lax.all_gather(to_low(param_attend), ("dp", "seq"), axis=1, tiled=True),
        lax.all_gather(to_low(param_expand), ("dp", "seq"), axis=1, tiled=True),
        lax.all_gather(to_low(param_reduce), ("dp", "seq"), axis=0, tiled=True),
        lax.all_gather(to_low(param_final), ("dp", "seq"), axis=0, tiled=True),
        lax.all_gather(to_low(param_biases), ("dp", "seq"), axis=0, tiled=True),
    )
    seq_index = lax.axis_index("seq")
    totals = None
    kept_parts = []
    loss_local = jnp.zeros((), jnp.float32)
    count_local = jnp.zeros((), jnp.float32)
    for batch_index in range(MICRO):
        batch = (
            latents[batch_index],
            noise_draw[batch_index],
            heights[batch_index],
            widths[batch_index],
            labels[batch_index],
            timesteps[batch_index],
            bias_tiles[batch_index],
        )
        loss_part, count_part, saved = layer_forward(weights, batch, seq_index)
        grads, parts = layer_backward(weights, batch, saved, seq_index)
        kept_parts.append(parts)
        totals = grads if totals is None else jax.tree.map(jnp.add, totals, grads)
        loss_local = loss_local + loss_part
        count_local = count_local + count_part
    shards = (
        lax.psum_scatter(totals[0], ("dp", "seq"), scatter_dimension=1, tiled=True),
        lax.psum_scatter(totals[1], ("dp", "seq"), scatter_dimension=2, tiled=True),
        lax.psum_scatter(totals[2], ("dp", "seq"), scatter_dimension=1, tiled=True),
        lax.psum_scatter(totals[3], ("dp", "seq"), scatter_dimension=1, tiled=True),
        lax.psum_scatter(totals[4], ("dp", "seq"), scatter_dimension=1, tiled=True),
        lax.psum_scatter(totals[5], ("dp", "seq"), scatter_dimension=1, tiled=True),
        lax.psum_scatter(totals[6], ("dp", "seq"), scatter_dimension=0, tiled=True),
        lax.psum_scatter(totals[7], ("dp", "seq"), scatter_dimension=0, tiled=True),
        lax.psum_scatter(totals[8], ("dp", "seq"), scatter_dimension=0, tiled=True),
    )
    squares_local = sum((jnp.sum(piece_grad * piece_grad) for piece_grad in shards))
    loss_total, value_count = lax.psum((loss_local, count_local), ("dp", "seq"))
    squared = lax.psum(squares_local, ("dp", "seq"))
    grad_norm = jnp.sqrt(squared)
    factor = LIMIT / jnp.maximum(grad_norm, LIMIT)
    params_in = (
        param_embed,
        param_square,
        param_table,
        param_shift,
        param_attend,
        param_expand,
        param_reduce,
        param_final,
        param_biases,
    )
    firsts = (
        first_embed,
        first_square,
        first_table,
        first_shift,
        first_attend,
        first_expand,
        first_reduce,
        first_final,
        first_biases,
    )
    seconds = (
        second_embed,
        second_square,
        second_table,
        second_shift,
        second_attend,
        second_expand,
        second_reduce,
        second_final,
        second_biases,
    )
    results = [
        adam_step(params_in[number], firsts[number], seconds[number], shards[number], factor)
        for number in range(9)
    ]
    fresh = (
        [results[number][0] for number in range(9)]
        + [results[number][1] for number in range(9)]
        + [results[number][2] for number in range(9)]
    )
    return tuple([loss_total, value_count, grad_norm] + fresh)


def solution(mesh):
    placed = (
        P(None, "dp", "seq", None),
        P(None, "dp", "seq", None),
        P(None, "dp"),
        P(None, "dp"),
        P(None, "dp"),
        P(None, "dp"),
        P(None, "dp", "seq", None, None),
        P(None, ("dp", "seq")),
        P(None, None, ("dp", "seq")),
        P(None, ("dp", "seq")),
        P(None, ("dp", "seq")),
        P(None, ("dp", "seq")),
        P(None, ("dp", "seq")),
        P(("dp", "seq"), None),
        P(("dp", "seq"), None),
        P(("dp", "seq")),
        P(None, ("dp", "seq")),
        P(None, None, ("dp", "seq")),
        P(None, ("dp", "seq")),
        P(None, ("dp", "seq")),
        P(None, ("dp", "seq")),
        P(None, ("dp", "seq")),
        P(("dp", "seq"), None),
        P(("dp", "seq"), None),
        P(("dp", "seq")),
        P(None, ("dp", "seq")),
        P(None, None, ("dp", "seq")),
        P(None, ("dp", "seq")),
        P(None, ("dp", "seq")),
        P(None, ("dp", "seq")),
        P(None, ("dp", "seq")),
        P(("dp", "seq"), None),
        P(("dp", "seq"), None),
        P(("dp", "seq")),
    )
    return jax.shard_map(
        on_device,
        mesh=mesh,
        in_specs=placed,
        out_specs=(
            P(),
            P(),
            P(),
            P(None, ("dp", "seq")),
            P(None, None, ("dp", "seq")),
            P(None, ("dp", "seq")),
            P(None, ("dp", "seq")),
            P(None, ("dp", "seq")),
            P(None, ("dp", "seq")),
            P(("dp", "seq"), None),
            P(("dp", "seq"), None),
            P(("dp", "seq")),
            P(None, ("dp", "seq")),
            P(None, None, ("dp", "seq")),
            P(None, ("dp", "seq")),
            P(None, ("dp", "seq")),
            P(None, ("dp", "seq")),
            P(None, ("dp", "seq")),
            P(("dp", "seq"), None),
            P(("dp", "seq"), None),
            P(("dp", "seq")),
            P(None, ("dp", "seq")),
            P(None, None, ("dp", "seq")),
            P(None, ("dp", "seq")),
            P(None, ("dp", "seq")),
            P(None, ("dp", "seq")),
            P(None, ("dp", "seq")),
            P(("dp", "seq"), None),
            P(("dp", "seq"), None),
            P(("dp", "seq")),
        ),
        check_vma=False,
    )
```

profile of v0, /device:TPU:0, one launch (start us, length us, event | category | flops | bytes accessed | tf_op | source)
XLA Modules:
  0.0 2063.7 jit_solution(3075636839004057467)
XLA Ops:
  18.1 42.6 %all-reduce = bf16[21888]{0:T(1024)(128)(2,1)S(1)} all-reduce(bf16[21888]{0:T(1024)(128)(2,1)S(1)} %dynamic-update-slice), channel_id=1, replica_groups=mesh['dp'=8,'seq'=4] {'dp','seq'}, use_global_device_ids=true, to_apply=%add | all-reduce | flops 21888 | bytes 87552
  61.3 43.5 %all-gather = bf16[32,36,272]{2,1,0:T(8,128)(2,1)S(1)} all-gather(bf16[1,36,272]{2,1,0:T(8,128)(2,1)S(1)} %convert_bitcast_fusion.2), channel_id=1, replica_groups=mesh['dp'=8,'seq'=4] {'dp','seq'}, dimensions={0}, use_global_device_ids=true | all-gather | bytes 646272 | tf_op jit(solution)/shard_map/all_gather | solution.py:391
  140.7 12.3 fusion.184
  153.0 10.9 copy.251
  165.6 54.4 %all-gather.21.cloned.1.call-done = bf16[32,108,1152]{2,1,0:T(8,128)(2,1)} async-done(((bf16[1,108,1152]{2,1,0:T(8,128)(2,1)}), bf16[32,108,1152]{2,1,0:T(8,128)(2,1)}) %all-gather.21.cloned.1.call-update) | async-done | bytes 7962640 | tf_op jit(solution)/shard_map/all_gather | solution.py:395
  229.1 128.6 %all-gather.13.cloned.1.call-done = bf16[1152,9216]{0,1:T(8,128)(2,1)} async-done(((bf16[1152,288]{0,1:T(8,128)(2,1)}), bf16[1152,9216]{0,1:T(8,128)(2,1)}) %all-gather.13.cloned.1.call-update) | async-done | bytes 21233680 | tf_op jit(solution)/shard_map/all_gather | solution.py:394
  422.8 29.2 %all-to-all-done = bf16[2,80,3,16,72]{1,4,2,0,3:T(8,128)(2,1)S(1)} async-done(((bf16[2,80,3,16,72]{1,4,2,0,3:T(8,128)(2,1)}), bf16[2,80,3,16,72]{1,4,2,0,3:T(8,128)(2,1)S(1)}, u32[]{:S(2)}, u32[]{:S(2)}) %all-to-all-start) | async-done | bytes 1105952 | tf_op jit(solution)/shard_map/all_to_all | solution.py:173
  483.4 43.6 %all-gather.3 = bf16[32,36,16]{1,2,0:T(8,128)(2,1)S(1)} all-gather(bf16[1,36,16]{1,2,0:T(8,128)(2,1)S(1)} %convert_bitcast_fusion.3), channel_id=1, replica_groups=mesh['dp'=8,'seq'=4] {'dp','seq'}, dimensions={0}, use_global_device_ids=true | all-gather | bytes 38016 | tf_op jit(solution)/shard_map/all_gather | solution.py:398
  527.9 10.9 copy.253
  582.6 12.6 convert_reduce_fusion.2
  617.6 12.2 convert_reduce_fusion.3
  693.3 10.9 all-to-all-done.5
  717.8 15.2 all-to-all-done.7
  764.3 24.8 %all-reduce.18.cloned.1.call-done = (bf16[2,9216]{1,0:T(2,128)(2,1)}, bf16[2,9216]{1,0:T(2,128)(2,1)}) async-done(((bf16[2,9216]{1,0:T(2,128)(2,1)}, bf16[2,9216]{1,0:T(2,128)(2,1)}), (bf16[2,9216]{1,0:T(2,128)(2,1)}, bf16[2,9216]{1,0:T(2,128)(2,1)})) %all-reduce.18.cloned.1.call-update) | async-done | bytes 73744 | tf_op jit(solution)/shard_map/psum | solution.py:295
  817.4 19.2 copy.237
  850.1 14.0 convolution_add_fusion.1
  875.8 15.4 convolution_add_fusion.2
  891.3 17.2 fusion.160
  908.5 31.3 %convolution_add_fusion = f32[1152,9216]{0,1:T(8,128)} fusion(f32[1152,9216]{0,1:T(8,128)} %fusion.160, f32[2,1152]{1,0:T(2,128)S(1)} %copy-done.85, bf16[2,9216]{1,0:T(2,128)(2,1)S(1)} %copy-done.78, f32[2]{0:T(128)S(1)} %copy-done.149), kind=kOutput, calls=%fused_computation | convolution fusion | flops 53150976 | bytes 84980744 | tf_op jit(solution)/shard_map/dot_general | solution.py:85
  964.1 297.8 %fusion.164 = (f32[1001,40]{0,1:T(8,128)S(1)}, f32[1152,112]{0,1:T(8,128)S(1)}) fusion(f32[1001,1152]{0,1:T(8,128)} %convolution_add_fusion.10, f32[1152,3456]{0,1:T(8,128)} %convolution_add_fusion.3), kind=kCustom, calls=%all-reduce-scatter.2 | all-reduce-scatter fusion | flops 5410050 | bytes 21214112
  1296.0 84.3 %reduce-scatter.14.cloned.1.call-done = f32[144,1152]{1,0:T(8,128)} async-done(((f32[4608,1152]{1,0:T(8,128)}), f32[144,1152]{1,0:T(8,128)}) %reduce-scatter.14.cloned.1.call-update) | async-done | bytes 663568 | tf_op jit(solution)/shard_map/reduce_scatter | solution.py:429
  1382.2 223.4 %reduce-scatter.12.cloned.1.call-done = f32[1152,144]{0,1:T(8,128)} async-done(((f32[1152,4608]{0,1:T(8,128)}), f32[1152,144]{0,1:T(8,128)}) %reduce-scatter.12.cloned.1.call-update) | async-done | bytes 663568 | tf_op jit(solution)/shard_map/reduce_scatter | solution.py:428
  1607.5 384.0 %reduce-scatter.10.cloned.1.call-done = f32[1152,288]{0,1:T(8,128)} async-done(((f32[1152,9216]{0,1:T(8,128)}), f32[1152,288]{0,1:T(8,128)}) %reduce-scatter.10.cloned.1.call-update) | async-done | bytes 1327120 | tf_op jit(solution)/shard_map/reduce_scatter | solution.py:426
  1997.8 39.6 %all-reduce.9 = (f32[]{:T(128)}, f32[]{:T(128)}, f32[]{:T(128)}) all-reduce(f32[]{:T(128)S(6)} %add.720, f32[]{:T(128)S(6)} %add.721, f32[]{:T(128)S(6)} %add.743), channel_id=1, replica_groups=mesh['dp'=8,'seq'=4] {'dp','seq'}, use_global_device_ids=true, to_apply=%region_18.21 | all-reduce | flops 3 | bytes 24 | tf_op jit(solution)/shard_map/psum | solution.py:434
  (776 shorter events, 458.2 us)
Async XLA Ops:
  7.2 123.8 %all-gather.19.cloned.1.call-start = ((), (), s32[]{:S(2)}) async-start(), calls=%async_computation.18 | async-start | bytes 2703360 | tf_op jit(solution)/shard_map/all_gather | solution.py:393
  8.9 131.8 %all-gather.11.cloned.1.call-start = ((), (), s32[]{:S(2)}) async-start(), calls=%async_computation.11 | async-start | bytes 5474304 | tf_op jit(solution)/shard_map/all_gather | solution.py:392
  10.8 209.1 %all-gather.21.cloned.1.call-start = ((), (), s32[]{:S(2)}) async-start(), calls=%async_computation.19 | async-start | bytes 8515584 | tf_op jit(solution)/shard_map/all_gather | solution.py:395
  12.7 345.1 %all-gather.13.cloned.1.call-start = ((), (), s32[]{:S(2)}) async-start(), calls=%async_computation.12 | async-start | bytes 21897216 | tf_op jit(solution)/shard_map/all_gather | solution.py:394
  15.0 546.9 %all-gather.15.cloned.1.call-start = ((), (), s32[]{:S(2)}) async-start(), calls=%async_computation.13 | async-start | bytes 10948608 | tf_op jit(solution)/shard_map/all_gather | solution.py:396
  15.8 555.4 %all-gather.17.cloned.1.call-start = ((), (), s32[]{:S(2)}) async-start(), calls=%async_computation.14 | async-start | bytes 10948608 | tf_op jit(solution)/shard_map/all_gather | solution.py:397
  378.7 31.8 %all-to-all-start.2 = ((bf16[2,80,3,16,72]{1,4,2,0,3:T(8,128)(2,1)}), bf16[2,80,3,16,72]{1,4,2,0,3:T(8,128)(2,1)}, u32[]{:S(2)}, u32[]{:S(2)}) async-start(bf16[2,80,3,16,72]{1,4,2,0,3:T(8,128)(2,1)} %copy.217), calls=%async_computation.2 | async-start | bytes 3538944 | tf_op jit(solution)/shard_map/all_to_all | solution.py:173
  410.5 41.6 %all-to-all-start = ((bf16[2,80,3,16,72]{1,4,2,0,3:T(8,128)(2,1)}), bf16[2,80,3,16,72]{1,4,2,0,3:T(8,128)(2,1)S(1)}, u32[]{:S(2)}, u32[]{:S(2)}) async-start(bf16[2,80,3,16,72]{1,4,2,0,3:T(8,128)(2,1)} %copy.209), calls=%async_computation | async-start | bytes 3538944 | tf_op jit(solution)/shard_map/all_to_all | solution.py:173
  465.0 13.7 all-to-all-start.1
  478.7 72.3 %all-to-all-start.3 = ((bf16[2,320,4,72]{3,2,0,1:T(4,128)(2,1)}), bf16[2,320,4,72]{3,2,0,1:T(4,128)(2,1)}, u32[]{:S(2)}, u32[]{:S(2)}) async-start(bf16[2,320,4,72]{3,2,0,1:T(4,128)(2,1)} %copy.221), calls=%async_computation.3 | async-start | bytes 1310720 | tf_op jit(solution)/shard_map/all_to_all | solution.py:182
  642.7 13.8 all-to-all-start.4
  656.5 14.2 all-to-all-start.6
  676.4 27.9 %all-to-all-start.5 = ((bf16[2,320,3,4,72]{4,3,0,2,1:T(4,128)(2,1)}), bf16[2,320,3,4,72]{4,3,0,2,1:T(4,128)(2,1)S(1)}, u32[]{:S(2)}, u32[]{:S(2)}) async-start(bf16[2,320,3,4,72]{4,3,0,2,1:T(4,128)(2,1)} %copy.228), calls=%async_computation.5 | async-start | bytes 3932160 | tf_op jit(solution)/shard_map/all_to_all | solution.py:271
  704.2 28.8 %all-to-all-start.7 = ((bf16[2,320,3,4,72]{4,3,0,2,1:T(4,128)(2,1)}), bf16[2,320,3,4,72]{4,3,0,2,1:T(4,128)(2,1)}, u32[]{:S(2)}, u32[]{:S(2)}) async-start(bf16[2,320,3,4,72]{4,3,0,2,1:T(4,128)(2,1)} %copy.235), calls=%async_computation.7 | async-start | bytes 3932160 | tf_op jit(solution)/shard_map/all_to_all | solution.py:271
  708.7 80.5 %all-reduce.18.cloned.1.call-start = ((), (), s32[]{:S(2)}) async-start(), calls=%async_computation.21 | async-start | bytes 147456 | tf_op jit(solution)/shard_map/psum | solution.py:295
  763.4 524.2 %all-reduce.16.cloned.1.call-start = ((), (), s32[]{:S(2)}) async-start(), calls=%async_computation.20 | async-start | bytes 24068096
  838.7 541.6 %reduce-scatter.14.cloned.1.call-start = ((), (), s32[]{:S(2)}) async-start(), calls=%async_computation.17 | async-start | bytes 21897216 | tf_op jit(solution)/shard_map/reduce_scatter | solution.py:429
  864.1 741.5 %reduce-scatter.12.cloned.1.call-start = ((), (), s32[]{:S(2)}) async-start(), calls=%async_computation.16 | async-start | bytes 21897216 | tf_op jit(solution)/shard_map/reduce_scatter | solution.py:428
  891.2 1100.3 %reduce-scatter.10.cloned.1.call-start = ((), (), s32[]{:S(2)}) async-start(), calls=%async_computation.15 | async-start | bytes 43794432 | tf_op jit(solution)/shard_map/reduce_scatter | solution.py:426
  1261.8 24.4 %collective-permute-start.4 = (f32[1152,112]{0,1:T(8,128)S(1)}, f32[1152,112]{0,1:T(8,128)S(1)}, u32[]{:S(2)}, u32[]{:S(2)}) collective-permute-start(f32[1152,112]{0,1:T(8,128)S(1)} %get-tuple-element.186), channel_id=1, source_target_pairs={{0,1},{1,2},{2,3},{3,4},{4,5},{5,6},{6,7},{7,8},{8,9},{9,10},{10,1... | collective-permute-start | bytes 1548296
  1263.2 21.7 %collective-permute-start.2 = (f32[1001,40]{0,1:T(8,128)S(1)}, f32[1001,40]{0,1:T(8,128)S(1)}, u32[]{:S(2)}, u32[]{:S(2)}) collective-permute-start(f32[1001,40]{0,1:T(8,128)S(1)} %get-tuple-element.185), channel_id=1, source_target_pairs={{0,3},{1,4},{2,5},{3,6},{4,7},{5,8},{6,9},{7,10},{8,11},{9,12},{10... | collective-permute-start | bytes 480488
  1264.5 20.4 collective-permute-start.1
  1271.9 13.0 collective-permute-start
  1276.1 10.1 collective-permute-start.5
  (226 other events, 9528.3 us)
Sparse Core Ops, SparseCore 0:
  11.5 60.6 all-gather.18
  75.6 65.0 all-gather.10
  144.2 75.6 all-gather.20
  223.3 134.4 all-gather.12
  361.1 103.4 all-gather.14
  467.9 87.8 all-gather.16
  763.5 25.5 all-reduce.17
  838.8 271.3 all-reduce.15
  1117.7 262.5 reduce-scatter.13
  1386.6 219.0 reduce-scatter.11
  1613.2 378.2 reduce-scatter.9
where the time goes:
time: 2070 us; the launch traced here: 2060 us
  waiting for transfers between devices  967 us (47%)
  blocking collectives  467 us (23%)
  matrix products  279 us (13%)
  local copies, waits for them, and re-layouts  185 us (9%)
  other arithmetic  85.9 us (4%)
  starting transfers between devices  51.7 us (2%)
  between operations  27.7 us (1%)
    reduce_scatter x1, waiting for transfers between devices, on_device(): lax.psum_scatter(totals[3], ('dp', 'seq'), scatter_dimension=1, tiled=True)  384 us
    unnamed x2, blocking collectives  340 us
    reduce_scatter x1, waiting for transfers between devices, on_device(): lax.psum_scatter(totals[5], ('dp', 'seq'), scatter_dimension=1, tiled=True)  223 us
    all_gather x1, waiting for transfers between devices, on_device(): lax.all_gather(to_low(param_shift), ('dp', 'seq'), axis=1, tiled=True)  129 us
    dot_general x20, matrix products, outer_rows(): lax.dot_general(left, right, (((0,), (0,)), ((), ())), preferred_element_...  125 us
    reduce_scatter x1, waiting for transfers between devices, on_device(): lax.psum_scatter(totals[6], ('dp', 'seq'), scatter_dimension=0, tiled=True)  84.3 us
    unnamed x496, local copies, waits for them, and re-layouts  70.5 us
    dot_general x14, matrix products, inner_cols(): lax.dot_general(left, right, (((1,), (1,)), ((), ())), preferred_element_...  68.2 us
  transfers between devices with their start and end apart: 25, of which 13 were waited for; matrix products, arithmetic and copies ran while one was open for 32% of the time, Pallas kernels for 0%

commit v1 on v0

v1 whole, which is shorter than its diff:
```python
import functools
import math

import jax
import jax.numpy as jnp
import numpy as np
from jax import lax
from jax.experimental import pallas as pl
from jax.experimental.pallas import tpu as pltpu
from jax.sharding import PartitionSpec as P

D = 1152
HEADS = 16
HEAD = 72
FF = 4608
FREQ = 256
PIN = 16
MICRO = 2
TSTEPS = 1000
STEP = 10
LANES = 128
AXES = ("dp", "seq")

BETA_ONE = 0.9
BETA_TWO = 0.95
EPSILON = 1e-08
DECAY = 0.1
RATE = 0.03
LIMIT = 1.0


def to_low(values_in):
    return values_in.astype(jnp.bfloat16)


def wide(values_in):
    return values_in.astype(jnp.float32)


def smooth_gate(values_in):
    return values_in * jax.nn.sigmoid(values_in)


def smooth_gate_slope(values_in):
    gate = jax.nn.sigmoid(values_in)
    return gate * (1.0 + values_in * (1.0 - gate))


def contract(left, right, left_dim, right_dim):
    return lax.dot_general(
        left,
        right,
        (((left_dim,), (right_dim,)), ((), ())),
        preferred_element_type=jnp.float32,
    )


def time_freq(steps_in):
    half_freq = FREQ // 2
    rate_table = jnp.exp(-math.log(10000.0) * jnp.arange(half_freq).astype(jnp.float32) / half_freq)
    angles = steps_in.astype(jnp.float32)[:, None] * rate_table[None, :]
    return jnp.concatenate([jnp.cos(angles), jnp.sin(angles)], -1)


def signal_level(steps_in):
    angles = (steps_in.astype(jnp.float32) / TSTEPS + 0.008) / 1.008 * (math.pi / 2)
    return jnp.cos(angles) * jnp.cos(angles)


def place_tables(slots, widest):
    quarter = D // 4
    lane = jnp.arange(D)
    rate = jnp.exp(-math.log(10000.0) * (lane % quarter).astype(jnp.float32) / quarter)
    fine = 16
    coarse = -(-slots // fine)
    steps = jnp.concatenate(
        [jnp.arange(coarse, dtype=jnp.float32) * fine, jnp.arange(fine, dtype=jnp.float32)]
    )
    angles = steps[:, None] * rate[None, :]
    sines, cosines = (jnp.sin(angles), jnp.cos(angles))
    sine_high, sine_low = (sines[:coarse, None], sines[None, coarse:])
    cosine_high, cosine_low = (cosines[:coarse, None], cosines[None, coarse:])
    table = jnp.where(
        lane // quarter % 2 == 0,
        sine_high * cosine_low + cosine_high * sine_low,
        cosine_high * cosine_low - sine_high * sine_low,
    ).reshape(coarse * fine, D)
    by_row = lane < 2 * quarter
    table = jnp.concatenate(
        [jnp.where(by_row, table[:slots], 0.0), jnp.where(by_row, 0.0, table[:widest])], 0
    )
    part_one = to_low(table)
    rest = table - wide(part_one)
    part_two = to_low(rest)
    part_three = to_low(rest - wide(part_two))
    return [part_one, part_two, part_three]


def place_picks(slot_ids, across, slots, widest):
    row_pos = (slot_ids // across)[:, None]
    col_pos = (slot_ids % across)[:, None] + slots
    spots = jnp.arange(slots + widest)[None, :]
    return to_low(((row_pos == spots) | (col_pos == spots)).astype(jnp.float32))


def after(values_in, earlier):
    return lax.optimization_barrier((values_in, earlier))[0]


def standardize(stream):
    centred = stream - jnp.mean(stream, -1, keepdims=True)
    scale = lax.rsqrt(jnp.mean(centred * centred, -1, keepdims=True) + 1e-06)
    return (centred * scale, scale)


def stretch_shift(unit, offset, stretch):
    return unit * (1.0 + stretch[:, None, :]) + offset[:, None, :]


def stretch_back(grad, unit, scale, stretch):
    grad_offset = jnp.sum(grad, 1)
    grad_stretch = jnp.sum(grad * unit, 1)
    grad_unit = grad * (1.0 + stretch[:, None, :])
    grad_stream = scale * (
        grad_unit
        - jnp.mean(grad_unit, -1, keepdims=True)
        - unit * jnp.mean(grad_unit * unit, -1, keepdims=True)
    )
    return (grad_stream, grad_offset, grad_stretch)


CUBE = 0.044715
ROOT = 0.7978845608028654


def gaussian_unit(values_in):
    inner = ROOT * (values_in + CUBE * values_in * values_in * values_in)
    return 0.5 * values_in * (1.0 + jnp.tanh(inner))


def gaussian_slope(values_in):
    inner = ROOT * (values_in + CUBE * values_in * values_in * values_in)
    bend = jnp.tanh(inner)
    return 0.5 * (1.0 + bend) + 0.5 * values_in * (1.0 - bend * bend) * ROOT * (
        1.0 + 3.0 * CUBE * values_in * values_in
    )


def attend_probs(nat_ref, bias_ref, head, own, keep):
    width = own * HEAD
    queries = nat_ref[:, head * HEAD : (head + 1) * HEAD]
    keys = nat_ref[:, width + head * HEAD : width + (head + 1) * HEAD]
    values = nat_ref[:, 2 * width + head * HEAD : 2 * width + (head + 1) * HEAD]
    scores = contract(queries, keys, 1, 1) * HEAD ** (-0.5) + wide(bias_ref[0, head])
    scores = jnp.where(keep, scores, -1e30)
    powers = jnp.exp(scores - jnp.max(scores, -1, keepdims=True))
    probs = powers * (1.0 / jnp.sum(powers, -1, keepdims=True))
    return (queries, keys, values, probs)


def attend_enter(meta_ref, triple_ref, nat_ref, masks):
    block = triple_ref.shape[2]
    for number, mask in enumerate(masks):
        first = pl.multiple_of((meta_ref[0] ^ mask) * block, 16)
        nat_ref[pl.ds(first, block), :] = triple_ref[number, 0]
    slots = nat_ref.shape[0]
    local = lax.broadcasted_iota(jnp.int32, (slots, slots), 1)
    return local < meta_ref[1 + pl.program_id(0)]


def attend_kernel(masks, meta_ref, triple_ref, bias_ref, context_ref, nat_ref):
    keep = attend_enter(meta_ref, triple_ref, nat_ref, masks)
    own, block = (bias_ref.shape[1], triple_ref.shape[2])
    mixed = []
    for head in range(own):
        _, _, values, probs = attend_probs(nat_ref, bias_ref, head, own, keep)
        mixed.append(to_low(contract(to_low(probs), values, 1, 0)))
    context = jnp.concatenate(mixed, 1)
    for number in range(len(masks)):
        context_ref[number, 0] = context[number * block : (number + 1) * block]


def attend_back_kernel(
    masks, meta_ref, triple_ref, bias_ref, grad_ref, out_ref, sums_ref, nat_ref, back_ref
):
    keep = attend_enter(meta_ref, triple_ref, nat_ref, masks)
    own, block = (bias_ref.shape[1], triple_ref.shape[2])
    width = own * HEAD
    grads = jnp.concatenate([grad_ref[number, 0] for number in range(len(masks))], 0)
    for head in range(own):
        queries, keys, values, probs = attend_probs(nat_ref, bias_ref, head, own, keep)
        grad_context = grads[:, head * HEAD : (head + 1) * HEAD]
        grad_probs = contract(grad_context, values, 1, 1)
        weighted = probs * grad_probs
        grad_scores = to_low(weighted - probs * jnp.sum(weighted, -1, keepdims=True))
        pieces = (
            contract(grad_scores, keys, 1, 0) * HEAD ** (-0.5),
            contract(grad_scores, queries, 0, 0) * HEAD ** (-0.5),
            contract(to_low(probs), grad_context, 0, 0),
        )
        for kind in range(3):
            begin = kind * width + head * HEAD
            back_ref[:, begin : begin + HEAD] = to_low(pieces[kind])
    sums_ref[0] = jnp.sum(wide(back_ref[...]), 0, keepdims=True)
    for number, mask in enumerate(masks):
        first = pl.multiple_of((meta_ref[0] ^ mask) * block, 16)
        out_ref[number, 0] = back_ref[pl.ds(first, block), :]


def attend_call(masks, meta, triple, bias_tiles, grads):
    images, own, slots, _ = bias_tiles.shape
    count, _, block, full = triple.shape
    width = own * HEAD
    backward = len(grads) > 0
    row = lambda image, meta_ref: (0, image, 0, 0)
    tri_spec = pl.BlockSpec((count, 1, block, full), row)
    slim_spec = pl.BlockSpec((count, 1, block, width), row)
    in_specs = [
        tri_spec,
        pl.BlockSpec((1, own, slots, slots), lambda image, meta_ref: (image, 0, 0, 0)),
    ] + [slim_spec] * len(grads)
    nat = pltpu.VMEM((slots, full), jnp.bfloat16)
    if backward:
        kernel, products = (attend_back_kernel, 6)
        out_shape = (
            jax.ShapeDtypeStruct(triple.shape, jnp.bfloat16),
            jax.ShapeDtypeStruct((images, 1, full), jnp.float32),
        )
        out_specs = (tri_spec, pl.BlockSpec((1, 1, full), lambda image, meta_ref: (image, 0, 0)))
        scratch = [nat, nat]
    else:
        kernel, products = (attend_kernel, 2)
        out_shape = jax.ShapeDtypeStruct((count, images, block, width), jnp.bfloat16)
        out_specs = slim_spec
        scratch = [nat]
    return pl.pallas_call(
        functools.partial(kernel, masks),
        out_shape=out_shape,
        grid_spec=pltpu.PrefetchScalarGridSpec(
            num_scalar_prefetch=1,
            grid=(images,),
            in_specs=in_specs,
            out_specs=out_specs,
            scratch_shapes=scratch,
        ),
        compiler_params=pltpu.CompilerParams(vmem_limit_bytes=40 * 2**20),
        cost_estimate=pl.CostEstimate(flops=1000, bytes_accessed=1000, transcendentals=0),
    )(meta, triple, bias_tiles, *grads)


def weight_copies(pick_ref, weight_ref, kind, held_ref, sem_ref):
    rows = weight_ref.shape[2]
    count = held_ref.shape[1] // rows
    copies = []
    for number in range(4 * count):
        target = held_ref.at[number // count, pl.ds(number % count * rows, rows)]
        copies.append(
            (
                number // count,
                pltpu.make_async_copy(
                    weight_ref.at[pick_ref[number], kind], target, sem_ref.at[kind, number]
                ),
            )
        )
    return copies


def start_copies(groups):
    @pl.when(pl.program_id(0) == 0)
    def _():
        for copies in groups:
            for _, copy in copies:
                copy.start()


def wait_copies(copies):
    for quarter in range(4):

        @pl.when(pl.program_id(0) == quarter)
        def _():
            for number, copy in copies:
                if number == quarter:
                    copy.wait()


def put_pair(total, own_ref, sent_ref):
    rows = own_ref.shape[0]

    @pl.when(pl.program_id(0) == pl.num_programs(0) - 1)
    def _():
        own_ref[...] = total[:rows]
        sent_ref[...] = to_low(total[rows:])


def add_up(total_ref, product):
    @pl.when(pl.program_id(0) == 0)
    def _():
        total_ref[...] = product

    @pl.when(pl.program_id(0) > 0)
    def _():
        total_ref[...] += product


def forward_kernel(
    pick_ref,
    normed_ref,
    bias_ref,
    weight_ref,
    up_ref,
    active_ref,
    own_ref,
    sent_ref,
    expand_held,
    reduce_held,
    total_ref,
    sem_ref,
):
    quarter = pl.program_id(0)
    expand_copies = weight_copies(pick_ref, weight_ref, 0, expand_held, sem_ref)
    reduce_copies = weight_copies(pick_ref, weight_ref, 1, reduce_held, sem_ref)
    start_copies([expand_copies, reduce_copies])
    wait_copies(expand_copies)
    upward = contract(normed_ref[...], expand_held[quarter], 1, 1) + bias_ref[0]
    up_ref[0] = upward
    active = to_low(gaussian_unit(upward))
    active_ref[0] = active
    wait_copies(reduce_copies)
    add_up(total_ref, contract(active, reduce_held[quarter], 1, 0))
    put_pair(total_ref, own_ref, sent_ref)


def backward_kernel(
    pick_ref,
    grad_ref,
    up_ref,
    weight_ref,
    out_ref,
    sums_ref,
    own_ref,
    sent_ref,
    expand_held,
    reduce_held,
    total_ref,
    sem_ref,
):
    quarter = pl.program_id(0)
    expand_copies = weight_copies(pick_ref, weight_ref, 0, expand_held, sem_ref)
    reduce_copies = weight_copies(pick_ref, weight_ref, 1, reduce_held, sem_ref)
    start_copies([reduce_copies, expand_copies])
    wait_copies(reduce_copies)
    grad_active = contract(grad_ref[...], reduce_held[quarter], 1, 1)
    grad_up = to_low(gaussian_slope(up_ref[0]) * grad_active)
    out_ref[0] = grad_up
    sums_ref[0] = jnp.sum(wide(grad_up), 0, keepdims=True)
    wait_copies(expand_copies)
    add_up(total_ref, contract(grad_up, expand_held[quarter], 1, 0))
    put_pair(total_ref, own_ref, sent_ref)


def hidden_call(kernel, pick, left, second, weights):
    rows = left.shape[0]
    size = second.shape[2]
    whole = pl.BlockSpec((rows, D), lambda quarter, pick_ref: (0, 0))
    slab = pl.BlockSpec((1, rows, size), lambda quarter, pick_ref: (quarter, 0, 0))
    line = pl.BlockSpec((1, 1, size), lambda quarter, pick_ref: (quarter, 0, 0))
    half = pl.BlockSpec((rows // 2, D), lambda quarter, pick_ref: (0, 0))
    if kernel is forward_kernel:
        second_spec, out_specs = (line, (slab, slab, half, half))
        kinds = (((4, rows, size), jnp.float32), ((4, rows, size), jnp.bfloat16))
    else:
        second_spec, out_specs = (slab, (slab, line, half, half))
        kinds = (((4, rows, size), jnp.bfloat16), ((4, 1, size), jnp.float32))
    kinds = kinds + (((rows // 2, D), jnp.float32), ((rows // 2, D), jnp.bfloat16))
    return pl.pallas_call(
        kernel,
        out_shape=tuple(jax.ShapeDtypeStruct(shape, kind) for shape, kind in kinds),
        grid_spec=pltpu.PrefetchScalarGridSpec(
            num_scalar_prefetch=1,
            grid=(4,),
            in_specs=[whole, second_spec, pl.BlockSpec(memory_space=pl.ANY)],
            out_specs=out_specs,
            scratch_shapes=[
                pltpu.VMEM((4, size, D), jnp.bfloat16),
                pltpu.VMEM((4, size, D), jnp.bfloat16),
                pltpu.VMEM((rows, D), jnp.float32),
                pltpu.SemaphoreType.DMA((2, 4 * size // weights.shape[2])),
            ],
        ),
        compiler_params=pltpu.CompilerParams(vmem_limit_bytes=56 * 2**20),
        cost_estimate=pl.CostEstimate(flops=1000, bytes_accessed=1000, transcendentals=0),
    )(pick, left, second, weights)


def outer_kernel(grad_up_ref, active_ref, normed_ref, grad_ref, *refs):
    outs, held, sem_ref = (refs[:7], refs[7:14], refs[14])
    step = pl.program_id(0)
    half = held[0].shape[1]
    products = (
        contract(grad_up_ref[0], normed_ref[...], 0, 0),
        contract(active_ref[0], grad_ref[...], 0, 0),
    )
    copies = [pltpu.make_async_copy(held[at], outs[at], sem_ref.at[at]) for at in range(7)]
    for turn in range(4):

        @pl.when(step == turn)
        def _():
            if turn == 3:
                for kind in range(2):
                    held[6][kind] = products[kind]
                copies[6].start()
            else:
                low_ref, high_ref = (held[2 * turn], held[2 * turn + 1])
                for kind in range(2):
                    low_ref[kind] = products[kind][:half].astype(low_ref.dtype)
                    high_ref[kind] = products[kind][half:].astype(high_ref.dtype)
                copies[2 * turn].start()
                copies[2 * turn + 1].start()

    @pl.when(step == 3)
    def _():
        for copy in copies:
            copy.wait()


def outer_call(grad_up, active, normed, grad_down):
    _, rows, size = grad_up.shape
    low, full = (jnp.bfloat16, jnp.float32)
    kinds = [low, low, full, low, low, full]
    shapes = [((2, size // 2, D), kind) for kind in kinds] + [((2, size, D), full)]
    slab = pl.BlockSpec(
        (1, rows, size),
        lambda step: (jnp.where(step == 0, 3, jnp.where(step == 3, 0, step)), 0, 0),
    )
    whole = pl.BlockSpec((rows, D), lambda step: (0, 0))
    return pl.pallas_call(
        outer_kernel,
        out_shape=tuple(jax.ShapeDtypeStruct(shape, kind) for shape, kind in shapes),
        grid=(4,),
        in_specs=[slab, slab, whole, whole],
        out_specs=tuple([pl.BlockSpec(memory_space=pl.ANY)] * 7),
        scratch_shapes=[pltpu.VMEM(shape, kind) for shape, kind in shapes]
        + [pltpu.SemaphoreType.DMA((7,))],
        compiler_params=pltpu.CompilerParams(vmem_limit_bytes=56 * 2**20),
        cost_estimate=pl.CostEstimate(flops=1000, bytes_accessed=1000, transcendentals=0),
    )(grad_up, active, normed, grad_down)


def unit_plan(devices, seq):
    share = 3 * D // devices
    unit = math.gcd(math.gcd(share, D // seq), HEAD)
    per = share // unit
    span = D // seq

    def group_of(number):
        return (number * unit % D) // span

    left = [{local: group_of(owner * per + local) for local in range(per)} for owner in range(devices)]
    send = np.zeros((per, devices), np.int32)
    target = np.zeros((per, devices), np.int32)
    held = np.zeros((per, devices), np.int32)
    for turn in range(per):
        match = [-1] * devices

        def seek(owner, seen):
            groups = set(left[owner].values())
            near = sorted(
                (place for place in range(devices) if place % seq in groups),
                key=lambda place: (place != owner, place // seq != owner // seq, place ^ owner),
            )
            for place in near:
                if place in seen:
                    continue
                seen.add(place)
                if match[place] < 0 or seek(match[place], seen):
                    match[place] = owner
                    return True
            return False

        for owner in range(devices):
            assert seek(owner, set())
        for place, owner in enumerate(match):
            local = next(item for item, group in left[owner].items() if group == place % seq)
            del left[owner][local]
            send[turn, owner] = local
            target[turn, owner] = place
            held[turn, place] = owner * per + local
    return (unit, per, send, target, held)


def unit_rows(devices, seq, unit, per, held):
    dp = devices // seq
    span = D // seq
    extra = D // devices
    rows = np.full((devices, dp * (per * unit + extra)), -1, np.int32)
    for place in range(devices):
        at = 0
        for mask in gather_masks(dp):
            for turn in range(per):
                first = int(held[turn, place ^ (mask * seq)]) * unit
                kind, inside = (first // D, first % D)
                begin = kind * span + inside - span * (place % seq)
                rows[place, at : at + unit] = np.arange(begin, begin + unit)
                at += unit
            at += extra
    return rows


def gather_masks(dp):
    masks = [0]
    bit = dp >> 1
    while bit:
        masks = masks + [item ^ bit for item in masks]
        bit >>= 1
    return masks


def make_step(mesh):
    dp, seq = (mesh.shape["dp"], mesh.shape["seq"])
    devices = dp * seq
    top = devices.bit_length() - 1
    seq_bits = seq.bit_length() - 1
    own_heads = HEADS // seq
    span = D // seq
    unit, per, unit_send, unit_target, unit_held = unit_plan(devices, seq)
    row_table = unit_rows(devices, seq, unit, per, unit_held)
    cols = D // devices
    shift_cols = 8 * D // devices
    hidden_share = FF // devices
    bias_share = (15 * D + FF) // devices
    dp_bits = list(range(top - 1, seq_bits - 1, -1))
    far_bits = list(range(top - 1, 2, -1))
    seq_down = list(range(seq_bits - 1, -1, -1))

    def masks_of(bits):
        masks = [0]
        for bit in bits:
            masks = masks + [mask ^ (1 << bit) for mask in masks]
        return masks

    slot_masks = masks_of(seq_down)

    def swap(values_in, bit):
        return lax.ppermute(
            values_in, AXES, [(place, place ^ (1 << bit)) for place in range(devices)]
        )

    def exchange(values_in):
        return lax.all_to_all(values_in, AXES, split_axis=0, concat_axis=0, tiled=True)

    def share_all(block):
        return exchange(jnp.broadcast_to(block[None], (devices,) + block.shape))

    def gather_rows(rows, bits):
        for bit in bits:
            rows = jnp.concatenate([rows, swap(rows, bit)], 0)
        return rows

    def fold_rows(rows, bits):
        for bit in bits:
            half = rows.shape[0] // 2
            rows = rows[:half] + wide(swap(to_low(rows[half:]), bit))
        return rows

    def fold_second(rows, bits):
        for bit in bits:
            half = rows.shape[1] // 2
            rows = rows[:, :half] + wide(swap(to_low(rows[:, half:]), bit))
        return rows

    def on_device(
        latents,
        noise_draw,
        heights,
        widths,
        labels,
        timesteps,
        bias_tiles,
        *states,
    ):
        params_in, firsts, seconds = (states[:9], states[9:18], states[18:])
        seq_index = lax.axis_index("seq")
        me = lax.axis_index("dp") * seq + seq_index
        local_slots = latents.shape[2]
        slots = local_slots * seq
        widest = min(slots, 32)
        images = latents.shape[0] * latents.shape[1]
        classes = params_in[2].shape[0]
        tokens = images * local_slots
        all_tokens = images * slots
        all_images = images * dp
        latent = latents.reshape(images, local_slots, PIN)
        noise_in = noise_draw.reshape(images, local_slots, PIN)
        height, across = (heights.reshape(images), widths.reshape(images))
        label_own, step_own = (labels.reshape(images), timesteps.reshape(images))
        bias_all = bias_tiles.reshape(images, own_heads, slots, slots)
        used = height * across

        embed_t = params_in[0].T
        square_t = jnp.transpose(params_in[1], (2, 0, 1))
        table_t = to_low(params_in[2].T)
        shift_t = to_low(params_in[3].T)
        attend_t = to_low(params_in[4].T)
        expand_t = to_low(params_in[5].T)
        reduce_r = to_low(params_in[6])

        small = jnp.concatenate(
            [to_low(params_in[8]), to_low(embed_t[:, :PIN]).reshape(-1), to_low(params_in[7]).reshape(-1)]
            + [
                to_low(wide(piece))
                for piece in (step_own // 32, step_own % 32, label_own // 32, label_own % 32)
            ]
        )
        length = -(-small.shape[0] // 2048) * 2048
        small = jnp.pad(small, (0, length - small.shape[0])).reshape(-1, LANES)
        embed_own = to_low(embed_t[:, PIN:]).reshape(-1, LANES)
        small = share_all(jnp.concatenate([small, embed_own], 0))
        embed_time = small[:, length // LANES :].reshape(D, FREQ)
        small = small[:, : length // LANES].reshape(devices, length)
        at = bias_share
        biases = wide(small[:, :at].reshape(-1))
        patch_t = small[:, at : at + cols * PIN].reshape(D, PIN)
        at = at + cols * PIN
        final_weight = small[:, at : at + cols * PIN].reshape(D, PIN)
        at = at + cols * PIN
        numbers = wide(small[::seq, at : at + 4 * images]).reshape(dp, 4, images).astype(jnp.int32)
        steps_all = (numbers[:, 0] * 32 + numbers[:, 1]).reshape(-1)
        labels_all = (numbers[:, 2] * 32 + numbers[:, 3]).reshape(-1)
        marks = [0, D, 2 * D, 3 * D, 11 * D, 12 * D, 13 * D, 14 * D, 14 * D + FF, 15 * D + FF]
        b_patch, b_time, b_cond, b_mod, b_query, b_value, b_proj, b_expand, b_reduce = [
            biases[marks[number] : marks[number + 1]] for number in range(9)
        ]

        attend_t = after(attend_t, small)
        received = []
        for turn in range(per):
            local = jnp.asarray(unit_send[turn])[me]
            received.append(
                lax.ppermute(
                    lax.dynamic_slice(attend_t, (local * unit, 0), (unit, D)),
                    AXES,
                    [(owner, int(unit_target[turn, owner])) for owner in range(devices)],
                )
            )
        both = jnp.concatenate(received + [to_low(square_t[:, 1])], 0)
        hidden_masks = [mask ^ far for mask in (0, 4, 2, 6) for far in masks_of(far_bits)]
        hidden_blocks = jnp.asarray(np.array(hidden_masks, np.int32)) ^ me
        hidden_pick = hidden_blocks[:, None] == jnp.arange(devices)[None, :]
        size = len(hidden_masks) * hidden_share // 4

        tables = place_tables(slots, widest)
        freq_in = to_low(time_freq(steps_all))

        def mine(vector, count):
            return lax.dynamic_slice(vector, (me * count,), (count,))[:, None]

        pre_time_all = contract(embed_time, freq_in, 1, 1) + b_time[:, None]
        hid_time = to_low(smooth_gate(pre_time_all))
        onehot = to_low(
            (labels_all[:, None] == jnp.arange(classes)[None, :]).astype(jnp.float32)
        )
        square_zero = to_low(square_t[:, 0])
        condition = (
            contract(square_zero, hid_time, 1, 0)
            + mine(b_cond, cols)
            + contract(table_t, onehot, 1, 1)
        )
        signal = signal_level(step_own)[:, None, None]
        latent = after(latent, hid_time)
        noisy_own = to_low(jnp.sqrt(signal) * latent + jnp.sqrt(1.0 - signal) * noise_in)
        noisy_own = noisy_own.reshape(tokens, PIN)
        noisy_all = gather_rows(noisy_own, seq_down)
        cond_own = to_low(smooth_gate(condition))
        both_first = gather_rows(after(both, hid_time), dp_bits[:1])
        both_second = gather_rows(after(both_first, cond_own), dp_bits[1:2])

        gathered = lax.all_gather(
            after(jnp.stack([expand_t, reduce_r]), both_second), AXES, axis=0
        )

        across_late = after(across, cond_own)
        block_of = jnp.asarray(np.array(slot_masks, np.int32)) ^ seq_index
        slot_ids = jnp.broadcast_to(
            block_of[:, None, None] * local_slots + jnp.arange(local_slots)[None, None, :],
            (seq, images, local_slots),
        ).reshape(-1)
        across_rows = jnp.broadcast_to(
            across_late[None, :, None], (seq, images, local_slots)
        ).reshape(-1)
        picks = place_picks(slot_ids, across_rows, slots, widest)
        stream_all = (
            contract(
                jnp.concatenate([picks] * 3 + [noisy_all], 1),
                jnp.concatenate(tables + [patch_t.T], 0),
                1,
                0,
            )
            + b_patch
        ).reshape(seq, images, local_slots, D)
        cond_act = after(share_all(cond_own), stream_all).reshape(D, all_images)
        mod_cols = contract(cond_act, shift_t, 0, 1) + mine(b_mod, shift_cols)[:, 0][None, :]
        mod_send = jnp.broadcast_to(
            mod_cols.reshape(dp, 1, images, shift_cols), (dp, seq, images, shift_cols)
        ).reshape(devices, images, shift_cols)
        unit_all, scale_all = standardize(after(stream_all, mod_cols))
        modulation = after(exchange(mod_send), scale_all)
        modulation = jnp.transpose(modulation, (1, 0, 2)).reshape(images, 8 * D)
        off_one, str_one, gate_one, off_two, str_two, gate_two, off_end, str_end = [
            modulation[:, number * D : (number + 1) * D] for number in range(8)
        ]

        both = gather_rows(after(both_second, mod_send), dp_bits[2:])
        my_rows = lax.dynamic_index_in_dim(jnp.asarray(row_table), me, 0, keepdims=False)
        place_units = to_low(
            (my_rows[:, None] == jnp.arange(3 * span)[None, :]).astype(jnp.float32)
        )
        attend_n = to_low(contract(both, place_units, 0, 0))
        normed_one = to_low(
            unit_all * (1.0 + str_one[None, :, None, :]) + off_one[None, :, None, :]
        ).reshape(all_tokens, D)
        stream_in = after(stream_all[0], normed_one)
        unit_one, scale_one = standardize(stream_in)

        def head_bias(vector):
            return lax.dynamic_slice(vector, (seq_index * span,), (span,))

        triple_bias = jnp.concatenate(
            [head_bias(b_query), jnp.zeros((span,), jnp.float32), head_bias(b_value)]
        )
        triple = to_low(contract(normed_one, attend_n, 1, 0) + triple_bias).reshape(
            seq, images, local_slots, 3 * span
        )
        proj_x = both.reshape(dp, per * unit + cols, D)[:, per * unit :].reshape(dp * cols, D)
        for bit in seq_down:
            proj_x = after(gather_rows(proj_x, [bit]), triple)
        slot_block = jnp.asarray(np.array(gather_masks(devices), np.int32)) ^ me
        source = slot_block[:, None] * cols + jnp.arange(cols)[None, :]
        place_proj = to_low(
            (source.reshape(-1)[:, None] == jnp.arange(D)[None, :]).astype(jnp.float32)
        )
        proj_n = to_low(contract(place_proj, proj_x, 0, 0))
        meta = jnp.concatenate([seq_index.reshape(1), used]).astype(jnp.int32)
        context = attend_call(slot_masks, meta, triple, bias_all, ())

        def over_seq(values_in):
            return lax.all_to_all(values_in, "seq", split_axis=0, concat_axis=0, tiled=True)

        merged = jnp.transpose(
            after(over_seq(context), (proj_n, stream_in)).reshape(seq, tokens, span), (1, 0, 2)
        ).reshape(tokens, D)
        attended = (contract(merged, proj_n, 1, 1) + b_proj).reshape(images, local_slots, D)
        stream_mid = stream_in + gate_one[:, None, :] * attended
        unit_two, scale_two = standardize(stream_mid)
        normed_own = to_low(stretch_shift(unit_two, off_two, str_two)).reshape(tokens, D)

        def pair_rows(rows):
            return jnp.concatenate([rows, swap(rows, 0)], 0)

        normed_two = pair_rows(normed_own)
        hidden_bias = jnp.sum(
            jnp.where(hidden_pick[:, :, None], b_expand.reshape(1, devices, hidden_share), 0.0), 1
        ).reshape(4, 1, size)
        if hidden_share % 16 == 0:
            hidden_index, weights = (hidden_blocks, gathered)
        else:
            weights = jnp.transpose(
                jnp.take(gathered, hidden_blocks, axis=0).reshape(4, -1, 2, hidden_share, D),
                (0, 2, 1, 3, 4),
            ).reshape(4, 2, size, D)
            hidden_index = jnp.arange(4, dtype=jnp.int32)
        upward, active, down_own, down_sent = hidden_call(
            forward_kernel, hidden_index, normed_two, hidden_bias, weights
        )
        downward = (down_own + wide(swap(down_sent, 0)) + b_reduce).reshape(images, local_slots, D)
        stream_out = stream_mid + gate_two[:, None, :] * downward
        unit_end, scale_end = standardize(stream_out)
        normed_end = to_low(stretch_shift(unit_end, off_end, str_end)).reshape(tokens, D)
        predicted = contract(normed_end, final_weight, 1, 0).reshape(images, local_slots, PIN)
        errors = predicted - noise_in
        kept = (seq_index * local_slots + jnp.arange(local_slots))[None, :] < used[:, None]
        kept = kept[:, :, None].astype(jnp.float32)
        loss_local = jnp.sum(kept * errors * errors)
        count_local = jnp.sum(kept) * PIN

        grad_pred = to_low(2.0 * kept * errors).reshape(tokens, PIN)
        grad_end = contract(grad_pred, final_weight, 1, 1).reshape(images, local_slots, D)
        grad_out, grad_off_end, grad_str_end = stretch_back(grad_end, unit_end, scale_end, str_end)
        grad_down_own = to_low(grad_out * gate_two[:, None, :]).reshape(tokens, D)
        grad_down = pair_rows(grad_down_own)
        grad_up, up_sums, two_own, two_sent = hidden_call(
            backward_kernel, hidden_index, grad_down, upward, weights
        )

        both_low, both_high, x_low, x_high, y_low, y_high, near = outer_call(
            grad_up, active, normed_two, grad_down
        )
        from_both_low, from_both_high = (swap(both_low, 1), swap(both_high, 2))
        from_x_high = swap(x_high, 2)
        grad_two = two_own + wide(after(swap(two_sent, 0), both_low))
        grad_two = grad_two.reshape(images, local_slots, D)
        grad_mid_norm, grad_off_two, grad_str_two = stretch_back(
            grad_two, unit_two, scale_two, str_two
        )
        grad_mid = grad_out + grad_mid_norm
        grad_att = to_low(grad_mid * gate_one[:, None, :]).reshape(tokens, D)
        grad_merged = to_low(contract(grad_att, proj_n, 1, 0))
        grad_merged = jnp.transpose(grad_merged.reshape(tokens, seq, span), (1, 0, 2))
        grad_att_x = to_low(contract(after(grad_att, grad_merged), place_proj, 1, 1))
        proj_parts = contract(grad_att_x, merged, 0, 0)
        x_low = to_low(after(x_low, grad_merged) + wide(from_both_low))
        y_high = to_low(after(y_high, grad_merged) + wide(from_both_high))
        from_x_low = swap(x_low, 2)
        proj_half = proj_parts.shape[0] // 2
        proj_sent = to_low(proj_parts[proj_half:])
        proj_parts = proj_parts[:proj_half] + wide(swap(proj_sent, 0))
        proj_half = proj_parts.shape[0] // 2
        proj_sent = to_low(proj_parts[proj_half:])
        proj_parts = proj_parts[:proj_half]
        from_proj = swap(proj_sent, 1)
        grad_context = after(over_seq(grad_merged), (proj_sent, x_low, y_high))
        grad_context = grad_context.reshape(seq, images, local_slots, span)

        grad_triple, triple_sums = attend_call(slot_masks, meta, triple, bias_all, (grad_context,))
        grad_triple = grad_triple.reshape(all_tokens, 3 * span)
        half = all_tokens // 2
        one_sent = to_low(contract(grad_triple[half:], attend_n, 1, 1))
        one_kept = contract(grad_triple[:half], attend_n, 1, 1)
        one_parts = one_kept + wide(swap(one_sent, 0))
        for bit in range(1, seq_bits):
            half = one_parts.shape[0] // 2
            one_last = to_low(one_parts[half:])
            one_came = swap(one_last, bit)
            if bit == seq_bits - 1:
                place_own = place_units.reshape(dp, -1, 3 * span)[:, : per * unit]
                place_own = place_own.reshape(dp * per * unit, 3 * span)
                grad_units = to_low(contract(after(grad_triple, one_last), place_own, 1, 1))
                middle = dp * per * unit // 2
                attend_sent = to_low(contract(grad_units[:, middle:], normed_one, 0, 0))
                attend_kept = contract(grad_units[:, :middle], normed_one, 0, 0)
                near_high = after(near, one_last)[:, size // 2 :] + wide(from_x_high)
                proj_parts = after(proj_parts, one_last) + wide(from_proj)
                from_y_high = swap(after(y_high, one_last), 1)
                from_y_low = swap(after(y_low, attend_sent), 1)
                one_came = after(one_came, (attend_sent, attend_kept, near_high))
            one_parts = one_parts[:half] + wide(one_came)
        grad_one = one_parts.reshape(images, local_slots, D)

        proj_parts = proj_parts.reshape(2, dp // 2, cols, D)

        def beside(attend_rows, proj_rows):
            attend_rows = attend_rows.reshape(dp // 2, per * unit, D)
            return jnp.concatenate([attend_rows, proj_rows], 1).reshape(-1, D)

        both_sent = beside(attend_sent, to_low(proj_parts[1]))
        both_parts = beside(attend_kept, proj_parts[0])
        both_half = both_parts.shape[0]
        from_both = swap(both_sent, dp_bits[-1])
        triple_sums = jnp.sum(triple_sums, 0).reshape(-1)

        grad_in_norm, grad_off_one, grad_str_one = stretch_back(
            grad_one, unit_one, scale_one, str_one
        )
        grad_in = to_low(grad_mid + grad_in_norm).reshape(tokens, D)

        grad_gate_one = jnp.sum(grad_mid * attended, 1)
        grad_gate_two = jnp.sum(grad_out * downward, 1)
        grad_mod_parts = jnp.concatenate(
            [
                grad_off_one,
                grad_str_one,
                grad_gate_one,
                grad_off_two,
                grad_str_two,
                grad_gate_two,
                grad_off_end,
                grad_str_end,
            ],
            -1,
        )
        grad_mod_sent = jnp.transpose(
            grad_mod_parts.reshape(images, devices, shift_cols), (1, 0, 2)
        )
        near_sent = to_low(after(near_high, grad_mod_sent) + wide(from_y_high))
        from_high = swap(near_sent, far_bits[-1])
        grad_mod = to_low(
            jnp.sum(
                after(exchange(grad_mod_sent), near_sent).reshape(dp, seq, images, shift_cols), 1
            )
        ).reshape(all_images, shift_cols)

        cond_parts = contract(shift_t, grad_mod, 0, 1).reshape(devices, cols, all_images)
        both_parts = after(both_parts, cond_parts) + wide(from_both)
        both_half = both_half // 2
        both_sent = to_low(both_parts[both_half:])
        from_both = swap(both_sent, dp_bits[-2])
        grad_shift = contract(after(grad_mod, cond_parts), cond_act, 0, 1)
        cond_came = after(exchange(cond_parts), (both_sent, grad_shift))
        grad_cond = to_low(smooth_gate_slope(condition) * jnp.sum(cond_came, 0))
        time_parts = contract(square_zero, grad_cond, 0, 0).reshape(devices, cols * all_images)

        grad_patch = contract(grad_in, noisy_own, 0, 0)
        grad_final = contract(normed_end, grad_pred, 0, 0)

        def heads_out(sums):
            return lax.dynamic_update_slice(
                jnp.zeros((D,), jnp.float32), sums, (seq_index * span,)
            )

        def spread_own(sums, length):
            return lax.dynamic_update_slice(
                jnp.zeros((length,), jnp.float32), sums, (me * sums.shape[0],)
            )

        up_nat = jnp.sum(
            jnp.where(hidden_pick[:, :, None], up_sums.reshape(-1, 1, hidden_share), 0.0), 0
        )
        bias_parts = jnp.concatenate(
            [
                jnp.sum(wide(grad_in), 0),
                jnp.zeros((D,), jnp.float32),
                spread_own(jnp.sum(wide(grad_cond), 1), D),
                spread_own(jnp.sum(wide(grad_mod), 0), 8 * D),
                heads_out(triple_sums[:span]),
                heads_out(triple_sums[2 * span :]),
                jnp.sum(wide(grad_att), 0),
                up_nat.reshape(-1),
                jnp.sum(wide(grad_down_own), 0),
            ]
        )
        mixed = jnp.concatenate(
            [
                time_parts,
                bias_parts.reshape(devices, bias_share),
                grad_patch.reshape(devices, cols * PIN),
                grad_final.reshape(devices, cols * PIN),
            ],
            1,
        )
        both_parts = after(both_parts[:both_half], mixed) + wide(from_both)
        both_half = both_half // 2
        both_sent = to_low(both_parts[both_half:])
        both_parts = both_parts[:both_half] + wide(swap(both_sent, dp_bits[-3]))
        near_low = after(near, time_parts)[:, : size // 2] + wide(from_x_low) + wide(from_y_low)
        near = near_low + wide(from_high)
        if len(far_bits) > 1:
            near_half = near.shape[1] // 2
            near_sent = to_low(near[:, near_half:])
            near = near[:, :near_half] + wide(swap(near_sent, far_bits[-2]))
        grad_table = contract(after(grad_cond, mixed), onehot, 1, 0)
        grad_time_two = contract(after(grad_cond, mixed), hid_time, 1, 1)
        mixed = after(exchange(mixed), (both_sent, near_sent, grad_table, grad_time_two))
        mixed = jnp.sum(mixed, 0)
        time_came, mixed = (mixed[: cols * all_images], mixed[cols * all_images :])
        grad_bias = mixed[:bias_share]
        grad_patch = mixed[bias_share : bias_share + cols * PIN].reshape(cols, PIN)
        grad_final = mixed[bias_share + cols * PIN :].reshape(cols, PIN)
        pre_time = lax.dynamic_slice(pre_time_all, (me * cols, 0), (cols, all_images))
        grad_pre = to_low(smooth_gate_slope(pre_time) * time_came.reshape(cols, all_images))
        time_sums = jnp.sum(wide(grad_pre), 1)
        near = fold_second(near, far_bits[:-2][::-1])
        grad_expand, grad_reduce = (near[0], near[1])
        both_parts = fold_rows(both_parts, dp_bits[:-3][::-1])
        grad_proj = both_parts[per * unit :]
        grad_time_one = contract(grad_pre, freq_in, 1, 0)

        grad_attend = jnp.zeros((per, unit, D), jnp.float32)
        for turn in range(per):
            piece = lax.ppermute(
                both_parts[turn * unit : (turn + 1) * unit],
                AXES,
                [(int(unit_target[turn, owner]), owner) for owner in range(devices)],
            )
            local = jnp.asarray(unit_send[turn])[me] == jnp.arange(per)
            grad_attend = jnp.where(local[:, None, None], piece[None], grad_attend)
        grad_attend = grad_attend.reshape(per * unit, D)

        grad_embed = jnp.concatenate([grad_patch, grad_time_one], 1)
        grad_square = jnp.stack([grad_time_two, grad_proj], 1)
        squares = sum(
            jnp.sum(piece * piece)
            for piece in (
                grad_patch,
                grad_time_one,
                grad_time_two,
                grad_proj,
                grad_table,
                grad_shift,
                grad_attend,
                grad_expand,
                grad_reduce,
                grad_final,
                grad_bias,
                time_sums,
            )
        )
        late = lax.dynamic_update_slice(
            jnp.zeros((devices * bias_share,), jnp.float32), time_sums, (D + me * cols,)
        ).reshape(devices, bias_share)
        numbers = jnp.stack([loss_local, count_local, squares])
        late = jnp.concatenate([late, jnp.broadcast_to(numbers[None], (devices, 3))], 1)
        late = jnp.sum(exchange(late), 0)
        loss_total, value_count, squared = [late[bias_share + number] for number in range(3)]
        grad_norm = jnp.sqrt(squared)
        factor = LIMIT / jnp.maximum(grad_norm, LIMIT)
        grad_bias = grad_bias + late[:bias_share]

        shards = (
            grad_embed.T,
            jnp.transpose(grad_square, (1, 2, 0)),
            grad_table.T,
            grad_shift.T,
            grad_attend.T,
            grad_expand.T,
            grad_reduce,
            grad_final,
            grad_bias,
        )
        results = [
            adam_step(params_in[number], firsts[number], seconds[number], shards[number], factor)
            for number in range(9)
        ]
        fresh = [results[number][part] for part in range(3) for number in range(9)]
        return tuple([loss_total, value_count, grad_norm] + fresh)

    return on_device


def adam_step(weight, moment, second, gradient, factor):
    clipped = gradient * factor
    moment = BETA_ONE * moment + (1.0 - BETA_ONE) * clipped
    second = BETA_TWO * second + (1.0 - BETA_TWO) * clipped * clipped
    fixed_one = moment / (1.0 - BETA_ONE**STEP)
    fixed_two = second / (1.0 - BETA_TWO**STEP)
    weight = weight - RATE * (fixed_one / (jnp.sqrt(fixed_two) + EPSILON) + DECAY * weight)
    return (weight, moment, second)


def solution(mesh):
    both = ("dp", "seq")
    state = (
        P(None, both),
        P(None, None, both),
        P(None, both),
        P(None, both),
        P(None, both),
        P(None, both),
        P(both, None),
        P(both, None),
        P(both),
    )
    batch = (
        P(None, "dp", "seq", None),
        P(None, "dp", "seq", None),
        P(None, "dp"),
        P(None, "dp"),
        P(None, "dp"),
        P(None, "dp"),
        P(None, "dp", "seq", None, None),
    )
    return jax.shard_map(
        make_step(mesh),
        mesh=mesh,
        in_specs=batch + state * 3,
        out_specs=(P(), P(), P()) + state * 3,
        check_vma=False,
    )
```

time: 2070 us -> 671 us (0.32)
  waiting for transfers between devices: 967 us -> 176 us
  blocking collectives: 467 us -> 0 us
  matrix products: 279 us -> 66.9 us
  Pallas kernels: 0 us -> 91.8 us
  local copies, waits for them, and re-layouts: 185 us -> 108 us
  starting transfers between devices: 51.7 us -> 86.8 us
    reduce_scatter x3 -> x0, waiting for transfers between devices: 692 us -> none  [the longest x1 384 us: on_device(): lax.psum_scatter(totals[3], ('dp', 'seq'), scatter_dimension=1, tiled=True)]
    unnamed x2 -> x0, blocking collectives: 340 us -> none
    dot_general x66 -> x26, matrix products: 279 us -> 66.9 us  [contract(): lax.dot_general(left, right, (((left_dim,), (right_dim,)), ((), ())), pre...]
    all_gather x6 -> x1, waiting for transfers between devices: 188 us -> 0.02 us  [on_device(): lax.all_gather(after(jnp.stack([expand_t, reduce_r]), both_second), AXES,...]
    ppermute x0 -> x32, waiting for transfers between devices: none -> 140 us  [the longest x26 117 us: swap(): lax.ppermute(values_in, AXES, [(place, place ^ 1 << bit) for place in ran...]
    pallas_call x0 -> x5, Pallas kernels: none -> 91.8 us  [the longest x2 45.5 us: hidden_call(): pl.pallas_call(kernel, out_shape=tuple((jax.ShapeDtypeStruct(shape, kind)...]
    all_gather x2 -> x0, blocking collectives: 87.1 us -> none  [the longest x1 43.6 us: on_device(): lax.all_gather(to_low(param_final), ('dp', 'seq'), axis=0, tiled=True)]
    ppermute x0 -> x32, starting transfers between devices: none -> 45.1 us  [the longest x26 28.5 us: swap(): lax.ppermute(values_in, AXES, [(place, place ^ 1 << bit) for place in ran...]
  transfers between devices with their start and end apart: 25 -> 42, of which waited for: 13 -> 20; matrix products, arithmetic and copies ran while one was open for 32% -> 32% of each run, Pallas kernels for 0% -> 4%
where the time goes in v1:
time: 671 us; the launch traced here: 664 us
  waiting for transfers between devices  176 us (26%)
  local copies, waits for them, and re-layouts  108 us (16%)
  other arithmetic  105 us (16%)
  Pallas kernels  91.8 us (14%)
  starting transfers between devices  86.8 us (13%)
  matrix products  66.9 us (10%)
  between operations  28.9 us (4%)
    ppermute x26, waiting for transfers between devices, swap(): lax.ppermute(values_in, AXES, [(place, place ^ 1 << bit) for place in ran...  117 us
    dot_general x26, matrix products, contract(): lax.dot_general(left, right, (((left_dim,), (right_dim,)), ((), ())), pre...  66.9 us
    pallas_call x2, Pallas kernels, hidden_call(): pl.pallas_call(kernel, out_shape=tuple((jax.ShapeDtypeStruct(shape, kind)...  45.5 us
    unnamed x334, local copies, waits for them, and re-layouts  39.3 us
    all_to_all x7, starting transfers between devices, exchange(): lax.all_to_all(values_in, AXES, split_axis=0, concat_axis=0, tiled=True)  33.3 us
    pallas_call x2, Pallas kernels, attend_call(): pl.pallas_call(functools.partial(kernel, masks), out_shape=out_shape, gri...  30.5 us
    ppermute x26, starting transfers between devices, swap(): lax.ppermute(values_in, AXES, [(place, place ^ 1 << bit) for place in ran...  28.5 us
    all_to_all x7, waiting for transfers between devices, exchange(): lax.all_to_all(values_in, AXES, split_axis=0, concat_axis=0, tiled=True)  27.4 us
  transfers between devices with their start and end apart: 42, of which 20 were waited for; matrix products, arithmetic and copies ran while one was open for 32% of the time, Pallas kernels for 4%

profile of v1, /device:TPU:0, one launch (start us, length us, event | category | flops | bytes accessed | tf_op | source)
XLA Modules:
  0.0 663.6 jit_solution(5601585917216045688)
XLA Ops:
  12.5 7.3 %all-to-all-start = ((bf16[32,88,128]{2,1,0:T(8,128)(2,1)}), bf16[32,88,128]{2,1,0:T(8,128)(2,1)S(1)}, u32[]{:S(2)}, u32[]{:S(2)}) async-start(bf16[32,88,128]{2,1,0:T(8,128)(2,1)} %broadcast_in_dim.239), calls=%async_computation | async-start | bytes 1441792 | tf_op jit(solution)/shard_map/all_to_all | solution.py:549
  24.1 14.9 %all-to-all-done = bf16[32,88,128]{2,1,0:T(8,128)(2,1)S(1)} async-done(((bf16[32,88,128]{2,1,0:T(8,128)(2,1)}), bf16[32,88,128]{2,1,0:T(8,128)(2,1)S(1)}, u32[]{:S(2)}, u32[]{:S(2)}) %all-to-all-start) | async-done | bytes 720928 | tf_op jit(solution)/shard_map/all_to_all | solution.py:549
  56.3 13.1 %collective-permute-done.5 = bf16[144,1152]{1,0:T(8,128)(2,1)S(1)} collective-permute-done((bf16[144,1152]{1,0:T(8,128)(2,1)S(1)}, bf16[144,1152]{1,0:T(8,128)(2,1)S(1)}, u32[]{:S(2)}, u32[]{:S(2)}) %collective-permute-start.5) | collective-permute-done | bytes 331808 | tf_op jit(solution)/shard_map/ppermute | solution.py:544
  70.6 14.9 %collective-permute-done.6 = bf16[288,1152]{1,0:T(8,128)(2,1)S(1)} collective-permute-done((bf16[288,1152]{1,0:T(8,128)(2,1)S(1)}, bf16[288,1152]{1,0:T(8,128)(2,1)S(1)}, u32[]{:S(2)}, u32[]{:S(2)}) %collective-permute-start.6) | collective-permute-done | bytes 663584 | tf_op jit(solution)/shard_map/ppermute | solution.py:544
  109.2 9.3 %convolution_add_fusion = f32[1280,1152]{1,0:T(8,128)} fusion(bf16[1280,1072]{1,0:T(8,128)(2,1)} %concatenate.86, f32[1152]{0:T(1024)S(1)} %copy-done.118, bf16[16,1152]{1,0:T(8,128)(2,1)S(1)} %copy.327, bf16[352,1152]{1,0:T(8,128)(2,1)} %get-tuple-element.436, bf16[352,1152]{1,0:T(8,128)(2,1)} %get-tuple-element.435, bf16[352,1152]{1,0:T(8,128)(2,1)S(1)} %fusion.14), kind=kOutput, calls=%fused_computation | convolution fusion | flops 3172810752 | bytes 11117056 | tf_op jit(solution)/shard_map/dot_general | solution.py:50
  121.4 5.9 all-to-all-start.2
  133.9 7.4 %all-to-all-done.2 = f32[32,4,288]{2,1,0:T(4,128)S(1)} async-done(((f32[32,4,288]{2,1,0:T(4,128)}), f32[32,4,288]{2,1,0:T(4,128)S(1)}, u32[]{:S(2)}, u32[]{:S(2)}) %all-to-all-start.2) | async-done | bytes 147488 | tf_op jit(solution)/shard_map/all_to_all | solution.py:549
  143.6 5.3 add_convert_fusion
  149.0 34.9 %collective-permute-done.7 = bf16[576,1152]{1,0:T(8,128)(2,1)S(1)} collective-permute-done((bf16[576,1152]{1,0:T(8,128)(2,1)S(1)}, bf16[576,1152]{1,0:T(8,128)(2,1)S(1)}, u32[]{:S(2)}, u32[]{:S(2)}) %collective-permute-start.7) | collective-permute-done | bytes 1327136 | tf_op jit(solution)/shard_map/ppermute | solution.py:544
  201.2 12.3 %collective-permute-done.8 = bf16[288,1152]{1,0:T(8,128)(2,1)} collective-permute-done((bf16[288,1152]{1,0:T(8,128)(2,1)S(1)}, bf16[288,1152]{1,0:T(8,128)(2,1)}, u32[]{:S(2)}, u32[]{:S(2)}) %collective-permute-start.8) | collective-permute-done | bytes 663584 | tf_op jit(solution)/shard_map/ppermute | solution.py:544
  222.7 13.8 %shard_map.643 = bf16[4,4,80,288]{3,2,1,0:T(8,128)(2,1)} custom-call(s32[5]{0:T(128)S(1)} %pad_add_fusion.meta_ref, bf16[4,4,80,864]{3,2,1,0:T(8,128)(2,1)S(1)} %bitcast.219, bf16[4,4,320,320]{3,2,1,0:T(8,128)(2,1)S(1)} %bitcast.221), custom_call_target="tpu_custom_call" | custom-call | flops 1000 | bytes 1000 | tf_op jit(solution)/shard_map/pallas_call | solution.py:236
  242.4 5.5 convolution_convert_fusion
  247.9 6.2 all-to-all-done.3
  266.0 21.8 %shard_map.644 = (f32[4,640,576]{2,1,0:T(8,128)}, bf16[4,640,576]{2,1,0:T(8,128)(2,1)}, f32[320,1152]{1,0:T(8,128)}, bf16[320,1152]{1,0:T(8,128)(2,1)}) custom-call(s32[16]{0:T(128)} %copy-done.123, bf16[640,1152]{1,0:T(8,128)(2,1)} %pad_maximum_fusion.3.normed_ref, f32[4,1,576]{2,1,0:T(1,128)} %reshape.774.bias_ref, bf16[32,2,144,1152]{3,2,1,0:T(8,128)(2,1)} %bitcast.225), custom_call_target="tpu_custom_call" | custom-call | flops 1000 | bytes 1000 | tf_op jit(solution)/shard_map/pallas_call | solution.py:375
  302.2 23.7 %shard_map.645 = (bf16[4,640,576]{2,1,0:T(8,128)(2,1)}, f32[4,1,576]{2,1,0:T(1,128)}, f32[320,1152]{1,0:T(8,128)}, bf16[320,1152]{1,0:T(8,128)(2,1)}) custom-call(s32[16]{0:T(128)} %copy-done.123, bf16[640,1152]{1,0:T(8,128)(2,1)} %pad_maximum_fusion.4.grad_ref, f32[4,640,576]{2,1,0:T(8,128)} %get-tuple-element.95.up_ref, bf16[32,2,144,1152]{3,2,1,0:T(8,128)(2,1)} %bitcast.226), custom_call_target="tpu_custom_call" | custom-call | flops 1000 | bytes 1000 | tf_op jit(solution)/shard_map/pallas_call | solution.py:375
  326.1 15.7 %shard_map.646 = (bf16[2,288,1152]{2,1,0:T(8,128)(2,1)}, bf16[2,288,1152]{2,1,0:T(8,128)(2,1)}, f32[2,288,1152]{2,1,0:T(8,128)}, bf16[2,288,1152]{2,1,0:T(8,128)...) custom-call(bf16[4,640,576]{2,1,0:T(8,128)(2,1)} %get-tuple-element.98.grad_up_ref, ...), custom_call_target="tpu_custom_call" | custom-call | flops 1000 | bytes 1000 | tf_op jit(solution)/shard_map/pallas_call | solution.py:436
  345.6 5.4 convert_reduce_fusion.1
  360.7 6.3 fusion.17
  387.8 16.8 %shard_map.647 = (bf16[4,4,80,864]{3,2,1,0:T(8,128)(2,1)S(1)}, f32[4,1,864]{2,1,0:T(1,128)S(1)}) custom-call(s32[5]{0:T(128)S(1)} %pad_add_fusion.meta_ref, bf16[4,4,80,864]{3,2,1,0:T(8,128)(2,1)S(1)} %bitcast.220, bf16[4,4,320,320]{3,2,1,0:T(8,128)(2,1)S(1)} %bitcast.222, bf16[4,4,80,288]{3,2,1,0:T(8,128)(2,1)S(1)} %bitcast.223), custom_call_target="tpu_custom_call" | custom-call | flops 1000 | bytes 1000 | tf_op jit(solution)/shard_map/pallas_call | solution.py:236
  428.1 8.4 %collective-permute-done.21 = bf16[288,1152]{1,0:T(8,128)(2,1)S(1)} collective-permute-done((bf16[288,1152]{1,0:T(8,128)(2,1)S(1)}, bf16[288,1152]{1,0:T(8,128)(2,1)S(1)}, u32[]{:S(2)}, u32[]{:S(2)}) %collective-permute-start.21) | collective-permute-done | bytes 663584 | tf_op jit(solution)/shard_map/ppermute | solution.py:544
  448.7 5.1 fusion.19
  547.2 22.7 %collective-permute-done.28 = f32[36,1152]{1,0:T(8,128)S(1)} collective-permute-done((f32[36,1152]{1,0:T(8,128)S(1)}, f32[36,1152]{1,0:T(8,128)S(1)}, u32[]{:S(2)}, u32[]{:S(2)}) %collective-permute-start.28) | collective-permute-done | bytes 165920 | tf_op jit(solution)/shard_map/ppermute | solution.py:968
  584.9 6.2 collective-permute-start.31
  600.5 15.8 %collective-permute-done.31 = bf16[2,144,1152]{2,1,0:T(8,128)(2,1)} collective-permute-done((bf16[2,144,1152]{2,1,0:T(8,128)(2,1)}, bf16[2,144,1152]{2,1,0:T(8,128)(2,1)}, u32[]{:S(2)}, u32[]{:S(2)}) %collective-permute-start.31) | collective-permute-done | bytes 663584 | tf_op jit(solution)/shard_map/ppermute | solution.py:544
  (703 shorter events, 335.8 us)
Async XLA Ops:
  12.5 26.5 %all-to-all-start = ((bf16[32,88,128]{2,1,0:T(8,128)(2,1)}), bf16[32,88,128]{2,1,0:T(8,128)(2,1)S(1)}, u32[]{:S(2)}, u32[]{:S(2)}) async-start(bf16[32,88,128]{2,1,0:T(8,128)(2,1)} %broadcast_in_dim.239), calls=%async_computation | async-start | bytes 1441792 | tf_op jit(solution)/shard_map/all_to_all | solution.py:549
  19.8 246.1 %all-gather.3.cloned.1.call-start = ((), (), s32[]{:S(2)}) async-start(), calls=%async_computation.9 | async-start | bytes 21897216 | tf_op jit(solution)/shard_map/all_gather | solution.py:677
  92.3 26.2 %all-to-all-start.1 = ((bf16[32,2,576]{2,1,0:T(2,128)(2,1)}), bf16[32,2,576]{2,1,0:T(2,128)(2,1)}, u32[]{:S(2)}, u32[]{:S(2)}) async-start(bf16[32,2,576]{2,1,0:T(2,128)(2,1)} %reshape.812), calls=%async_computation.1 | async-start | bytes 163840 | tf_op jit(solution)/shard_map/all_to_all | solution.py:549
  121.4 19.9 %all-to-all-start.2 = ((f32[32,4,288]{2,1,0:T(4,128)}), f32[32,4,288]{2,1,0:T(4,128)S(1)}, u32[]{:S(2)}, u32[]{:S(2)}) async-start(f32[32,4,288]{2,1,0:T(4,128)} %bitcast.13), calls=%async_computation.2 | async-start | bytes 393216 | tf_op jit(solution)/shard_map/all_to_all | solution.py:549
  141.4 42.5 %collective-permute-start.7 = (bf16[576,1152]{1,0:T(8,128)(2,1)S(1)}, bf16[576,1152]{1,0:T(8,128)(2,1)S(1)}, u32[]{:S(2)}, u32[]{:S(2)}) collective-permute-start(bf16[576,1152]{1,0:T(8,128)(2,1)S(1)} %constant_dynamic-update-slice_fusion), channel_id=1, source_target_pairs={{0,4},{1,5},{2,6},{3,7},{4,0},{5,1},{6,2},{7,3},{8,12},{9,13},{10,... | collective-permute-start | bytes 3981320 | tf_op jit(solution)/shard_map/ppermute | solution.py:544
  186.0 27.5 %collective-permute-start.8 = (bf16[288,1152]{1,0:T(8,128)(2,1)S(1)}, bf16[288,1152]{1,0:T(8,128)(2,1)}, u32[]{:S(2)}, u32[]{:S(2)}) collective-permute-start(bf16[288,1152]{1,0:T(8,128)(2,1)S(1)} %reshape.769), channel_id=1, source_target_pairs={{0,2},{1,3},{2,0},{3,1},{4,6},{5,7},{6,4},{7,5},{8,10},{9,11},{10,... | collective-permute-start | bytes 1990664 | tf_op jit(solution)/shard_map/ppermute | solution.py:544
  215.9 24.6 %collective-permute-start.9 = (bf16[576,1152]{1,0:T(8,128)(2,1)}, bf16[576,1152]{1,0:T(8,128)(2,1)}, u32[]{:S(2)}, u32[]{:S(2)}) collective-permute-start(bf16[576,1152]{1,0:T(8,128)(2,1)} %pad_maximum_fusion.5), channel_id=1, source_target_pairs={{0,1},{1,0},{2,3},{3,2},{4,5},{5,4},{6,7},{7,6},{8,9},{9,8},{10,11... | collective-permute-start | bytes 3981320 | tf_op jit(solution)/shard_map/ppermute | solution.py:544
  341.8 31.8 %collective-permute-start.16 = (bf16[2,288,1152]{2,1,0:T(8,128)(2,1)}, bf16[2,288,1152]{2,1,0:T(8,128)(2,1)}, u32[]{:S(2)}, u32[]{:S(2)}) collective-permute-start(bf16[2,288,1152]{2,1,0:T(8,128)(2,1)} %get-tuple-element.107), channel_id=1, source_target_pairs={{0,4},{1,5},{2,6},{3,7},{4,0},{5,1},{6,2},{7,3},{8,12},{9,13},{10,... | collective-permute-start | bytes 3981320 | tf_op jit(solution)/shard_map/ppermute | solution.py:544
  343.2 33.9 %collective-permute-start.15 = (bf16[2,288,1152]{2,1,0:T(8,128)(2,1)}, bf16[2,288,1152]{2,1,0:T(8,128)(2,1)}, u32[]{:S(2)}, u32[]{:S(2)}) collective-permute-start(bf16[2,288,1152]{2,1,0:T(8,128)(2,1)} %get-tuple-element.100), channel_id=1, source_target_pairs={{0,2},{1,3},{2,0},{3,1},{4,6},{5,7},{6,4},{7,5},{8,10},{9,11},{10,... | collective-permute-start | bytes 3981320 | tf_op jit(solution)/shard_map/ppermute | solution.py:544
  356.3 27.8 %all-to-all-start.4 = ((bf16[4,320,288]{1,2,0:T(8,128)(2,1)}), bf16[4,320,288]{1,2,0:T(8,128)(2,1)}, u32[]{:S(2)}, u32[]{:S(2)}) async-start(bf16[4,320,288]{1,2,0:T(8,128)(2,1)} %bitcast.41), calls=%async_computation.4 | async-start | bytes 1769472 | tf_op jit(solution)/shard_map/all_to_all | solution.py:746
  417.9 39.4 %collective-permute-start.19 = (bf16[2,288,1152]{2,1,0:T(8,128)(2,1)}, bf16[2,288,1152]{2,1,0:T(8,128)(2,1)}, u32[]{:S(2)}, u32[]{:S(2)}) collective-permute-start(bf16[2,288,1152]{2,1,0:T(8,128)(2,1)} %get-tuple-element.113), channel_id=1, source_target_pairs={{0,4},{1,5},{2,6},{3,7},{4,0},{5,1},{6,2},{7,3},{8,12},{9,13},{10,... | collective-permute-start | bytes 3981320 | tf_op jit(solution)/shard_map/ppermute | solution.py:544
  418.8 17.8 %collective-permute-start.21 = (bf16[288,1152]{1,0:T(8,128)(2,1)S(1)}, bf16[288,1152]{1,0:T(8,128)(2,1)S(1)}, u32[]{:S(2)}, u32[]{:S(2)}) collective-permute-start(bf16[288,1152]{1,0:T(8,128)(2,1)S(1)} %copy-done.50), channel_id=1, source_target_pairs={{0,2},{1,3},{2,0},{3,1},{4,6},{5,7},{6,4},{7,5},{8,10},{9,11},{10,... | collective-permute-start | bytes 1990664 | tf_op jit(solution)/shard_map/ppermute | solution.py:544
  426.5 34.8 %collective-permute-start.18 = (bf16[320,1152]{1,0:T(8,128)(2,1)}, bf16[320,1152]{1,0:T(8,128)(2,1)}, u32[]{:S(2)}, u32[]{:S(2)}) collective-permute-start(bf16[320,1152]{1,0:T(8,128)(2,1)} %slice.476), channel_id=1, source_target_pairs={{0,2},{1,3},{2,0},{3,1},{4,6},{5,7},{6,4},{7,5},{8,10},{9,11},{10,... | collective-permute-start | bytes 2211848 | tf_op jit(solution)/shard_map/ppermute | solution.py:544
  437.5 44.5 %collective-permute-start.20 = (bf16[2,288,1152]{2,1,0:T(8,128)(2,1)}, bf16[2,288,1152]{2,1,0:T(8,128)(2,1)}, u32[]{:S(2)}, u32[]{:S(2)}) collective-permute-start(bf16[2,288,1152]{2,1,0:T(8,128)(2,1)} %add_convert_fusion.3), channel_id=1, source_target_pairs={{0,2},{1,3},{2,0},{3,1},{4,6},{5,7},{6,4},{7,5},{8,10},{9,11},{10,... | collective-permute-start | bytes 3981320 | tf_op jit(solution)/shard_map/ppermute | solution.py:544
  447.4 45.6 %collective-permute-start.22 = (bf16[576,1152]{1,0:T(8,128)(2,1)}, bf16[576,1152]{1,0:T(8,128)(2,1)}, u32[]{:S(2)}, u32[]{:S(2)}) collective-permute-start(bf16[576,1152]{1,0:T(8,128)(2,1)} %bitcast.53), channel_id=1, source_target_pairs={{0,4},{1,5},{2,6},{3,7},{4,0},{5,1},{6,2},{7,3},{8,12},{9,13},{10,... | collective-permute-start | bytes 3981320 | tf_op jit(solution)/shard_map/ppermute | solution.py:544
  497.1 21.4 %collective-permute-start.23 = (bf16[288,1152]{1,0:T(8,128)(2,1)}, bf16[288,1152]{1,0:T(8,128)(2,1)}, u32[]{:S(2)}, u32[]{:S(2)}) collective-permute-start(bf16[288,1152]{1,0:T(8,128)(2,1)} %slice.478), channel_id=1, source_target_pairs={{0,8},{1,9},{2,10},{3,11},{4,12},{5,13},{6,14},{7,15},{8,0},{9,1},... | collective-permute-start | bytes 1990664 | tf_op jit(solution)/shard_map/ppermute | solution.py:544
  521.5 17.7 %collective-permute-start.27 = (bf16[144,1152]{1,0:T(8,128)(2,1)}, bf16[144,1152]{1,0:T(8,128)(2,1)S(1)}, u32[]{:S(2)}, u32[]{:S(2)}) collective-permute-start(bf16[144,1152]{1,0:T(8,128)(2,1)} %slice.480), channel_id=1, source_target_pairs={{0,16},{1,17},{2,18},{3,19},{4,20},{5,21},{6,22},{7,23},{8,24},{9,... | collective-permute-start | bytes 995336 | tf_op jit(solution)/shard_map/ppermute | solution.py:544
  527.1 51.9 %collective-permute-start.24 = (bf16[2,288,1152]{2,1,0:T(8,128)(2,1)}, bf16[2,288,1152]{2,1,0:T(8,128)(2,1)}, u32[]{:S(2)}, u32[]{:S(2)}) collective-permute-start(bf16[2,288,1152]{2,1,0:T(8,128)(2,1)} %add_convert_fusion.4), channel_id=1, source_target_pairs={{0,4},{1,5},{2,6},{3,7},{4,0},{5,1},{6,2},{7,3},{8,12},{9,13},{10,... | collective-permute-start | bytes 3981320 | tf_op jit(solution)/shard_map/ppermute | solution.py:544
  528.7 50.3 %collective-permute-start.25 = (bf16[2,288,1152]{2,1,0:T(8,128)(2,1)}, bf16[2,288,1152]{2,1,0:T(8,128)(2,1)}, u32[]{:S(2)}, u32[]{:S(2)}) collective-permute-start(bf16[2,288,1152]{2,1,0:T(8,128)(2,1)} %get-tuple-element.127), channel_id=1, source_target_pairs={{0,2},{1,3},{2,0},{3,1},{4,6},{5,7},{6,4},{7,5},{8,10},{9,11},{10,... | collective-permute-start | bytes 3981320 | tf_op jit(solution)/shard_map/ppermute | solution.py:544
  530.2 48.8 %collective-permute-start.26 = (bf16[2,288,1152]{2,1,0:T(8,128)(2,1)}, bf16[2,288,1152]{2,1,0:T(8,128)(2,1)}, u32[]{:S(2)}, u32[]{:S(2)}) collective-permute-start(bf16[2,288,1152]{2,1,0:T(8,128)(2,1)} %add_convert_fusion.2), channel_id=1, source_target_pairs={{0,8},{1,9},{2,10},{3,11},{4,12},{5,13},{6,14},{7,15},{8,0},{9,1},... | collective-permute-start | bytes 3981320 | tf_op jit(solution)/shard_map/ppermute | solution.py:544
  531.7 45.6 %all-to-all-start.7 = ((f32[32,1,2988]{2,1,0:T(1,128)}), f32[32,1,2988]{2,1,0:T(1,128)S(1)}, u32[]{:S(2)}, u32[]{:S(2)}) async-start(f32[32,1,2988]{2,1,0:T(1,128)} %copy.342), calls=%async_computation.7 | async-start | bytes 786432 | tf_op jit(solution)/shard_map/all_to_all | solution.py:549
  540.6 29.3 %collective-permute-start.28 = (f32[36,1152]{1,0:T(8,128)S(1)}, f32[36,1152]{1,0:T(8,128)S(1)}, u32[]{:S(2)}, u32[]{:S(2)}) collective-permute-start(f32[36,1152]{1,0:T(8,128)S(1)} %get-tuple-element.443), channel_id=1, source_target_pairs={{28,0},{0,1},{4,2},{1,3},{5,4},{10,5},{6,6},{14,7},{15,8},{11,9},{... | collective-permute-start | bytes 497672 | tf_op jit(solution)/shard_map/ppermute | solution.py:968
  544.0 33.3 %collective-permute-start.29 = (f32[36,1152]{1,0:T(8,128)S(1)}, f32[36,1152]{1,0:T(8,128)S(1)}, u32[]{:S(2)}, u32[]{:S(2)}) collective-permute-start(f32[36,1152]{1,0:T(8,128)S(1)} %get-tuple-element.442), channel_id=1, source_target_pairs={{4,0},{0,1},{8,2},{1,3},{5,4},{10,5},{6,6},{14,7},{3,8},{15,9},{11... | collective-permute-start | bytes 497672 | tf_op jit(solution)/shard_map/ppermute | solution.py:968
  584.9 31.3 %collective-permute-start.31 = (bf16[2,144,1152]{2,1,0:T(8,128)(2,1)}, bf16[2,144,1152]{2,1,0:T(8,128)(2,1)}, u32[]{:S(2)}, u32[]{:S(2)}) collective-permute-start(bf16[2,144,1152]{2,1,0:T(8,128)(2,1)} %slice.477), channel_id=1, source_target_pairs={{0,16},{1,17},{2,18},{3,19},{4,20},{5,21},{6,22},{7,23},{8,24},{9,... | collective-permute-start | bytes 1990664 | tf_op jit(solution)/shard_map/ppermute | solution.py:544
  (173 other events, 1314.0 us)
Sparse Core Ops, SparseCore 0:
  85.7 150.0 all-gather.2

commit v2 on v1

--- a/solution.py
+++ b/solution.py
@@ -248,21 +248,30 @@
     )(meta, triple, bias_tiles, *grads)
 
 
+PARTS = 3
+
+
 def weight_copies(pick_ref, weight_ref, kind, held_ref, sem_ref):
     rows = weight_ref.shape[2]
-    count = held_ref.shape[1] // rows
+    part = held_ref.shape[0] // PARTS
     copies = []
-    for number in range(4 * count):
-        target = held_ref.at[number // count, pl.ds(number % count * rows, rows)]
+    for number in range(held_ref.shape[0] // rows):
         copies.append(
             (
-                number // count,
+                number * rows // part,
                 pltpu.make_async_copy(
-                    weight_ref.at[pick_ref[number], kind], target, sem_ref.at[kind, number]
+                    weight_ref.at[pick_ref[number], kind],
+                    held_ref.at[pl.ds(number * rows, rows)],
+                    sem_ref.at[kind, number],
                 ),
             )
         )
     return copies
+
+
+def held_part(held_ref):
+    part = held_ref.shape[0] // PARTS
+    return held_ref[pl.ds(pl.multiple_of(pl.program_id(0) * part, part), part), :]
 
 
 def start_copies(groups):
@@ -274,7 +283,7 @@
 
 
 def wait_copies(copies):
-    for quarter in range(4):
+    for quarter in range(PARTS):
 
         @pl.when(pl.program_id(0) == quarter)
         def _():
@@ -316,17 +325,16 @@
     total_ref,
     sem_ref,
 ):
-    quarter = pl.program_id(0)
     expand_copies = weight_copies(pick_ref, weight_ref, 0, expand_held, sem_ref)
     reduce_copies = weight_copies(pick_ref, weight_ref, 1, reduce_held, sem_ref)
     start_copies([expand_copies, reduce_copies])
     wait_copies(expand_copies)
-    upward = contract(normed_ref[...], expand_held[quarter], 1, 1) + bias_ref[0]
+    upward = contract(normed_ref[...], held_part(expand_held), 1, 1) + bias_ref[0]
     up_ref[0] = upward
     active = to_low(gaussian_unit(upward))
     active_ref[0] = active
     wait_copies(reduce_copies)
-    add_up(total_ref, contract(active, reduce_held[quarter], 1, 0))
+    add_up(total_ref, contract(active, held_part(reduce_held), 1, 0))
     put_pair(total_ref, own_ref, sent_ref)
 
 
@@ -344,17 +352,16 @@
     total_ref,
     sem_ref,
 ):
-    quarter = pl.program_id(0)
     expand_copies = weight_copies(pick_ref, weight_ref, 0, expand_held, sem_ref)
     reduce_copies = weight_copies(pick_ref, weight_ref, 1, reduce_held, sem_ref)
     start_copies([reduce_copies, expand_copies])
     wait_copies(reduce_copies)
-    grad_active = contract(grad_ref[...], reduce_held[quarter], 1, 1)
+    grad_active = contract(grad_ref[...], held_part(reduce_held), 1, 1)
     grad_up = to_low(gaussian_slope(up_ref[0]) * grad_active)
     out_ref[0] = grad_up
     sums_ref[0] = jnp.sum(wide(grad_up), 0, keepdims=True)
     wait_copies(expand_copies)
-    add_up(total_ref, contract(grad_up, expand_held[quarter], 1, 0))
+    add_up(total_ref, contract(grad_up, held_part(expand_held), 1, 0))
     put_pair(total_ref, own_ref, sent_ref)
 
 
@@ -367,24 +374,24 @@
     half = pl.BlockSpec((rows // 2, D), lambda quarter, pick_ref: (0, 0))
     if kernel is forward_kernel:
         second_spec, out_specs = (line, (slab, slab, half, half))
-        kinds = (((4, rows, size), jnp.float32), ((4, rows, size), jnp.bfloat16))
+        kinds = (((PARTS, rows, size), jnp.float32), ((PARTS, rows, size), jnp.bfloat16))
     else:
         second_spec, out_specs = (slab, (slab, line, half, half))
-        kinds = (((4, rows, size), jnp.bfloat16), ((4, 1, size), jnp.float32))
+        kinds = (((PARTS, rows, size), jnp.bfloat16), ((PARTS, 1, size), jnp.float32))
     kinds = kinds + (((rows // 2, D), jnp.float32), ((rows // 2, D), jnp.bfloat16))
     return pl.pallas_call(
         kernel,
         out_shape=tuple(jax.ShapeDtypeStruct(shape, kind) for shape, kind in kinds),
         grid_spec=pltpu.PrefetchScalarGridSpec(
             num_scalar_prefetch=1,
-            grid=(4,),
+            grid=(PARTS,),
             in_specs=[whole, second_spec, pl.BlockSpec(memory_space=pl.ANY)],
             out_specs=out_specs,
             scratch_shapes=[
-                pltpu.VMEM((4, size, D), jnp.bfloat16),
-                pltpu.VMEM((4, size, D), jnp.bfloat16),
+                pltpu.VMEM((PARTS * size, D), jnp.bfloat16),
+                pltpu.VMEM((PARTS * size, D), jnp.bfloat16),
                 pltpu.VMEM((rows, D), jnp.float32),
-                pltpu.SemaphoreType.DMA((2, 4 * size // weights.shape[2])),
+                pltpu.SemaphoreType.DMA((2, PARTS * size // weights.shape[2])),
             ],
         ),
         compiler_params=pltpu.CompilerParams(vmem_limit_bytes=56 * 2**20),
@@ -392,51 +399,55 @@
     )(pick, left, second, weights)
 
 
+def piece_ranges(total):
+    eighth = total // 8
+    marks = [(6, 7), (7, 8), (2, 3), (3, 4), (4, 5), (5, 6), (0, 2)]
+    return [(first * eighth, last * eighth) for first, last in marks]
+
+
 def outer_kernel(grad_up_ref, active_ref, normed_ref, grad_ref, *refs):
     outs, held, sem_ref = (refs[:7], refs[7:14], refs[14])
-    step = pl.program_id(0)
-    half = held[0].shape[1]
+    part = grad_up_ref.shape[2]
     products = (
         contract(grad_up_ref[0], normed_ref[...], 0, 0),
         contract(active_ref[0], grad_ref[...], 0, 0),
     )
     copies = [pltpu.make_async_copy(held[at], outs[at], sem_ref.at[at]) for at in range(7)]
-    for turn in range(4):
-
-        @pl.when(step == turn)
+    ranges = piece_ranges(PARTS * part)
+    for turn in range(PARTS):
+        begin = (PARTS - 1 - turn) * part
+
+        @pl.when(pl.program_id(0) == turn)
         def _():
-            if turn == 3:
+            for at, (first, last) in enumerate(ranges):
+                low, high = (max(first, begin), min(last, begin + part))
                 for kind in range(2):
-                    held[6][kind] = products[kind]
-                copies[6].start()
-            else:
-                low_ref, high_ref = (held[2 * turn], held[2 * turn + 1])
-                for kind in range(2):
-                    low_ref[kind] = products[kind][:half].astype(low_ref.dtype)
-                    high_ref[kind] = products[kind][half:].astype(high_ref.dtype)
-                copies[2 * turn].start()
-                copies[2 * turn + 1].start()
-
-    @pl.when(step == 3)
+                    if low < high:
+                        value = products[kind][low - begin : high - begin]
+                        held[at][kind, low - first : high - first] = value.astype(held[at].dtype)
+                if begin <= first < begin + part:
+                    copies[at].start()
+
+    @pl.when(pl.program_id(0) == PARTS - 1)
     def _():
         for copy in copies:
             copy.wait()
 
 
 def outer_call(grad_up, active, normed, grad_down):
-    _, rows, size = grad_up.shape
+    _, rows, part = grad_up.shape
     low, full = (jnp.bfloat16, jnp.float32)
-    kinds = [low, low, full, low, low, full]
-    shapes = [((2, size // 2, D), kind) for kind in kinds] + [((2, size, D), full)]
-    slab = pl.BlockSpec(
-        (1, rows, size),
-        lambda step: (jnp.where(step == 0, 3, jnp.where(step == 3, 0, step)), 0, 0),
-    )
+    kinds = (low, low, full, low, low, full, full)
+    shapes = [
+        ((2, last - first, D), kind)
+        for (first, last), kind in zip(piece_ranges(PARTS * part), kinds)
+    ]
+    slab = pl.BlockSpec((1, rows, part), lambda step: (PARTS - 1 - step, 0, 0))
     whole = pl.BlockSpec((rows, D), lambda step: (0, 0))
     return pl.pallas_call(
         outer_kernel,
         out_shape=tuple(jax.ShapeDtypeStruct(shape, kind) for shape, kind in shapes),
-        grid=(4,),
+        grid=(PARTS,),
         in_specs=[slab, slab, whole, whole],
         out_specs=tuple([pl.BlockSpec(memory_space=pl.ANY)] * 7),
         scratch_shapes=[pltpu.VMEM(shape, kind) for shape, kind in shapes]
@@ -730,17 +741,18 @@
         triple = to_low(contract(normed_one, attend_n, 1, 0) + triple_bias).reshape(
             seq, images, local_slots, 3 * span
         )
+        meta = jnp.concatenate([seq_index.reshape(1), used]).astype(jnp.int32)
+        context = attend_call(slot_masks, meta, triple, bias_all, ())
+
         proj_x = both.reshape(dp, per * unit + cols, D)[:, per * unit :].reshape(dp * cols, D)
         for bit in seq_down:
-            proj_x = after(gather_rows(proj_x, [bit]), triple)
+            proj_x = after(gather_rows(proj_x, [bit]), context)
         slot_block = jnp.asarray(np.array(gather_masks(devices), np.int32)) ^ me
         source = slot_block[:, None] * cols + jnp.arange(cols)[None, :]
         place_proj = to_low(
             (source.reshape(-1)[:, None] == jnp.arange(D)[None, :]).astype(jnp.float32)
         )
         proj_n = to_low(contract(place_proj, proj_x, 0, 0))
-        meta = jnp.concatenate([seq_index.reshape(1), used]).astype(jnp.int32)
-        context = attend_call(slot_masks, meta, triple, bias_all, ())
 
         def over_seq(values_in):
             return lax.all_to_all(values_in, "seq", split_axis=0, concat_axis=0, tiled=True)
@@ -759,7 +771,7 @@
         normed_two = pair_rows(normed_own)
         hidden_bias = jnp.sum(
             jnp.where(hidden_pick[:, :, None], b_expand.reshape(1, devices, hidden_share), 0.0), 1
-        ).reshape(4, 1, size)
+        ).reshape(PARTS, 1, 4 * size // PARTS)
         if hidden_share % 16 == 0:
             hidden_index, weights = (hidden_blocks, gathered)
         else:
@@ -809,7 +821,7 @@
         proj_parts = contract(grad_att_x, merged, 0, 0)
         x_low = to_low(after(x_low, grad_merged) + wide(from_both_low))
         y_high = to_low(after(y_high, grad_merged) + wide(from_both_high))
-        from_x_low = swap(x_low, 2)
+        from_x_low, from_y_high = (swap(x_low, 2), swap(y_high, 1))
         proj_half = proj_parts.shape[0] // 2
         proj_sent = to_low(proj_parts[proj_half:])
         proj_parts = proj_parts[:proj_half] + wide(swap(proj_sent, 0))
@@ -828,6 +840,11 @@
         one_parts = one_kept + wide(swap(one_sent, 0))
         for bit in range(1, seq_bits):
             half = one_parts.shape[0] // 2
+            if bit == seq_bits - 1:
+                near_high = after(near, one_sent)[:, size // 2 :]
+                near_sent = to_low(near_high + wide(from_x_high) + wide(from_y_high))
+                from_high = swap(near_sent, far_bits[-1])
+                one_parts = after(one_parts, near_sent)
             one_last = to_low(one_parts[half:])
             one_came = swap(one_last, bit)
             if bit == seq_bits - 1:
@@ -837,11 +854,9 @@
                 middle = dp * per * unit // 2
                 attend_sent = to_low(contract(grad_units[:, middle:], normed_one, 0, 0))
                 attend_kept = contract(grad_units[:, :middle], normed_one, 0, 0)
-                near_high = after(near, one_last)[:, size // 2 :] + wide(from_x_high)
-                proj_parts = after(proj_parts, one_last) + wide(from_proj)
-                from_y_high = swap(after(y_high, one_last), 1)
-                from_y_low = swap(after(y_low, attend_sent), 1)
-                one_came = after(one_came, (attend_sent, attend_kept, near_high))
+                proj_parts = proj_parts + wide(after(from_proj, attend_sent))
+                from_y_low = swap(after(y_low, one_last), 1)
+                one_came = after(one_came, (attend_sent, attend_kept))
             one_parts = one_parts[:half] + wide(one_came)
         grad_one = one_parts.reshape(images, local_slots, D)
 
@@ -854,7 +869,6 @@
         both_sent = beside(attend_sent, to_low(proj_parts[1]))
         both_parts = beside(attend_kept, proj_parts[0])
         both_half = both_parts.shape[0]
-        from_both = swap(both_sent, dp_bits[-1])
         triple_sums = jnp.sum(triple_sums, 0).reshape(-1)
 
         grad_in_norm, grad_off_one, grad_str_one = stretch_back(
@@ -880,24 +894,6 @@
         grad_mod_sent = jnp.transpose(
             grad_mod_parts.reshape(images, devices, shift_cols), (1, 0, 2)
         )
-        near_sent = to_low(after(near_high, grad_mod_sent) + wide(from_y_high))
-        from_high = swap(near_sent, far_bits[-1])
-        grad_mod = to_low(
-            jnp.sum(
-                after(exchange(grad_mod_sent), near_sent).reshape(dp, seq, images, shift_cols), 1
-            )
-        ).reshape(all_images, shift_cols)
-
-        cond_parts = contract(shift_t, grad_mod, 0, 1).reshape(devices, cols, all_images)
-        both_parts = after(both_parts, cond_parts) + wide(from_both)
-        both_half = both_half // 2
-        both_sent = to_low(both_parts[both_half:])
-        from_both = swap(both_sent, dp_bits[-2])
-        grad_shift = contract(after(grad_mod, cond_parts), cond_act, 0, 1)
-        cond_came = after(exchange(cond_parts), (both_sent, grad_shift))
-        grad_cond = to_low(smooth_gate_slope(condition) * jnp.sum(cond_came, 0))
-        time_parts = contract(square_zero, grad_cond, 0, 0).reshape(devices, cols * all_images)
-
         grad_patch = contract(grad_in, noisy_own, 0, 0)
         grad_final = contract(normed_end, grad_pred, 0, 0)
 
@@ -906,31 +902,47 @@
                 jnp.zeros((D,), jnp.float32), sums, (seq_index * span,)
             )
 
-        def spread_own(sums, length):
-            return lax.dynamic_update_slice(
-                jnp.zeros((length,), jnp.float32), sums, (me * sums.shape[0],)
-            )
-
         up_nat = jnp.sum(
             jnp.where(hidden_pick[:, :, None], up_sums.reshape(-1, 1, hidden_share), 0.0), 0
         )
         bias_parts = jnp.concatenate(
             [
                 jnp.sum(wide(grad_in), 0),
-                jnp.zeros((D,), jnp.float32),
-                spread_own(jnp.sum(wide(grad_cond), 1), D),
-                spread_own(jnp.sum(wide(grad_mod), 0), 8 * D),
+                jnp.zeros((10 * D,), jnp.float32),
                 heads_out(triple_sums[:span]),
                 heads_out(triple_sums[2 * span :]),
                 jnp.sum(wide(grad_att), 0),
                 up_nat.reshape(-1),
                 jnp.sum(wide(grad_down_own), 0),
             ]
-        )
+        ).reshape(devices, bias_share)
+        from_both = swap(after(both_sent, grad_mod_sent), dp_bits[-1])
+        grad_mod = to_low(
+            jnp.sum(
+                after(exchange(grad_mod_sent), bias_parts).reshape(dp, seq, images, shift_cols), 1
+            )
+        ).reshape(all_images, shift_cols)
+
+        cond_parts = contract(shift_t, grad_mod, 0, 1).reshape(devices, cols, all_images)
+        both_parts = after(both_parts, cond_parts) + wide(from_both)
+        both_half = both_half // 2
+        both_sent = to_low(both_parts[both_half:])
+        from_both = swap(both_sent, dp_bits[-2])
+        near_low = after(near, both_sent)[:, : size // 2] + wide(from_x_low) + wide(from_y_low)
+        near = near_low + wide(from_high)
+        if len(far_bits) > 1:
+            near_half = near.shape[1] // 2
+            near_sent = to_low(near[:, near_half:])
+            near_kept = near[:, :near_half]
+        grad_shift = contract(after(grad_mod, cond_parts), cond_act, 0, 1)
+        cond_came = after(exchange(cond_parts), (near_sent, grad_shift))
+        grad_cond = to_low(smooth_gate_slope(condition) * jnp.sum(cond_came, 0))
+        time_parts = contract(square_zero, grad_cond, 0, 0).reshape(devices, cols * all_images)
+
         mixed = jnp.concatenate(
             [
                 time_parts,
-                bias_parts.reshape(devices, bias_share),
+                bias_parts,
                 grad_patch.reshape(devices, cols * PIN),
                 grad_final.reshape(devices, cols * PIN),
             ],
@@ -940,15 +952,11 @@
         both_half = both_half // 2
         both_sent = to_low(both_parts[both_half:])
         both_parts = both_parts[:both_half] + wide(swap(both_sent, dp_bits[-3]))
-        near_low = after(near, time_parts)[:, : size // 2] + wide(from_x_low) + wide(from_y_low)
-        near = near_low + wide(from_high)
         if len(far_bits) > 1:
-            near_half = near.shape[1] // 2
-            near_sent = to_low(near[:, near_half:])
-            near = near[:, :near_half] + wide(swap(near_sent, far_bits[-2]))
+            near_came = swap(after(near_sent, both_sent), far_bits[-2])
         grad_table = contract(after(grad_cond, mixed), onehot, 1, 0)
         grad_time_two = contract(after(grad_cond, mixed), hid_time, 1, 1)
-        mixed = after(exchange(mixed), (both_sent, near_sent, grad_table, grad_time_two))
+        mixed = after(exchange(mixed), (both_sent, grad_table, grad_time_two))
         mixed = jnp.sum(mixed, 0)
         time_came, mixed = (mixed[: cols * all_images], mixed[cols * all_images :])
         grad_bias = mixed[:bias_share]
@@ -957,6 +965,10 @@
         pre_time = lax.dynamic_slice(pre_time_all, (me * cols, 0), (cols, all_images))
         grad_pre = to_low(smooth_gate_slope(pre_time) * time_came.reshape(cols, all_images))
         time_sums = jnp.sum(wide(grad_pre), 1)
+        cond_sums = jnp.sum(wide(after(grad_cond, mixed)), 1)
+        mod_sums = jnp.sum(wide(after(grad_mod, mixed)), 0)
+        if len(far_bits) > 1:
+            near = near_kept + wide(after(near_came, grad_pre))
         near = fold_second(near, far_bits[:-2][::-1])
         grad_expand, grad_reduce = (near[0], near[1])
         both_parts = fold_rows(both_parts, dp_bits[:-3][::-1])
@@ -991,11 +1003,14 @@
                 grad_final,
                 grad_bias,
                 time_sums,
+                cond_sums,
+                mod_sums,
             )
         )
-        late = lax.dynamic_update_slice(
-            jnp.zeros((devices * bias_share,), jnp.float32), time_sums, (D + me * cols,)
-        ).reshape(devices, bias_share)
+        late = jnp.zeros((devices * bias_share,), jnp.float32)
+        for sums, first in ((time_sums, D), (cond_sums, 2 * D), (mod_sums, 3 * D)):
+            late = lax.dynamic_update_slice(late, sums, (first + me * sums.shape[0],))
+        late = late.reshape(devices, bias_share)
         numbers = jnp.stack([loss_local, count_local, squares])
         late = jnp.concatenate([late, jnp.broadcast_to(numbers[None], (devices, 3))], 1)
         late = jnp.sum(exchange(late), 0)

time: 671 us -> 628 us (0.936)
  waiting for transfers between devices: 176 us -> 162 us
  local copies, waits for them, and re-layouts: 108 us -> 95.5 us
  Pallas kernels: 91.8 us -> 84 us
    ppermute x3, waiting for transfers between devices: 23.5 us -> 0.01 us  [on_device(): lax.ppermute(both_parts[turn * unit:(turn + 1) * unit], AXES, [(int(unit_...]
    all_to_all x7, waiting for transfers between devices: 27.4 us -> 48.7 us  [exchange(): lax.all_to_all(values_in, AXES, split_axis=0, concat_axis=0, tiled=True)]
    ppermute x26, waiting for transfers between devices: 117 us -> 105 us  [swap(): lax.ppermute(values_in, AXES, [(place, place ^ 1 << bit) for place in ran...]
    unnamed x334 -> x344, local copies, waits for them, and re-layouts: 39.3 us -> 27.3 us
    pallas_call x2, Pallas kernels: 45.5 us -> 37.4 us  [hidden_call(): pl.pallas_call(kernel, out_shape=tuple((jax.ShapeDtypeStruct(shape, kind)...]
    ppermute x26, starting transfers between devices: 28.5 us -> 20.9 us  [swap(): lax.ppermute(values_in, AXES, [(place, place ^ 1 << bit) for place in ran...]
    convert_element_type x14 -> x15, other arithmetic: 20.5 us -> 21.3 us  [to_low(): return values_in.astype(jnp.bfloat16)]
  transfers between devices with their start and end apart: 42 -> 42, of which waited for: 20 -> 19; matrix products, arithmetic and copies ran while one was open for 32% -> 33% of each run, Pallas kernels for 4% -> 8%
where the time goes in v2:
time: 628 us; the launch traced here: 620 us
  waiting for transfers between devices  162 us (26%)
  other arithmetic  103 us (16%)
  local copies, waits for them, and re-layouts  95.5 us (15%)
  Pallas kernels  84 us (13%)
  starting transfers between devices  80.9 us (13%)
  matrix products  63.8 us (10%)
  between operations  30.4 us (5%)
    ppermute x26, waiting for transfers between devices, swap(): lax.ppermute(values_in, AXES, [(place, place ^ 1 << bit) for place in ran...  105 us
    dot_general x26, matrix products, contract(): lax.dot_general(left, right, (((left_dim,), (right_dim,)), ((), ())), pre...  63.8 us
    all_to_all x7, waiting for transfers between devices, exchange(): lax.all_to_all(values_in, AXES, split_axis=0, concat_axis=0, tiled=True)  48.7 us
    pallas_call x2, Pallas kernels, hidden_call(): pl.pallas_call(kernel, out_shape=tuple((jax.ShapeDtypeStruct(shape, kind)...  37.4 us
    all_to_all x7, starting transfers between devices, exchange(): lax.all_to_all(values_in, AXES, split_axis=0, concat_axis=0, tiled=True)  34.1 us
    pallas_call x2, Pallas kernels, attend_call(): pl.pallas_call(functools.partial(kernel, masks), out_shape=out_shape, gri...  30.5 us
    unnamed x344, local copies, waits for them, and re-layouts  27.3 us
    convert_element_type x15, other arithmetic, to_low(): return values_in.astype(jnp.bfloat16)  21.3 us
  transfers between devices with their start and end apart: 42, of which 19 were waited for; matrix products, arithmetic and copies ran while one was open for 33% of the time, Pallas kernels for 8%

profile of v2, /device:TPU:0, one launch (start us, length us, event | category | flops | bytes accessed | tf_op | source)
XLA Modules:
  0.0 620.1 jit_solution(3745137683773838698)
XLA Ops:
  12.5 7.3 %all-to-all-start = ((bf16[32,88,128]{2,1,0:T(8,128)(2,1)}), bf16[32,88,128]{2,1,0:T(8,128)(2,1)S(1)}, u32[]{:S(2)}, u32[]{:S(2)}) async-start(bf16[32,88,128]{2,1,0:T(8,128)(2,1)} %broadcast_in_dim.239), calls=%async_computation | async-start | bytes 1441792 | tf_op jit(solution)/shard_map/all_to_all | solution.py:560
  24.2 14.8 %all-to-all-done = bf16[32,88,128]{2,1,0:T(8,128)(2,1)S(1)} async-done(((bf16[32,88,128]{2,1,0:T(8,128)(2,1)}), bf16[32,88,128]{2,1,0:T(8,128)(2,1)S(1)}, u32[]{:S(2)}, u32[]{:S(2)}) %all-to-all-start) | async-done | bytes 720928 | tf_op jit(solution)/shard_map/all_to_all | solution.py:560
  56.2 13.2 %collective-permute-done.5 = bf16[144,1152]{1,0:T(8,128)(2,1)S(1)} collective-permute-done((bf16[144,1152]{1,0:T(8,128)(2,1)S(1)}, bf16[144,1152]{1,0:T(8,128)(2,1)S(1)}, u32[]{:S(2)}, u32[]{:S(2)}) %collective-permute-start.5) | collective-permute-done | bytes 331808 | tf_op jit(solution)/shard_map/ppermute | solution.py:555
  70.6 14.9 %collective-permute-done.6 = bf16[288,1152]{1,0:T(8,128)(2,1)S(1)} collective-permute-done((bf16[288,1152]{1,0:T(8,128)(2,1)S(1)}, bf16[288,1152]{1,0:T(8,128)(2,1)S(1)}, u32[]{:S(2)}, u32[]{:S(2)}) %collective-permute-start.6) | collective-permute-done | bytes 663584 | tf_op jit(solution)/shard_map/ppermute | solution.py:555
  107.4 5.1 concatenate.86
  112.5 9.3 %convolution_add_fusion = f32[1280,1152]{1,0:T(8,128)} fusion(bf16[1280,1072]{1,0:T(8,128)(2,1)} %concatenate.86, f32[1152]{0:T(1024)} %get-tuple-element.444, bf16[16,1152]{1,0:T(8,128)(2,1)} %copy.284, bf16[352,1152]{1,0:T(8,128)(2,1)} %get-tuple-element.412, bf16[352,1152]{1,0:T(8,128)(2,1)} %get-tuple-element.411, bf16[352,1152]{1,0:T(8,128)(2,1)S(1)} %fusion.14), kind=kOutput, calls=%fused_computation | convolution fusion | flops 3172810752 | bytes 11117056 | tf_op jit(solution)/shard_map/dot_general | solution.py:50
  123.7 5.9 all-to-all-start.2
  136.2 7.4 %all-to-all-done.2 = f32[32,4,288]{2,1,0:T(4,128)S(1)} async-done(((f32[32,4,288]{2,1,0:T(4,128)}), f32[32,4,288]{2,1,0:T(4,128)S(1)}, u32[]{:S(2)}, u32[]{:S(2)}) %all-to-all-start.2) | async-done | bytes 147488 | tf_op jit(solution)/shard_map/all_to_all | solution.py:560
  146.0 5.3 add_convert_fusion
  151.5 37.2 %collective-permute-done.7 = bf16[576,1152]{1,0:T(8,128)(2,1)S(1)} collective-permute-done((bf16[576,1152]{1,0:T(8,128)(2,1)S(1)}, bf16[576,1152]{1,0:T(8,128)(2,1)S(1)}, u32[]{:S(2)}, u32[]{:S(2)}) %collective-permute-start.7) | collective-permute-done | bytes 1327136 | tf_op jit(solution)/shard_map/ppermute | solution.py:555
  192.3 4.9 convolution_convert_fusion.2
  208.1 13.8 %shard_map.643 = bf16[4,4,80,288]{3,2,1,0:T(8,128)(2,1)} custom-call(s32[5]{0:T(128)S(1)} %pad_add_fusion.meta_ref, bf16[4,4,80,864]{3,2,1,0:T(8,128)(2,1)S(1)} %bitcast.219, bf16[4,4,320,320]{3,2,1,0:T(8,128)(2,1)S(1)} %bitcast.221), custom_call_target="tpu_custom_call" | custom-call | flops 1000 | bytes 1000 | tf_op jit(solution)/shard_map/pallas_call | solution.py:236
  234.4 5.5 convolution_convert_fusion
  239.9 6.2 %all-to-all-done.3 = bf16[4,4,80,288]{3,2,1,0:T(8,128)(2,1)S(1)} async-done(((bf16[4,4,80,288]{3,2,1,0:T(8,128)(2,1)}), bf16[4,4,80,288]{3,2,1,0:T(8,128)(2,1)S(1)}, u32[]{:S(2)}, u32[]{:S(2)}) %all-to-all-start.3) | async-done | bytes 737312 | tf_op jit(solution)/shard_map/all_to_all | solution.py:758
  258.0 17.9 %shard_map.644 = (f32[3,640,768]{2,1,0:T(8,128)}, bf16[3,640,768]{2,1,0:T(8,128)(2,1)}, f32[320,1152]{1,0:T(8,128)}, bf16[320,1152]{1,0:T(8,128)(2,1)}) custom-call(s32[16]{0:T(128)} %copy-done.126, bf16[640,1152]{1,0:T(8,128)(2,1)} %pad_maximum_fusion.3.normed_ref, f32[3,1,768]{2,1,0:T(1,128)} %reshape.774.bias_ref, bf16[32,2,144,1152]{3,2,1,0:T(8,128)(2,1)} %bitcast.225), custom_call_target="tpu_custom_call" | custom-call | flops 1000 | bytes 1000 | tf_op jit(solution)/shard_map/pallas_call | solution.py:382
  289.7 19.6 %shard_map.645 = (bf16[3,640,768]{2,1,0:T(8,128)(2,1)}, f32[3,1,768]{2,1,0:T(1,128)}, f32[320,1152]{1,0:T(8,128)}, bf16[320,1152]{1,0:T(8,128)(2,1)}) custom-call(s32[16]{0:T(128)} %copy-done.126, bf16[640,1152]{1,0:T(8,128)(2,1)} %pad_maximum_fusion.4.grad_ref, f32[3,640,768]{2,1,0:T(8,128)} %get-tuple-element.99.up_ref, bf16[32,2,144,1152]{3,2,1,0:T(8,128)(2,1)} %bitcast.226), custom_call_target="tpu_custom_call" | custom-call | flops 1000 | bytes 1000 | tf_op jit(solution)/shard_map/pallas_call | solution.py:382
  316.9 16.0 %shard_map.646 = (bf16[2,288,1152]{2,1,0:T(8,128)(2,1)}, bf16[2,288,1152]{2,1,0:T(8,128)(2,1)}, f32[2,288,1152]{2,1,0:T(8,128)}, bf16[2,288,1152]{2,1,0:T(8,128)...) custom-call(bf16[3,640,768]{2,1,0:T(8,128)(2,1)} %get-tuple-element.102.grad_up_ref, ...), custom_call_target="tpu_custom_call" | custom-call | flops 1000 | bytes 1000 | tf_op jit(solution)/shard_map/pallas_call | solution.py:447
  338.7 5.4 convert_reduce_fusion.1
  353.8 6.3 %fusion.17 = f32[1152,1152]{1,0:T(8,128)} fusion(bf16[320,1152]{0,1:T(8,128)(2,1)S(1)} %bitcast.268, bf16[320,1152]{1,0:T(8,128)(2,1)} %bitcast.272, s32[1152]{0:T(1024)S(1)} %copy-done.125), kind=kOutput, calls=%fused_computation.105 | convolution fusion | flops 1703043072 | bytes 6787584 | tf_op jit(solution)/shard_map/dot_general | solution.py:50
  380.8 16.8 %shard_map.647 = (bf16[4,4,80,864]{3,2,1,0:T(8,128)(2,1)S(1)}, f32[4,1,864]{2,1,0:T(1,128)S(1)}) custom-call(s32[5]{0:T(128)S(1)} %pad_add_fusion.meta_ref, bf16[4,4,80,864]{3,2,1,0:T(8,128)(2,1)S(1)} %bitcast.220, bf16[4,4,320,320]{3,2,1,0:T(8,128)(2,1)S(1)} %bitcast.222, bf16[4,4,80,288]{3,2,1,0:T(8,128)(2,1)S(1)} %bitcast.223), custom_call_target="tpu_custom_call" | custom-call | flops 1000 | bytes 1000 | tf_op jit(solution)/shard_map/pallas_call | solution.py:236
  452.7 18.1 %all-to-all-done.5 = f32[32,4,288]{2,1,0:T(4,128)S(1)} async-done(((f32[32,4,288]{2,1,0:T(4,128)}), f32[32,4,288]{2,1,0:T(4,128)S(1)}, u32[]{:S(2)}, u32[]{:S(2)}) %all-to-all-start.5) | async-done | bytes 147488 | tf_op jit(solution)/shard_map/all_to_all | solution.py:560
  479.5 7.1 %all-to-all-done.6 = f32[32,1,1152]{2,1,0:T(1,128)S(1)} async-done(((f32[32,1,1152]{2,1,0:T(1,128)}), f32[32,1,1152]{2,1,0:T(1,128)S(1)}, u32[]{:S(2)}, u32[]{:S(2)}) %all-to-all-start.6) | async-done | bytes 147488 | tf_op jit(solution)/shard_map/all_to_all | solution.py:560
  523.7 22.7 %collective-permute-done.27 = bf16[144,1152]{1,0:T(8,128)(2,1)} collective-permute-done((bf16[144,1152]{1,0:T(8,128)(2,1)}, bf16[144,1152]{1,0:T(8,128)(2,1)}, u32[]{:S(2)}, u32[]{:S(2)}) %collective-permute-start.27) | collective-permute-done | bytes 331808 | tf_op jit(solution)/shard_map/ppermute | solution.py:555
  574.4 8.7 %all-to-all-start.8 = ((f32[32,1,687]{2,1,0:T(1,128)}), f32[32,1,687]{2,1,0:T(1,128)}, u32[]{:S(2)}, u32[]{:S(2)}) async-start(f32[32,1,687]{2,1,0:T(1,128)} %all_to_all.45), calls=%async_computation.8 | async-start | bytes 196608 | tf_op jit(solution)/shard_map/all_to_all | solution.py:560
  (712 shorter events, 300.4 us)
Async XLA Ops:
  12.5 26.5 %all-to-all-start = ((bf16[32,88,128]{2,1,0:T(8,128)(2,1)}), bf16[32,88,128]{2,1,0:T(8,128)(2,1)S(1)}, u32[]{:S(2)}, u32[]{:S(2)}) async-start(bf16[32,88,128]{2,1,0:T(8,128)(2,1)} %broadcast_in_dim.239), calls=%async_computation | async-start | bytes 1441792 | tf_op jit(solution)/shard_map/all_to_all | solution.py:560
  19.8 238.1 %all-gather.3.cloned.1.call-start = ((), (), s32[]{:S(2)}) async-start(), calls=%async_computation.9 | async-start | bytes 21897216 | tf_op jit(solution)/shard_map/all_gather | solution.py:688
  92.9 28.9 %all-to-all-start.1 = ((bf16[32,2,576]{2,1,0:T(2,128)(2,1)}), bf16[32,2,576]{2,1,0:T(2,128)(2,1)S(1)}, u32[]{:S(2)}, u32[]{:S(2)}) async-start(bf16[32,2,576]{2,1,0:T(2,128)(2,1)} %reshape.812), calls=%async_computation.1 | async-start | bytes 163840 | tf_op jit(solution)/shard_map/all_to_all | solution.py:560
  123.7 19.9 %all-to-all-start.2 = ((f32[32,4,288]{2,1,0:T(4,128)}), f32[32,4,288]{2,1,0:T(4,128)S(1)}, u32[]{:S(2)}, u32[]{:S(2)}) async-start(f32[32,4,288]{2,1,0:T(4,128)} %bitcast.13), calls=%async_computation.2 | async-start | bytes 393216 | tf_op jit(solution)/shard_map/all_to_all | solution.py:560
  143.8 44.9 %collective-permute-start.7 = (bf16[576,1152]{1,0:T(8,128)(2,1)S(1)}, bf16[576,1152]{1,0:T(8,128)(2,1)S(1)}, u32[]{:S(2)}, u32[]{:S(2)}) collective-permute-start(bf16[576,1152]{1,0:T(8,128)(2,1)S(1)} %constant_dynamic-update-slice_fusion), channel_id=1, source_target_pairs={{0,4},{1,5},{2,6},{3,7},{4,0},{5,1},{6,2},{7,3},{8,12},{9,13},{10,... | collective-permute-start | bytes 3981320 | tf_op jit(solution)/shard_map/ppermute | solution.py:555
  190.7 31.2 %collective-permute-start.8 = (bf16[288,1152]{1,0:T(8,128)(2,1)S(1)}, bf16[288,1152]{1,0:T(8,128)(2,1)}, u32[]{:S(2)}, u32[]{:S(2)}) collective-permute-start(bf16[288,1152]{1,0:T(8,128)(2,1)S(1)} %reshape.769), channel_id=1, source_target_pairs={{0,2},{1,3},{2,0},{3,1},{4,6},{5,7},{6,4},{7,5},{8,10},{9,11},{10,... | collective-permute-start | bytes 1990664 | tf_op jit(solution)/shard_map/ppermute | solution.py:555
  228.5 17.6 %all-to-all-start.3 = ((bf16[4,4,80,288]{3,2,1,0:T(8,128)(2,1)}), bf16[4,4,80,288]{3,2,1,0:T(8,128)(2,1)S(1)}, u32[]{:S(2)}, u32[]{:S(2)}) async-start(bf16[4,4,80,288]{3,2,1,0:T(8,128)(2,1)} %shard_map.643), calls=%async_computation.3 | async-start | bytes 1966080 | tf_op jit(solution)/shard_map/all_to_all | solution.py:758
  309.3 26.4 %collective-permute-start.13 = (bf16[320,1152]{1,0:T(8,128)(2,1)}, bf16[320,1152]{1,0:T(8,128)(2,1)S(1)}, u32[]{:S(2)}, u32[]{:S(2)}) collective-permute-start(bf16[320,1152]{1,0:T(8,128)(2,1)} %get-tuple-element.101), channel_id=1, source_target_pairs={{0,1},{1,0},{2,3},{3,2},{4,5},{5,4},{6,7},{7,6},{8,9},{9,8},{10,11... | collective-permute-start | bytes 2211848 | tf_op jit(solution)/shard_map/ppermute | solution.py:555
  332.9 32.6 %collective-permute-start.16 = (bf16[2,288,1152]{2,1,0:T(8,128)(2,1)}, bf16[2,288,1152]{2,1,0:T(8,128)(2,1)}, u32[]{:S(2)}, u32[]{:S(2)}) collective-permute-start(bf16[2,288,1152]{2,1,0:T(8,128)(2,1)} %get-tuple-element.111), channel_id=1, source_target_pairs={{0,4},{1,5},{2,6},{3,7},{4,0},{5,1},{6,2},{7,3},{8,12},{9,13},{10,... | collective-permute-start | bytes 3981320 | tf_op jit(solution)/shard_map/ppermute | solution.py:555
  335.3 34.1 %collective-permute-start.15 = (bf16[2,288,1152]{2,1,0:T(8,128)(2,1)}, bf16[2,288,1152]{2,1,0:T(8,128)(2,1)}, u32[]{:S(2)}, u32[]{:S(2)}) collective-permute-start(bf16[2,288,1152]{2,1,0:T(8,128)(2,1)} %get-tuple-element.104), channel_id=1, source_target_pairs={{0,2},{1,3},{2,0},{3,1},{4,6},{5,7},{6,4},{7,5},{8,10},{9,11},{10,... | collective-permute-start | bytes 3981320 | tf_op jit(solution)/shard_map/ppermute | solution.py:555
  335.6 74.5 %collective-permute-start.18 = (bf16[2,288,1152]{2,1,0:T(8,128)(2,1)}, bf16[2,288,1152]{2,1,0:T(8,128)(2,1)}, u32[]{:S(2)}, u32[]{:S(2)}) collective-permute-start(bf16[2,288,1152]{2,1,0:T(8,128)(2,1)} %get-tuple-element.116), channel_id=1, source_target_pairs={{0,4},{1,5},{2,6},{3,7},{4,0},{5,1},{6,2},{7,3},{8,12},{9,13},{10,... | collective-permute-start | bytes 3981320 | tf_op jit(solution)/shard_map/ppermute | solution.py:555
  349.4 27.7 %all-to-all-start.4 = ((bf16[4,320,288]{1,2,0:T(8,128)(2,1)}), bf16[4,320,288]{1,2,0:T(8,128)(2,1)}, u32[]{:S(2)}, u32[]{:S(2)}) async-start(bf16[4,320,288]{1,2,0:T(8,128)(2,1)} %bitcast.41), calls=%async_computation.4 | async-start | bytes 1769472 | tf_op jit(solution)/shard_map/all_to_all | solution.py:758
  369.0 41.1 %collective-permute-start.19 = (bf16[2,288,1152]{2,1,0:T(8,128)(2,1)}, bf16[2,288,1152]{2,1,0:T(8,128)(2,1)}, u32[]{:S(2)}, u32[]{:S(2)}) collective-permute-start(bf16[2,288,1152]{2,1,0:T(8,128)(2,1)} %add_convert_fusion.3), channel_id=1, source_target_pairs={{0,2},{1,3},{2,0},{3,1},{4,6},{5,7},{6,4},{7,5},{8,10},{9,11},{10,... | collective-permute-start | bytes 3981320 | tf_op jit(solution)/shard_map/ppermute | solution.py:555
  407.2 87.3 %collective-permute-start.23 = (bf16[2,288,1152]{2,1,0:T(8,128)(2,1)}, bf16[2,288,1152]{2,1,0:T(8,128)(2,1)}, u32[]{:S(2)}, u32[]{:S(2)}) collective-permute-start(bf16[2,288,1152]{2,1,0:T(8,128)(2,1)} %add_convert_fusion.4), channel_id=1, source_target_pairs={{0,4},{1,5},{2,6},{3,7},{4,0},{5,1},{6,2},{7,3},{8,12},{9,13},{10,... | collective-permute-start | bytes 3981320 | tf_op jit(solution)/shard_map/ppermute | solution.py:555
  407.2 17.7 %collective-permute-start.21 = (bf16[288,1152]{1,0:T(8,128)(2,1)S(1)}, bf16[288,1152]{1,0:T(8,128)(2,1)S(1)}, u32[]{:S(2)}, u32[]{:S(2)}) collective-permute-start(bf16[288,1152]{1,0:T(8,128)(2,1)S(1)} %copy-done.54), channel_id=1, source_target_pairs={{0,2},{1,3},{2,0},{3,1},{4,6},{5,7},{6,4},{7,5},{8,10},{9,11},{10,... | collective-permute-start | bytes 1990664 | tf_op jit(solution)/shard_map/ppermute | solution.py:555
  414.3 80.2 %collective-permute-start.25 = (bf16[2,288,1152]{2,1,0:T(8,128)(2,1)}, bf16[2,288,1152]{2,1,0:T(8,128)(2,1)}, u32[]{:S(2)}, u32[]{:S(2)}) collective-permute-start(bf16[2,288,1152]{2,1,0:T(8,128)(2,1)} %add_convert_fusion.2), channel_id=1, source_target_pairs={{0,8},{1,9},{2,10},{3,11},{4,12},{5,13},{6,14},{7,15},{8,0},{9,1},... | collective-permute-start | bytes 3981320 | tf_op jit(solution)/shard_map/ppermute | solution.py:555
  418.7 22.1 %collective-permute-start.20 = (bf16[320,1152]{1,0:T(8,128)(2,1)}, bf16[320,1152]{1,0:T(8,128)(2,1)}, u32[]{:S(2)}, u32[]{:S(2)}) collective-permute-start(bf16[320,1152]{1,0:T(8,128)(2,1)} %slice.480), channel_id=1, source_target_pairs={{0,2},{1,3},{2,0},{3,1},{4,6},{5,7},{6,4},{7,5},{8,10},{9,11},{10,... | collective-permute-start | bytes 2211848 | tf_op jit(solution)/shard_map/ppermute | solution.py:555
  434.0 60.5 %collective-permute-start.24 = (bf16[2,288,1152]{2,1,0:T(8,128)(2,1)}, bf16[2,288,1152]{2,1,0:T(8,128)(2,1)}, u32[]{:S(2)}, u32[]{:S(2)}) collective-permute-start(bf16[2,288,1152]{2,1,0:T(8,128)(2,1)} %get-tuple-element.128), channel_id=1, source_target_pairs={{0,2},{1,3},{2,0},{3,1},{4,6},{5,7},{6,4},{7,5},{8,10},{9,11},{10,... | collective-permute-start | bytes 3981320 | tf_op jit(solution)/shard_map/ppermute | solution.py:555
  448.0 22.8 %all-to-all-start.5 = ((f32[32,4,288]{2,1,0:T(4,128)}), f32[32,4,288]{2,1,0:T(4,128)S(1)}, u32[]{:S(2)}, u32[]{:S(2)}) async-start(f32[32,4,288]{2,1,0:T(4,128)} %copy.293), calls=%async_computation.5 | async-start | bytes 393216 | tf_op jit(solution)/shard_map/all_to_all | solution.py:560
  450.6 38.1 %collective-permute-start.22 = (bf16[576,1152]{1,0:T(8,128)(2,1)}, bf16[576,1152]{1,0:T(8,128)(2,1)}, u32[]{:S(2)}, u32[]{:S(2)}) collective-permute-start(bf16[576,1152]{1,0:T(8,128)(2,1)} %bitcast.262), channel_id=1, source_target_pairs={{0,4},{1,5},{2,6},{3,7},{4,0},{5,1},{6,2},{7,3},{8,12},{9,13},{10,... | collective-permute-start | bytes 3981320 | tf_op jit(solution)/shard_map/ppermute | solution.py:555
  493.0 20.2 %collective-permute-start.26 = (bf16[288,1152]{1,0:T(8,128)(2,1)}, bf16[288,1152]{1,0:T(8,128)(2,1)}, u32[]{:S(2)}, u32[]{:S(2)}) collective-permute-start(bf16[288,1152]{1,0:T(8,128)(2,1)} %slice.482), channel_id=1, source_target_pairs={{0,8},{1,9},{2,10},{3,11},{4,12},{5,13},{6,14},{7,15},{8,0},{9,1},... | collective-permute-start | bytes 1990664 | tf_op jit(solution)/shard_map/ppermute | solution.py:555
  501.8 17.4 %all-to-all-start.7 = ((f32[32,1,2988]{2,1,0:T(1,128)}), f32[32,1,2988]{2,1,0:T(1,128)S(1)}, u32[]{:S(2)}, u32[]{:S(2)}) async-start(f32[32,1,2988]{2,1,0:T(1,128)} %copy.298), calls=%async_computation.7 | async-start | bytes 786432 | tf_op jit(solution)/shard_map/all_to_all | solution.py:560
  516.3 30.1 %collective-permute-start.27 = (bf16[144,1152]{1,0:T(8,128)(2,1)}, bf16[144,1152]{1,0:T(8,128)(2,1)}, u32[]{:S(2)}, u32[]{:S(2)}) collective-permute-start(bf16[144,1152]{1,0:T(8,128)(2,1)} %slice.484), channel_id=1, source_target_pairs={{0,16},{1,17},{2,18},{3,19},{4,20},{5,21},{6,22},{7,23},{8,24},{9,... | collective-permute-start | bytes 995336 | tf_op jit(solution)/shard_map/ppermute | solution.py:555
  519.1 46.9 %collective-permute-start.31 = (bf16[2,144,1152]{2,1,0:T(8,128)(2,1)}, bf16[2,144,1152]{2,1,0:T(8,128)(2,1)}, u32[]{:S(2)}, u32[]{:S(2)}) collective-permute-start(bf16[2,144,1152]{2,1,0:T(8,128)(2,1)} %slice.481), channel_id=1, source_target_pairs={{0,16},{1,17},{2,18},{3,19},{4,20},{5,21},{6,22},{7,23},{8,24},{9,... | collective-permute-start | bytes 1990664 | tf_op jit(solution)/shard_map/ppermute | solution.py:555
  (178 other events, 1197.0 us)
Sparse Core Ops, SparseCore 0:
  85.7 151.9 all-gather.2

commit v3 on v2

--- a/solution.py
+++ b/solution.py
@@ -682,12 +682,6 @@
         noisy_own = noisy_own.reshape(tokens, PIN)
         noisy_all = gather_rows(noisy_own, seq_down)
         cond_own = to_low(smooth_gate(condition))
-        both_first = gather_rows(after(both, hid_time), dp_bits[:1])
-        both_second = gather_rows(after(both_first, cond_own), dp_bits[1:2])
-
-        gathered = lax.all_gather(
-            after(jnp.stack([expand_t, reduce_r]), both_second), AXES, axis=0
-        )
 
         across_late = after(across, cond_own)
         block_of = jnp.asarray(np.array(slot_masks, np.int32)) ^ seq_index
@@ -708,7 +702,14 @@
             )
             + b_patch
         ).reshape(seq, images, local_slots, D)
-        cond_act = after(share_all(cond_own), stream_all).reshape(D, all_images)
+        cond_came = share_all(cond_own)
+        cond_act = cond_came.reshape(D, all_images)
+        both_first = gather_rows(after(both, hid_time), dp_bits[:1])
+        both_second = gather_rows(both_first, dp_bits[1:2])
+
+        gathered = lax.all_gather(
+            after(jnp.stack([expand_t, reduce_r]), (both_second, cond_came)), AXES, axis=0
+        )
         mod_cols = contract(cond_act, shift_t, 0, 1) + mine(b_mod, shift_cols)[:, 0][None, :]
         mod_send = jnp.broadcast_to(
             mod_cols.reshape(dp, 1, images, shift_cols), (dp, seq, images, shift_cols)
@@ -848,8 +849,10 @@
             one_last = to_low(one_parts[half:])
             one_came = swap(one_last, bit)
             if bit == seq_bits - 1:
-                place_own = place_units.reshape(dp, -1, 3 * span)[:, : per * unit]
-                place_own = place_own.reshape(dp * per * unit, 3 * span)
+                own_rows = after(my_rows, one_last).reshape(dp, -1)[:, : per * unit].reshape(-1)
+                place_own = to_low(
+                    (own_rows[:, None] == jnp.arange(3 * span)[None, :]).astype(jnp.float32)
+                )
                 grad_units = to_low(contract(after(grad_triple, one_last), place_own, 1, 1))
                 middle = dp * per * unit // 2
                 attend_sent = to_low(contract(grad_units[:, middle:], normed_one, 0, 0))
@@ -982,7 +985,7 @@
                 AXES,
                 [(int(unit_target[turn, owner]), owner) for owner in range(devices)],
             )
-            local = jnp.asarray(unit_send[turn])[me] == jnp.arange(per)
+            local = after(jnp.asarray(unit_send[turn])[me], both_sent) == jnp.arange(per)
             grad_attend = jnp.where(local[:, None, None], piece[None], grad_attend)
         grad_attend = grad_attend.reshape(per * unit, D)
 

time: 628 us -> 618 us (0.984)
  local copies, waits for them, and re-layouts: 95.5 us -> 88.9 us
    ppermute x26, waiting for transfers between devices: 105 us -> 80.9 us  [swap(): lax.ppermute(values_in, AXES, [(place, place ^ 1 << bit) for place in ran...]
    all_to_all x7, waiting for transfers between devices: 48.7 us -> 61.6 us  [exchange(): lax.all_to_all(values_in, AXES, split_axis=0, concat_axis=0, tiled=True)]
    unnamed x344 -> x343, local copies, waits for them, and re-layouts: 27.3 us -> 29.2 us
    convert_element_type x15 -> x14, other arithmetic: 21.3 us -> 20.7 us  [to_low(): return values_in.astype(jnp.bfloat16)]
  transfers between devices with their start and end apart: 42 -> 42, of which waited for: 19 -> 22; matrix products, arithmetic and copies ran while one was open for 33% -> 32% of each run, Pallas kernels for 8% -> 8%
where the time goes in v3:
time: 618 us; the launch traced here: 612 us
  waiting for transfers between devices  160 us (26%)
  other arithmetic  103 us (17%)
  local copies, waits for them, and re-layouts  88.9 us (14%)
  Pallas kernels  83.8 us (14%)
  starting transfers between devices  81.7 us (13%)
  matrix products  64 us (10%)
  between operations  30.3 us (5%)
    ppermute x26, waiting for transfers between devices, swap(): lax.ppermute(values_in, AXES, [(place, place ^ 1 << bit) for place in ran...  80.9 us
    dot_general x26, matrix products, contract(): lax.dot_general(left, right, (((left_dim,), (right_dim,)), ((), ())), pre...  64 us
    all_to_all x7, waiting for transfers between devices, exchange(): lax.all_to_all(values_in, AXES, split_axis=0, concat_axis=0, tiled=True)  61.6 us
    pallas_call x2, Pallas kernels, hidden_call(): pl.pallas_call(kernel, out_shape=tuple((jax.ShapeDtypeStruct(shape, kind)...  37.3 us
    all_to_all x7, starting transfers between devices, exchange(): lax.all_to_all(values_in, AXES, split_axis=0, concat_axis=0, tiled=True)  33.7 us
    pallas_call x2, Pallas kernels, attend_call(): pl.pallas_call(functools.partial(kernel, masks), out_shape=out_shape, gri...  30.5 us
    unnamed x343, local copies, waits for them, and re-layouts  29.2 us
    ppermute x26, starting transfers between devices, swap(): lax.ppermute(values_in, AXES, [(place, place ^ 1 << bit) for place in ran...  22.2 us
  transfers between devices with their start and end apart: 42, of which 22 were waited for; matrix products, arithmetic and copies ran while one was open for 32% of the time, Pallas kernels for 8%

profile of v3, /device:TPU:0, one launch (start us, length us, event | category | flops | bytes accessed | tf_op | source)
XLA Modules:
  0.0 611.9 jit_solution(16659704340771532568)
XLA Ops:
  12.5 7.3 %all-to-all-start = ((bf16[32,88,128]{2,1,0:T(8,128)(2,1)}), bf16[32,88,128]{2,1,0:T(8,128)(2,1)S(1)}, u32[]{:S(2)}, u32[]{:S(2)}) async-start(bf16[32,88,128]{2,1,0:T(8,128)(2,1)} %broadcast_in_dim.240), calls=%async_computation | async-start | bytes 1441792 | tf_op jit(solution)/shard_map/all_to_all | solution.py:560
  25.1 14.0 %all-to-all-done = bf16[32,88,128]{2,1,0:T(8,128)(2,1)S(1)} async-done(((bf16[32,88,128]{2,1,0:T(8,128)(2,1)}), bf16[32,88,128]{2,1,0:T(8,128)(2,1)S(1)}, u32[]{:S(2)}, u32[]{:S(2)}) %all-to-all-start) | async-done | bytes 720928 | tf_op jit(solution)/shard_map/all_to_all | solution.py:560
  55.6 13.1 %collective-permute-done.5 = bf16[144,1152]{1,0:T(8,128)(2,1)S(1)} collective-permute-done((bf16[144,1152]{1,0:T(8,128)(2,1)S(1)}, bf16[144,1152]{1,0:T(8,128)(2,1)S(1)}, u32[]{:S(2)}, u32[]{:S(2)}) %collective-permute-start.5) | collective-permute-done | bytes 331808 | tf_op jit(solution)/shard_map/ppermute | solution.py:555
  75.3 14.7 %all-to-all-done.1 = bf16[32,2,576]{2,1,0:T(2,128)(2,1)S(1)} async-done(((bf16[32,2,576]{2,1,0:T(2,128)(2,1)}), bf16[32,2,576]{2,1,0:T(2,128)(2,1)S(1)}, u32[]{:S(2)}, u32[]{:S(2)}) %all-to-all-start.1) | async-done | bytes 73760 | tf_op jit(solution)/shard_map/all_to_all | solution.py:560
  102.5 5.0 concatenate.87
  107.5 9.6 %convolution_add_fusion = f32[1280,1152]{1,0:T(8,128)} fusion(bf16[1280,1072]{1,0:T(8,128)(2,1)} %concatenate.87, f32[1152]{0:T(1024)S(1)} %get-tuple-element.448, bf16[16,1152]{1,0:T(8,128)(2,1)S(1)} %copy.284, bf16[352,1152]{1,0:T(8,128)(2,1)} %get-tuple-element.416, bf16[352,1152]{1,0:T(8,128)(2,1)} %get-tuple-element.415, bf16[352,1152]{1,0:T(8,128)(2,1)} %fusion.15), kind=kOutput, calls=%fused_computation | convolution fusion | flops 3172810752 | bytes 11117056 | tf_op jit(solution)/shard_map/dot_general | solution.py:50
  128.1 6.9 %all-to-all-done.2 = f32[32,4,288]{2,1,0:T(4,128)S(1)} async-done(((f32[32,4,288]{2,1,0:T(4,128)}), f32[32,4,288]{2,1,0:T(4,128)S(1)}, u32[]{:S(2)}, u32[]{:S(2)}) %all-to-all-start.2) | async-done | bytes 147488 | tf_op jit(solution)/shard_map/all_to_all | solution.py:560
  137.4 5.4 add_convert_fusion
  142.9 31.0 %collective-permute-done.7 = bf16[576,1152]{1,0:T(8,128)(2,1)S(1)} collective-permute-done((bf16[576,1152]{1,0:T(8,128)(2,1)S(1)}, bf16[576,1152]{1,0:T(8,128)(2,1)S(1)}, u32[]{:S(2)}, u32[]{:S(2)}) %collective-permute-start.7) | collective-permute-done | bytes 1327136 | tf_op jit(solution)/shard_map/ppermute | solution.py:555
  193.2 13.8 %shard_map.643 = bf16[4,4,80,288]{3,2,1,0:T(8,128)(2,1)} custom-call(s32[5]{0:T(128)S(1)} %pad_add_fusion.meta_ref, bf16[4,4,80,864]{3,2,1,0:T(8,128)(2,1)S(1)} %bitcast.218, bf16[4,4,320,320]{3,2,1,0:T(8,128)(2,1)S(1)} %bitcast.220), custom_call_target="tpu_custom_call" | custom-call | flops 1000 | bytes 1000 | tf_op jit(solution)/shard_map/pallas_call | solution.py:236
  220.4 5.5 convolution_convert_fusion
  225.9 9.5 %all-to-all-done.3 = bf16[4,4,80,288]{3,2,1,0:T(8,128)(2,1)S(1)} async-done(((bf16[4,4,80,288]{3,2,1,0:T(8,128)(2,1)}), bf16[4,4,80,288]{3,2,1,0:T(8,128)(2,1)S(1)}, u32[]{:S(2)}, u32[]{:S(2)}) %all-to-all-start.3) | async-done | bytes 737312 | tf_op jit(solution)/shard_map/all_to_all | solution.py:759
  247.3 5.9 all-gather.3.cloned.1.call-done
  253.3 17.8 %shard_map.644 = (f32[3,640,768]{2,1,0:T(8,128)}, bf16[3,640,768]{2,1,0:T(8,128)(2,1)}, f32[320,1152]{1,0:T(8,128)}, bf16[320,1152]{1,0:T(8,128)(2,1)}) custom-call(s32[16]{0:T(128)} %copy-done.129, bf16[640,1152]{1,0:T(8,128)(2,1)} %pad_maximum_fusion.3.normed_ref, f32[3,1,768]{2,1,0:T(1,128)} %reshape.766.bias_ref, bf16[32,2,144,1152]{3,2,1,0:T(8,128)(2,1)} %bitcast.224), custom_call_target="tpu_custom_call" | custom-call | flops 1000 | bytes 1000 | tf_op jit(solution)/shard_map/pallas_call | solution.py:382
  285.5 19.5 %shard_map.645 = (bf16[3,640,768]{2,1,0:T(8,128)(2,1)}, f32[3,1,768]{2,1,0:T(1,128)}, f32[320,1152]{1,0:T(8,128)}, bf16[320,1152]{1,0:T(8,128)(2,1)}) custom-call(s32[16]{0:T(128)} %copy-done.129, bf16[640,1152]{1,0:T(8,128)(2,1)} %pad_maximum_fusion.4.grad_ref, f32[3,640,768]{2,1,0:T(8,128)} %get-tuple-element.99.up_ref, bf16[32,2,144,1152]{3,2,1,0:T(8,128)(2,1)} %bitcast.225), custom_call_target="tpu_custom_call" | custom-call | flops 1000 | bytes 1000 | tf_op jit(solution)/shard_map/pallas_call | solution.py:382
  305.4 16.0 %shard_map.646 = (bf16[2,288,1152]{2,1,0:T(8,128)(2,1)}, bf16[2,288,1152]{2,1,0:T(8,128)(2,1)}, f32[2,288,1152]{2,1,0:T(8,128)}, bf16[2,288,1152]{2,1,0:T(8,128)...) custom-call(bf16[3,640,768]{2,1,0:T(8,128)(2,1)} %get-tuple-element.102.grad_up_ref, ...), custom_call_target="tpu_custom_call" | custom-call | flops 1000 | bytes 1000 | tf_op jit(solution)/shard_map/pallas_call | solution.py:447
  327.6 5.4 convert_reduce_fusion.1
  342.7 6.3 %fusion.18 = f32[1152,1152]{1,0:T(8,128)} fusion(bf16[320,1152]{0,1:T(8,128)(2,1)S(1)} %bitcast.267, bf16[320,1152]{1,0:T(8,128)(2,1)} %bitcast.271, s32[1152]{0:T(1024)S(1)} %copy-done.128), kind=kOutput, calls=%fused_computation.106 | convolution fusion | flops 1703043072 | bytes 6787584 | tf_op jit(solution)/shard_map/dot_general | solution.py:50
  369.2 16.8 %shard_map.647 = (bf16[4,4,80,864]{3,2,1,0:T(8,128)(2,1)S(1)}, f32[4,1,864]{2,1,0:T(1,128)S(1)}) custom-call(s32[5]{0:T(128)S(1)} %pad_add_fusion.meta_ref, bf16[4,4,80,864]{3,2,1,0:T(8,128)(2,1)S(1)} %bitcast.219, bf16[4,4,320,320]{3,2,1,0:T(8,128)(2,1)S(1)} %bitcast.221, bf16[4,4,80,288]{3,2,1,0:T(8,128)(2,1)S(1)} %bitcast.222), custom_call_target="tpu_custom_call" | custom-call | flops 1000 | bytes 1000 | tf_op jit(solution)/shard_map/pallas_call | solution.py:236
  444.5 15.3 %all-to-all-done.5 = f32[32,4,288]{2,1,0:T(4,128)S(1)} async-done(((f32[32,4,288]{2,1,0:T(4,128)}), f32[32,4,288]{2,1,0:T(4,128)S(1)}, u32[]{:S(2)}, u32[]{:S(2)}) %all-to-all-start.5) | async-done | bytes 147488 | tf_op jit(solution)/shard_map/all_to_all | solution.py:560
  469.0 9.6 %all-to-all-done.6 = f32[32,1,1152]{2,1,0:T(1,128)S(1)} async-done(((f32[32,1,1152]{2,1,0:T(1,128)}), f32[32,1,1152]{2,1,0:T(1,128)S(1)}, u32[]{:S(2)}, u32[]{:S(2)}) %all-to-all-start.6) | async-done | bytes 147488 | tf_op jit(solution)/shard_map/all_to_all | solution.py:560
  500.4 5.0 collective-permute-done.26
  517.7 20.6 %collective-permute-done.27 = bf16[144,1152]{1,0:T(8,128)(2,1)} collective-permute-done((bf16[144,1152]{1,0:T(8,128)(2,1)}, bf16[144,1152]{1,0:T(8,128)(2,1)}, u32[]{:S(2)}, u32[]{:S(2)}) %collective-permute-start.27) | collective-permute-done | bytes 331808 | tf_op jit(solution)/shard_map/ppermute | solution.py:555
  566.3 8.6 %all-to-all-start.8 = ((f32[32,1,687]{2,1,0:T(1,128)}), f32[32,1,687]{2,1,0:T(1,128)}, u32[]{:S(2)}, u32[]{:S(2)}) async-start(f32[32,1,687]{2,1,0:T(1,128)} %all_to_all.45), calls=%async_computation.8 | async-start | bytes 196608 | tf_op jit(solution)/shard_map/all_to_all | solution.py:560
  (711 shorter events, 299.0 us)
Async XLA Ops:
  12.5 26.5 %all-to-all-start = ((bf16[32,88,128]{2,1,0:T(8,128)(2,1)}), bf16[32,88,128]{2,1,0:T(8,128)(2,1)S(1)}, u32[]{:S(2)}, u32[]{:S(2)}) async-start(bf16[32,88,128]{2,1,0:T(8,128)(2,1)} %broadcast_in_dim.240), calls=%async_computation | async-start | bytes 1441792 | tf_op jit(solution)/shard_map/all_to_all | solution.py:560
  69.6 20.9 %collective-permute-start.6 = (bf16[288,1152]{1,0:T(8,128)(2,1)}, bf16[288,1152]{1,0:T(8,128)(2,1)}, u32[]{:S(2)}, u32[]{:S(2)}) collective-permute-start(bf16[288,1152]{1,0:T(8,128)(2,1)} %pad_maximum_fusion.7), channel_id=1, source_target_pairs={{0,8},{1,9},{2,10},{3,11},{4,12},{5,13},{6,14},{7,15},{8,0},{9,1},... | collective-permute-start | bytes 1990664 | tf_op jit(solution)/shard_map/ppermute | solution.py:555
  70.7 19.3 %all-to-all-start.1 = ((bf16[32,2,576]{2,1,0:T(2,128)(2,1)}), bf16[32,2,576]{2,1,0:T(2,128)(2,1)S(1)}, u32[]{:S(2)}, u32[]{:S(2)}) async-start(bf16[32,2,576]{2,1,0:T(2,128)(2,1)} %reshape.803), calls=%async_computation.1 | async-start | bytes 163840 | tf_op jit(solution)/shard_map/all_to_all | solution.py:560
  75.0 178.2 %all-gather.3.cloned.1.call-start = ((), (), s32[]{:S(2)}) async-start(), calls=%async_computation.9 | async-start | bytes 21897216 | tf_op jit(solution)/shard_map/all_gather | solution.py:710
  135.2 38.6 %collective-permute-start.7 = (bf16[576,1152]{1,0:T(8,128)(2,1)S(1)}, bf16[576,1152]{1,0:T(8,128)(2,1)S(1)}, u32[]{:S(2)}, u32[]{:S(2)}) collective-permute-start(bf16[576,1152]{1,0:T(8,128)(2,1)S(1)} %constant_dynamic-update-slice_fusion), channel_id=1, source_target_pairs={{0,4},{1,5},{2,6},{3,7},{4,0},{5,1},{6,2},{7,3},{8,12},{9,13},{10,... | collective-permute-start | bytes 3981320 | tf_op jit(solution)/shard_map/ppermute | solution.py:555
  175.8 31.4 %collective-permute-start.8 = (bf16[288,1152]{1,0:T(8,128)(2,1)S(1)}, bf16[288,1152]{1,0:T(8,128)(2,1)}, u32[]{:S(2)}, u32[]{:S(2)}) collective-permute-start(bf16[288,1152]{1,0:T(8,128)(2,1)S(1)} %reshape.761), channel_id=1, source_target_pairs={{0,2},{1,3},{2,0},{3,1},{4,6},{5,7},{6,4},{7,5},{8,10},{9,11},{10,... | collective-permute-start | bytes 1990664 | tf_op jit(solution)/shard_map/ppermute | solution.py:555
  214.5 21.0 %all-to-all-start.3 = ((bf16[4,4,80,288]{3,2,1,0:T(8,128)(2,1)}), bf16[4,4,80,288]{3,2,1,0:T(8,128)(2,1)S(1)}, u32[]{:S(2)}, u32[]{:S(2)}) async-start(bf16[4,4,80,288]{3,2,1,0:T(8,128)(2,1)} %shard_map.643), calls=%async_computation.3 | async-start | bytes 1966080 | tf_op jit(solution)/shard_map/all_to_all | solution.py:759
  305.0 19.6 %collective-permute-start.13 = (bf16[320,1152]{1,0:T(8,128)(2,1)}, bf16[320,1152]{1,0:T(8,128)(2,1)S(1)}, u32[]{:S(2)}, u32[]{:S(2)}) collective-permute-start(bf16[320,1152]{1,0:T(8,128)(2,1)} %get-tuple-element.101), channel_id=1, source_target_pairs={{0,1},{1,0},{2,3},{3,2},{4,5},{5,4},{6,7},{7,6},{8,9},{9,8},{10,11... | collective-permute-start | bytes 2211848 | tf_op jit(solution)/shard_map/ppermute | solution.py:555
  321.4 32.6 %collective-permute-start.16 = (bf16[2,288,1152]{2,1,0:T(8,128)(2,1)}, bf16[2,288,1152]{2,1,0:T(8,128)(2,1)}, u32[]{:S(2)}, u32[]{:S(2)}) collective-permute-start(bf16[2,288,1152]{2,1,0:T(8,128)(2,1)} %get-tuple-element.111), channel_id=1, source_target_pairs={{0,4},{1,5},{2,6},{3,7},{4,0},{5,1},{6,2},{7,3},{8,12},{9,13},{10,... | collective-permute-start | bytes 3981320 | tf_op jit(solution)/shard_map/ppermute | solution.py:555
  323.7 34.5 %collective-permute-start.15 = (bf16[2,288,1152]{2,1,0:T(8,128)(2,1)}, bf16[2,288,1152]{2,1,0:T(8,128)(2,1)}, u32[]{:S(2)}, u32[]{:S(2)}) collective-permute-start(bf16[2,288,1152]{2,1,0:T(8,128)(2,1)} %get-tuple-element.104), channel_id=1, source_target_pairs={{0,2},{1,3},{2,0},{3,1},{4,6},{5,7},{6,4},{7,5},{8,10},{9,11},{10,... | collective-permute-start | bytes 3981320 | tf_op jit(solution)/shard_map/ppermute | solution.py:555
  324.6 74.3 %collective-permute-start.18 = (bf16[2,288,1152]{2,1,0:T(8,128)(2,1)}, bf16[2,288,1152]{2,1,0:T(8,128)(2,1)}, u32[]{:S(2)}, u32[]{:S(2)}) collective-permute-start(bf16[2,288,1152]{2,1,0:T(8,128)(2,1)} %get-tuple-element.116), channel_id=1, source_target_pairs={{0,4},{1,5},{2,6},{3,7},{4,0},{5,1},{6,2},{7,3},{8,12},{9,13},{10,... | collective-permute-start | bytes 3981320 | tf_op jit(solution)/shard_map/ppermute | solution.py:555
  338.3 27.2 %all-to-all-start.4 = ((bf16[4,320,288]{1,2,0:T(8,128)(2,1)}), bf16[4,320,288]{1,2,0:T(8,128)(2,1)}, u32[]{:S(2)}, u32[]{:S(2)}) async-start(bf16[4,320,288]{1,2,0:T(8,128)(2,1)} %bitcast.41), calls=%async_computation.4 | async-start | bytes 1769472 | tf_op jit(solution)/shard_map/all_to_all | solution.py:759
  357.4 41.5 %collective-permute-start.19 = (bf16[2,288,1152]{2,1,0:T(8,128)(2,1)}, bf16[2,288,1152]{2,1,0:T(8,128)(2,1)}, u32[]{:S(2)}, u32[]{:S(2)}) collective-permute-start(bf16[2,288,1152]{2,1,0:T(8,128)(2,1)} %add_convert_fusion.3), channel_id=1, source_target_pairs={{0,2},{1,3},{2,0},{3,1},{4,6},{5,7},{6,4},{7,5},{8,10},{9,11},{10,... | collective-permute-start | bytes 3981320 | tf_op jit(solution)/shard_map/ppermute | solution.py:555
  396.0 90.4 %collective-permute-start.23 = (bf16[2,288,1152]{2,1,0:T(8,128)(2,1)}, bf16[2,288,1152]{2,1,0:T(8,128)(2,1)}, u32[]{:S(2)}, u32[]{:S(2)}) collective-permute-start(bf16[2,288,1152]{2,1,0:T(8,128)(2,1)} %add_convert_fusion.4), channel_id=1, source_target_pairs={{0,4},{1,5},{2,6},{3,7},{4,0},{5,1},{6,2},{7,3},{8,12},{9,13},{10,... | collective-permute-start | bytes 3981320 | tf_op jit(solution)/shard_map/ppermute | solution.py:555
  396.1 19.4 %collective-permute-start.21 = (bf16[288,1152]{1,0:T(8,128)(2,1)}, bf16[288,1152]{1,0:T(8,128)(2,1)}, u32[]{:S(2)}, u32[]{:S(2)}) collective-permute-start(bf16[288,1152]{1,0:T(8,128)(2,1)} %slice.483), channel_id=1, source_target_pairs={{0,2},{1,3},{2,0},{3,1},{4,6},{5,7},{6,4},{7,5},{8,10},{9,11},{10,... | collective-permute-start | bytes 1990664 | tf_op jit(solution)/shard_map/ppermute | solution.py:555
  403.1 83.3 %collective-permute-start.25 = (bf16[2,288,1152]{2,1,0:T(8,128)(2,1)}, bf16[2,288,1152]{2,1,0:T(8,128)(2,1)}, u32[]{:S(2)}, u32[]{:S(2)}) collective-permute-start(bf16[2,288,1152]{2,1,0:T(8,128)(2,1)} %add_convert_fusion.2), channel_id=1, source_target_pairs={{0,8},{1,9},{2,10},{3,11},{4,12},{5,13},{6,14},{7,15},{8,0},{9,1},... | collective-permute-start | bytes 3981320 | tf_op jit(solution)/shard_map/ppermute | solution.py:555
  409.4 20.6 %collective-permute-start.20 = (bf16[320,1152]{1,0:T(8,128)(2,1)}, bf16[320,1152]{1,0:T(8,128)(2,1)}, u32[]{:S(2)}, u32[]{:S(2)}) collective-permute-start(bf16[320,1152]{1,0:T(8,128)(2,1)} %slice.480), channel_id=1, source_target_pairs={{0,2},{1,3},{2,0},{3,1},{4,6},{5,7},{6,4},{7,5},{8,10},{9,11},{10,... | collective-permute-start | bytes 2211848 | tf_op jit(solution)/shard_map/ppermute | solution.py:555
  425.6 60.8 %collective-permute-start.24 = (bf16[2,288,1152]{2,1,0:T(8,128)(2,1)}, bf16[2,288,1152]{2,1,0:T(8,128)(2,1)}, u32[]{:S(2)}, u32[]{:S(2)}) collective-permute-start(bf16[2,288,1152]{2,1,0:T(8,128)(2,1)} %get-tuple-element.129), channel_id=1, source_target_pairs={{0,2},{1,3},{2,0},{3,1},{4,6},{5,7},{6,4},{7,5},{8,10},{9,11},{10,... | collective-permute-start | bytes 3981320 | tf_op jit(solution)/shard_map/ppermute | solution.py:555
  437.9 21.9 %all-to-all-start.5 = ((f32[32,4,288]{2,1,0:T(4,128)}), f32[32,4,288]{2,1,0:T(4,128)S(1)}, u32[]{:S(2)}, u32[]{:S(2)}) async-start(f32[32,4,288]{2,1,0:T(4,128)} %copy.293), calls=%async_computation.5 | async-start | bytes 393216 | tf_op jit(solution)/shard_map/all_to_all | solution.py:560
  442.5 38.3 %collective-permute-start.22 = (bf16[576,1152]{1,0:T(8,128)(2,1)}, bf16[576,1152]{1,0:T(8,128)(2,1)}, u32[]{:S(2)}, u32[]{:S(2)}) collective-permute-start(bf16[576,1152]{1,0:T(8,128)(2,1)} %bitcast.261), channel_id=1, source_target_pairs={{0,4},{1,5},{2,6},{3,7},{4,0},{5,1},{6,2},{7,3},{8,12},{9,13},{10,... | collective-permute-start | bytes 3981320 | tf_op jit(solution)/shard_map/ppermute | solution.py:555
  485.0 20.4 %collective-permute-start.26 = (bf16[288,1152]{1,0:T(8,128)(2,1)}, bf16[288,1152]{1,0:T(8,128)(2,1)}, u32[]{:S(2)}, u32[]{:S(2)}) collective-permute-start(bf16[288,1152]{1,0:T(8,128)(2,1)} %slice.482), channel_id=1, source_target_pairs={{0,8},{1,9},{2,10},{3,11},{4,12},{5,13},{6,14},{7,15},{8,0},{9,1},... | collective-permute-start | bytes 1990664 | tf_op jit(solution)/shard_map/ppermute | solution.py:555
  493.7 19.6 %all-to-all-start.7 = ((f32[32,1,2988]{2,1,0:T(1,128)}), f32[32,1,2988]{2,1,0:T(1,128)S(1)}, u32[]{:S(2)}, u32[]{:S(2)}) async-start(f32[32,1,2988]{2,1,0:T(1,128)} %copy.298), calls=%async_computation.7 | async-start | bytes 786432 | tf_op jit(solution)/shard_map/all_to_all | solution.py:560
  508.4 29.9 %collective-permute-start.27 = (bf16[144,1152]{1,0:T(8,128)(2,1)}, bf16[144,1152]{1,0:T(8,128)(2,1)}, u32[]{:S(2)}, u32[]{:S(2)}) collective-permute-start(bf16[144,1152]{1,0:T(8,128)(2,1)} %slice.484), channel_id=1, source_target_pairs={{0,16},{1,17},{2,18},{3,19},{4,20},{5,21},{6,22},{7,23},{8,24},{9,... | collective-permute-start | bytes 995336 | tf_op jit(solution)/shard_map/ppermute | solution.py:555
  511.0 46.9 %collective-permute-start.31 = (bf16[2,144,1152]{2,1,0:T(8,128)(2,1)}, bf16[2,144,1152]{2,1,0:T(8,128)(2,1)}, u32[]{:S(2)}, u32[]{:S(2)}) collective-permute-start(bf16[2,144,1152]{2,1,0:T(8,128)(2,1)} %slice.481), channel_id=1, source_target_pairs={{0,16},{1,17},{2,18},{3,19},{4,20},{5,21},{6,22},{7,23},{8,24},{9,... | collective-permute-start | bytes 1990664 | tf_op jit(solution)/shard_map/ppermute | solution.py:555
  (177 other events, 1231.3 us)
Sparse Core Ops, SparseCore 0:
  91.8 161.3 all-gather.2

commit v4 on v3

--- a/solution.py
+++ b/solution.py
@@ -956,7 +956,7 @@
         both_sent = to_low(both_parts[both_half:])
         both_parts = both_parts[:both_half] + wide(swap(both_sent, dp_bits[-3]))
         if len(far_bits) > 1:
-            near_came = swap(after(near_sent, both_sent), far_bits[-2])
+            near_came = swap(after(near_sent, both_parts), far_bits[-2])
         grad_table = contract(after(grad_cond, mixed), onehot, 1, 0)
         grad_time_two = contract(after(grad_cond, mixed), hid_time, 1, 1)
         mixed = after(exchange(mixed), (both_sent, grad_table, grad_time_two))

time: 618 us -> 621 us (level)
  transfers between devices with their start and end apart: 42 -> 42, of which waited for: 22 -> 23; matrix products, arithmetic and copies ran while one was open for 32% -> 31% of each run, Pallas kernels for 8% -> 8%
where the time goes in v4:
time: 621 us; the launch traced here: 616 us
  waiting for transfers between devices  161 us (26%)
  other arithmetic  103 us (17%)
  local copies, waits for them, and re-layouts  88.9 us (14%)
  starting transfers between devices  83.9 us (14%)
  Pallas kernels  83.8 us (13%)
  matrix products  64 us (10%)
  between operations  30.3 us (5%)
    ppermute x26, waiting for transfers between devices, swap(): lax.ppermute(values_in, AXES, [(place, place ^ 1 << bit) for place in ran...  77.6 us
    dot_general x26, matrix products, contract(): lax.dot_general(left, right, (((left_dim,), (right_dim,)), ((), ())), pre...  64 us
    all_to_all x7, waiting for transfers between devices, exchange(): lax.all_to_all(values_in, AXES, split_axis=0, concat_axis=0, tiled=True)  61.6 us
    pallas_call x2, Pallas kernels, hidden_call(): pl.pallas_call(kernel, out_shape=tuple((jax.ShapeDtypeStruct(shape, kind)...  37.3 us
    all_to_all x7, starting transfers between devices, exchange(): lax.all_to_all(values_in, AXES, split_axis=0, concat_axis=0, tiled=True)  34.8 us
    pallas_call x2, Pallas kernels, attend_call(): pl.pallas_call(functools.partial(kernel, masks), out_shape=out_shape, gri...  30.5 us
    unnamed x343, local copies, waits for them, and re-layouts  29.2 us
    ppermute x26, starting transfers between devices, swap(): lax.ppermute(values_in, AXES, [(place, place ^ 1 << bit) for place in ran...  21.9 us
  transfers between devices with their start and end apart: 42, of which 23 were waited for; matrix products, arithmetic and copies ran while one was open for 31% of the time, Pallas kernels for 8%

profile of v4, /device:TPU:0, one launch (start us, length us, event | category | flops | bytes accessed | tf_op | source)
XLA Modules:
  0.0 615.5 jit_solution(2285542952312941577)
XLA Ops:
  12.5 7.3 %all-to-all-start = ((bf16[32,88,128]{2,1,0:T(8,128)(2,1)}), bf16[32,88,128]{2,1,0:T(8,128)(2,1)S(1)}, u32[]{:S(2)}, u32[]{:S(2)}) async-start(bf16[32,88,128]{2,1,0:T(8,128)(2,1)} %broadcast_in_dim.240), calls=%async_computation | async-start | bytes 1441792 | tf_op jit(solution)/shard_map/all_to_all | solution.py:560
  25.1 14.0 %all-to-all-done = bf16[32,88,128]{2,1,0:T(8,128)(2,1)S(1)} async-done(((bf16[32,88,128]{2,1,0:T(8,128)(2,1)}), bf16[32,88,128]{2,1,0:T(8,128)(2,1)S(1)}, u32[]{:S(2)}, u32[]{:S(2)}) %all-to-all-start) | async-done | bytes 720928 | tf_op jit(solution)/shard_map/all_to_all | solution.py:560
  55.6 13.1 %collective-permute-done.5 = bf16[144,1152]{1,0:T(8,128)(2,1)S(1)} collective-permute-done((bf16[144,1152]{1,0:T(8,128)(2,1)S(1)}, bf16[144,1152]{1,0:T(8,128)(2,1)S(1)}, u32[]{:S(2)}, u32[]{:S(2)}) %collective-permute-start.5) | collective-permute-done | bytes 331808 | tf_op jit(solution)/shard_map/ppermute | solution.py:555
  75.3 14.7 %all-to-all-done.1 = bf16[32,2,576]{2,1,0:T(2,128)(2,1)S(1)} async-done(((bf16[32,2,576]{2,1,0:T(2,128)(2,1)}), bf16[32,2,576]{2,1,0:T(2,128)(2,1)S(1)}, u32[]{:S(2)}, u32[]{:S(2)}) %all-to-all-start.1) | async-done | bytes 73760 | tf_op jit(solution)/shard_map/all_to_all | solution.py:560
  102.5 5.0 concatenate.87
  107.5 9.6 %convolution_add_fusion = f32[1280,1152]{1,0:T(8,128)} fusion(bf16[1280,1072]{1,0:T(8,128)(2,1)} %concatenate.87, f32[1152]{0:T(1024)S(1)} %get-tuple-element.448, bf16[16,1152]{1,0:T(8,128)(2,1)S(1)} %copy.284, bf16[352,1152]{1,0:T(8,128)(2,1)} %get-tuple-element.416, bf16[352,1152]{1,0:T(8,128)(2,1)} %get-tuple-element.415, bf16[352,1152]{1,0:T(8,128)(2,1)} %fusion.15), kind=kOutput, calls=%fused_computation | convolution fusion | flops 3172810752 | bytes 11117056 | tf_op jit(solution)/shard_map/dot_general | solution.py:50
  128.1 6.9 %all-to-all-done.2 = f32[32,4,288]{2,1,0:T(4,128)S(1)} async-done(((f32[32,4,288]{2,1,0:T(4,128)}), f32[32,4,288]{2,1,0:T(4,128)S(1)}, u32[]{:S(2)}, u32[]{:S(2)}) %all-to-all-start.2) | async-done | bytes 147488 | tf_op jit(solution)/shard_map/all_to_all | solution.py:560
  137.4 5.4 add_convert_fusion
  142.9 31.0 %collective-permute-done.7 = bf16[576,1152]{1,0:T(8,128)(2,1)S(1)} collective-permute-done((bf16[576,1152]{1,0:T(8,128)(2,1)S(1)}, bf16[576,1152]{1,0:T(8,128)(2,1)S(1)}, u32[]{:S(2)}, u32[]{:S(2)}) %collective-permute-start.7) | collective-permute-done | bytes 1327136 | tf_op jit(solution)/shard_map/ppermute | solution.py:555
  193.2 13.8 %shard_map.643 = bf16[4,4,80,288]{3,2,1,0:T(8,128)(2,1)} custom-call(s32[5]{0:T(128)S(1)} %pad_add_fusion.meta_ref, bf16[4,4,80,864]{3,2,1,0:T(8,128)(2,1)S(1)} %bitcast.218, bf16[4,4,320,320]{3,2,1,0:T(8,128)(2,1)S(1)} %bitcast.220), custom_call_target="tpu_custom_call" | custom-call | flops 1000 | bytes 1000 | tf_op jit(solution)/shard_map/pallas_call | solution.py:236
  220.4 5.5 convolution_convert_fusion
  225.9 9.5 %all-to-all-done.3 = bf16[4,4,80,288]{3,2,1,0:T(8,128)(2,1)S(1)} async-done(((bf16[4,4,80,288]{3,2,1,0:T(8,128)(2,1)}), bf16[4,4,80,288]{3,2,1,0:T(8,128)(2,1)S(1)}, u32[]{:S(2)}, u32[]{:S(2)}) %all-to-all-start.3) | async-done | bytes 737312 | tf_op jit(solution)/shard_map/all_to_all | solution.py:759
  247.3 5.9 all-gather.3.cloned.1.call-done
  253.3 17.8 %shard_map.644 = (f32[3,640,768]{2,1,0:T(8,128)}, bf16[3,640,768]{2,1,0:T(8,128)(2,1)}, f32[320,1152]{1,0:T(8,128)}, bf16[320,1152]{1,0:T(8,128)(2,1)}) custom-call(s32[16]{0:T(128)} %copy-done.129, bf16[640,1152]{1,0:T(8,128)(2,1)} %pad_maximum_fusion.3.normed_ref, f32[3,1,768]{2,1,0:T(1,128)} %reshape.766.bias_ref, bf16[32,2,144,1152]{3,2,1,0:T(8,128)(2,1)} %bitcast.224), custom_call_target="tpu_custom_call" | custom-call | flops 1000 | bytes 1000 | tf_op jit(solution)/shard_map/pallas_call | solution.py:382
  285.5 19.5 %shard_map.645 = (bf16[3,640,768]{2,1,0:T(8,128)(2,1)}, f32[3,1,768]{2,1,0:T(1,128)}, f32[320,1152]{1,0:T(8,128)}, bf16[320,1152]{1,0:T(8,128)(2,1)}) custom-call(s32[16]{0:T(128)} %copy-done.129, bf16[640,1152]{1,0:T(8,128)(2,1)} %pad_maximum_fusion.4.grad_ref, f32[3,640,768]{2,1,0:T(8,128)} %get-tuple-element.99.up_ref, bf16[32,2,144,1152]{3,2,1,0:T(8,128)(2,1)} %bitcast.225), custom_call_target="tpu_custom_call" | custom-call | flops 1000 | bytes 1000 | tf_op jit(solution)/shard_map/pallas_call | solution.py:382
  305.4 16.0 %shard_map.646 = (bf16[2,288,1152]{2,1,0:T(8,128)(2,1)}, bf16[2,288,1152]{2,1,0:T(8,128)(2,1)}, f32[2,288,1152]{2,1,0:T(8,128)}, bf16[2,288,1152]{2,1,0:T(8,128)...) custom-call(bf16[3,640,768]{2,1,0:T(8,128)(2,1)} %get-tuple-element.102.grad_up_ref, ...), custom_call_target="tpu_custom_call" | custom-call | flops 1000 | bytes 1000 | tf_op jit(solution)/shard_map/pallas_call | solution.py:447
  327.6 5.4 convert_reduce_fusion.1
  342.7 6.3 %fusion.18 = f32[1152,1152]{1,0:T(8,128)} fusion(bf16[320,1152]{0,1:T(8,128)(2,1)S(1)} %bitcast.267, bf16[320,1152]{1,0:T(8,128)(2,1)} %bitcast.271, s32[1152]{0:T(1024)S(1)} %copy-done.128), kind=kOutput, calls=%fused_computation.106 | convolution fusion | flops 1703043072 | bytes 6787584 | tf_op jit(solution)/shard_map/dot_general | solution.py:50
  369.2 16.8 %shard_map.647 = (bf16[4,4,80,864]{3,2,1,0:T(8,128)(2,1)S(1)}, f32[4,1,864]{2,1,0:T(1,128)S(1)}) custom-call(s32[5]{0:T(128)S(1)} %pad_add_fusion.meta_ref, bf16[4,4,80,864]{3,2,1,0:T(8,128)(2,1)S(1)} %bitcast.219, bf16[4,4,320,320]{3,2,1,0:T(8,128)(2,1)S(1)} %bitcast.221, bf16[4,4,80,288]{3,2,1,0:T(8,128)(2,1)S(1)} %bitcast.222), custom_call_target="tpu_custom_call" | custom-call | flops 1000 | bytes 1000 | tf_op jit(solution)/shard_map/pallas_call | solution.py:236
  444.5 15.3 %all-to-all-done.5 = f32[32,4,288]{2,1,0:T(4,128)S(1)} async-done(((f32[32,4,288]{2,1,0:T(4,128)}), f32[32,4,288]{2,1,0:T(4,128)S(1)}, u32[]{:S(2)}, u32[]{:S(2)}) %all-to-all-start.5) | async-done | bytes 147488 | tf_op jit(solution)/shard_map/all_to_all | solution.py:560
  469.0 9.6 %all-to-all-done.6 = f32[32,1,1152]{2,1,0:T(1,128)S(1)} async-done(((f32[32,1,1152]{2,1,0:T(1,128)}), f32[32,1,1152]{2,1,0:T(1,128)S(1)}, u32[]{:S(2)}, u32[]{:S(2)}) %all-to-all-start.6) | async-done | bytes 147488 | tf_op jit(solution)/shard_map/all_to_all | solution.py:560
  516.8 6.6 %collective-permute-done.27 = bf16[144,1152]{1,0:T(8,128)(2,1)} collective-permute-done((bf16[144,1152]{1,0:T(8,128)(2,1)}, bf16[144,1152]{1,0:T(8,128)(2,1)}, u32[]{:S(2)}, u32[]{:S(2)}) %collective-permute-start.27) | collective-permute-done | bytes 331808 | tf_op jit(solution)/shard_map/ppermute | solution.py:555
  547.8 12.6 %collective-permute-done.31 = bf16[2,144,1152]{2,1,0:T(8,128)(2,1)} collective-permute-done((bf16[2,144,1152]{2,1,0:T(8,128)(2,1)}, bf16[2,144,1152]{2,1,0:T(8,128)(2,1)}, u32[]{:S(2)}, u32[]{:S(2)}) %collective-permute-start.31) | collective-permute-done | bytes 663584 | tf_op jit(solution)/shard_map/ppermute | solution.py:555
  568.7 9.7 %all-to-all-start.8 = ((f32[32,1,687]{2,1,0:T(1,128)}), f32[32,1,687]{2,1,0:T(1,128)}, u32[]{:S(2)}, u32[]{:S(2)}) async-start(f32[32,1,687]{2,1,0:T(1,128)} %all_to_all.45), calls=%async_computation.8 | async-start | bytes 196608 | tf_op jit(solution)/shard_map/all_to_all | solution.py:560
  (711 shorter events, 307.9 us)
Async XLA Ops:
  12.5 26.5 %all-to-all-start = ((bf16[32,88,128]{2,1,0:T(8,128)(2,1)}), bf16[32,88,128]{2,1,0:T(8,128)(2,1)S(1)}, u32[]{:S(2)}, u32[]{:S(2)}) async-start(bf16[32,88,128]{2,1,0:T(8,128)(2,1)} %broadcast_in_dim.240), calls=%async_computation | async-start | bytes 1441792 | tf_op jit(solution)/shard_map/all_to_all | solution.py:560
  69.6 20.9 %collective-permute-start.6 = (bf16[288,1152]{1,0:T(8,128)(2,1)}, bf16[288,1152]{1,0:T(8,128)(2,1)}, u32[]{:S(2)}, u32[]{:S(2)}) collective-permute-start(bf16[288,1152]{1,0:T(8,128)(2,1)} %pad_maximum_fusion.7), channel_id=1, source_target_pairs={{0,8},{1,9},{2,10},{3,11},{4,12},{5,13},{6,14},{7,15},{8,0},{9,1},... | collective-permute-start | bytes 1990664 | tf_op jit(solution)/shard_map/ppermute | solution.py:555
  70.7 19.3 %all-to-all-start.1 = ((bf16[32,2,576]{2,1,0:T(2,128)(2,1)}), bf16[32,2,576]{2,1,0:T(2,128)(2,1)S(1)}, u32[]{:S(2)}, u32[]{:S(2)}) async-start(bf16[32,2,576]{2,1,0:T(2,128)(2,1)} %reshape.803), calls=%async_computation.1 | async-start | bytes 163840 | tf_op jit(solution)/shard_map/all_to_all | solution.py:560
  75.0 178.2 %all-gather.3.cloned.1.call-start = ((), (), s32[]{:S(2)}) async-start(), calls=%async_computation.9 | async-start | bytes 21897216 | tf_op jit(solution)/shard_map/all_gather | solution.py:710
  135.2 38.6 %collective-permute-start.7 = (bf16[576,1152]{1,0:T(8,128)(2,1)S(1)}, bf16[576,1152]{1,0:T(8,128)(2,1)S(1)}, u32[]{:S(2)}, u32[]{:S(2)}) collective-permute-start(bf16[576,1152]{1,0:T(8,128)(2,1)S(1)} %constant_dynamic-update-slice_fusion), channel_id=1, source_target_pairs={{0,4},{1,5},{2,6},{3,7},{4,0},{5,1},{6,2},{7,3},{8,12},{9,13},{10,... | collective-permute-start | bytes 3981320 | tf_op jit(solution)/shard_map/ppermute | solution.py:555
  175.8 31.4 %collective-permute-start.8 = (bf16[288,1152]{1,0:T(8,128)(2,1)S(1)}, bf16[288,1152]{1,0:T(8,128)(2,1)}, u32[]{:S(2)}, u32[]{:S(2)}) collective-permute-start(bf16[288,1152]{1,0:T(8,128)(2,1)S(1)} %reshape.761), channel_id=1, source_target_pairs={{0,2},{1,3},{2,0},{3,1},{4,6},{5,7},{6,4},{7,5},{8,10},{9,11},{10,... | collective-permute-start | bytes 1990664 | tf_op jit(solution)/shard_map/ppermute | solution.py:555
  214.5 21.0 %all-to-all-start.3 = ((bf16[4,4,80,288]{3,2,1,0:T(8,128)(2,1)}), bf16[4,4,80,288]{3,2,1,0:T(8,128)(2,1)S(1)}, u32[]{:S(2)}, u32[]{:S(2)}) async-start(bf16[4,4,80,288]{3,2,1,0:T(8,128)(2,1)} %shard_map.643), calls=%async_computation.3 | async-start | bytes 1966080 | tf_op jit(solution)/shard_map/all_to_all | solution.py:759
  305.0 19.6 %collective-permute-start.13 = (bf16[320,1152]{1,0:T(8,128)(2,1)}, bf16[320,1152]{1,0:T(8,128)(2,1)S(1)}, u32[]{:S(2)}, u32[]{:S(2)}) collective-permute-start(bf16[320,1152]{1,0:T(8,128)(2,1)} %get-tuple-element.101), channel_id=1, source_target_pairs={{0,1},{1,0},{2,3},{3,2},{4,5},{5,4},{6,7},{7,6},{8,9},{9,8},{10,11... | collective-permute-start | bytes 2211848 | tf_op jit(solution)/shard_map/ppermute | solution.py:555
  321.4 32.6 %collective-permute-start.16 = (bf16[2,288,1152]{2,1,0:T(8,128)(2,1)}, bf16[2,288,1152]{2,1,0:T(8,128)(2,1)}, u32[]{:S(2)}, u32[]{:S(2)}) collective-permute-start(bf16[2,288,1152]{2,1,0:T(8,128)(2,1)} %get-tuple-element.111), channel_id=1, source_target_pairs={{0,4},{1,5},{2,6},{3,7},{4,0},{5,1},{6,2},{7,3},{8,12},{9,13},{10,... | collective-permute-start | bytes 3981320 | tf_op jit(solution)/shard_map/ppermute | solution.py:555
  323.7 34.5 %collective-permute-start.15 = (bf16[2,288,1152]{2,1,0:T(8,128)(2,1)}, bf16[2,288,1152]{2,1,0:T(8,128)(2,1)}, u32[]{:S(2)}, u32[]{:S(2)}) collective-permute-start(bf16[2,288,1152]{2,1,0:T(8,128)(2,1)} %get-tuple-element.104), channel_id=1, source_target_pairs={{0,2},{1,3},{2,0},{3,1},{4,6},{5,7},{6,4},{7,5},{8,10},{9,11},{10,... | collective-permute-start | bytes 3981320 | tf_op jit(solution)/shard_map/ppermute | solution.py:555
  324.6 74.3 %collective-permute-start.18 = (bf16[2,288,1152]{2,1,0:T(8,128)(2,1)}, bf16[2,288,1152]{2,1,0:T(8,128)(2,1)}, u32[]{:S(2)}, u32[]{:S(2)}) collective-permute-start(bf16[2,288,1152]{2,1,0:T(8,128)(2,1)} %get-tuple-element.116), channel_id=1, source_target_pairs={{0,4},{1,5},{2,6},{3,7},{4,0},{5,1},{6,2},{7,3},{8,12},{9,13},{10,... | collective-permute-start | bytes 3981320 | tf_op jit(solution)/shard_map/ppermute | solution.py:555
  338.3 27.2 %all-to-all-start.4 = ((bf16[4,320,288]{1,2,0:T(8,128)(2,1)}), bf16[4,320,288]{1,2,0:T(8,128)(2,1)}, u32[]{:S(2)}, u32[]{:S(2)}) async-start(bf16[4,320,288]{1,2,0:T(8,128)(2,1)} %bitcast.41), calls=%async_computation.4 | async-start | bytes 1769472 | tf_op jit(solution)/shard_map/all_to_all | solution.py:759
  357.4 41.5 %collective-permute-start.19 = (bf16[2,288,1152]{2,1,0:T(8,128)(2,1)}, bf16[2,288,1152]{2,1,0:T(8,128)(2,1)}, u32[]{:S(2)}, u32[]{:S(2)}) collective-permute-start(bf16[2,288,1152]{2,1,0:T(8,128)(2,1)} %add_convert_fusion.3), channel_id=1, source_target_pairs={{0,2},{1,3},{2,0},{3,1},{4,6},{5,7},{6,4},{7,5},{8,10},{9,11},{10,... | collective-permute-start | bytes 3981320 | tf_op jit(solution)/shard_map/ppermute | solution.py:555
  396.0 90.4 %collective-permute-start.23 = (bf16[2,288,1152]{2,1,0:T(8,128)(2,1)}, bf16[2,288,1152]{2,1,0:T(8,128)(2,1)}, u32[]{:S(2)}, u32[]{:S(2)}) collective-permute-start(bf16[2,288,1152]{2,1,0:T(8,128)(2,1)} %add_convert_fusion.4), channel_id=1, source_target_pairs={{0,4},{1,5},{2,6},{3,7},{4,0},{5,1},{6,2},{7,3},{8,12},{9,13},{10,... | collective-permute-start | bytes 3981320 | tf_op jit(solution)/shard_map/ppermute | solution.py:555
  396.1 19.4 %collective-permute-start.21 = (bf16[288,1152]{1,0:T(8,128)(2,1)}, bf16[288,1152]{1,0:T(8,128)(2,1)}, u32[]{:S(2)}, u32[]{:S(2)}) collective-permute-start(bf16[288,1152]{1,0:T(8,128)(2,1)} %slice.483), channel_id=1, source_target_pairs={{0,2},{1,3},{2,0},{3,1},{4,6},{5,7},{6,4},{7,5},{8,10},{9,11},{10,... | collective-permute-start | bytes 1990664 | tf_op jit(solution)/shard_map/ppermute | solution.py:555
  403.1 83.3 %collective-permute-start.25 = (bf16[2,288,1152]{2,1,0:T(8,128)(2,1)}, bf16[2,288,1152]{2,1,0:T(8,128)(2,1)}, u32[]{:S(2)}, u32[]{:S(2)}) collective-permute-start(bf16[2,288,1152]{2,1,0:T(8,128)(2,1)} %add_convert_fusion.2), channel_id=1, source_target_pairs={{0,8},{1,9},{2,10},{3,11},{4,12},{5,13},{6,14},{7,15},{8,0},{9,1},... | collective-permute-start | bytes 3981320 | tf_op jit(solution)/shard_map/ppermute | solution.py:555
  409.4 20.6 %collective-permute-start.20 = (bf16[320,1152]{1,0:T(8,128)(2,1)}, bf16[320,1152]{1,0:T(8,128)(2,1)}, u32[]{:S(2)}, u32[]{:S(2)}) collective-permute-start(bf16[320,1152]{1,0:T(8,128)(2,1)} %slice.480), channel_id=1, source_target_pairs={{0,2},{1,3},{2,0},{3,1},{4,6},{5,7},{6,4},{7,5},{8,10},{9,11},{10,... | collective-permute-start | bytes 2211848 | tf_op jit(solution)/shard_map/ppermute | solution.py:555
  425.6 60.8 %collective-permute-start.24 = (bf16[2,288,1152]{2,1,0:T(8,128)(2,1)}, bf16[2,288,1152]{2,1,0:T(8,128)(2,1)}, u32[]{:S(2)}, u32[]{:S(2)}) collective-permute-start(bf16[2,288,1152]{2,1,0:T(8,128)(2,1)} %get-tuple-element.129), channel_id=1, source_target_pairs={{0,2},{1,3},{2,0},{3,1},{4,6},{5,7},{6,4},{7,5},{8,10},{9,11},{10,... | collective-permute-start | bytes 3981320 | tf_op jit(solution)/shard_map/ppermute | solution.py:555
  437.9 21.9 %all-to-all-start.5 = ((f32[32,4,288]{2,1,0:T(4,128)}), f32[32,4,288]{2,1,0:T(4,128)S(1)}, u32[]{:S(2)}, u32[]{:S(2)}) async-start(f32[32,4,288]{2,1,0:T(4,128)} %copy.293), calls=%async_computation.5 | async-start | bytes 393216 | tf_op jit(solution)/shard_map/all_to_all | solution.py:560
  442.5 38.3 %collective-permute-start.22 = (bf16[576,1152]{1,0:T(8,128)(2,1)}, bf16[576,1152]{1,0:T(8,128)(2,1)}, u32[]{:S(2)}, u32[]{:S(2)}) collective-permute-start(bf16[576,1152]{1,0:T(8,128)(2,1)} %bitcast.261), channel_id=1, source_target_pairs={{0,4},{1,5},{2,6},{3,7},{4,0},{5,1},{6,2},{7,3},{8,12},{9,13},{10,... | collective-permute-start | bytes 3981320 | tf_op jit(solution)/shard_map/ppermute | solution.py:555
  485.0 20.4 %collective-permute-start.26 = (bf16[288,1152]{1,0:T(8,128)(2,1)}, bf16[288,1152]{1,0:T(8,128)(2,1)}, u32[]{:S(2)}, u32[]{:S(2)}) collective-permute-start(bf16[288,1152]{1,0:T(8,128)(2,1)} %slice.482), channel_id=1, source_target_pairs={{0,8},{1,9},{2,10},{3,11},{4,12},{5,13},{6,14},{7,15},{8,0},{9,1},... | collective-permute-start | bytes 1990664 | tf_op jit(solution)/shard_map/ppermute | solution.py:555
  493.7 19.2 %all-to-all-start.7 = ((f32[32,1,2988]{2,1,0:T(1,128)}), f32[32,1,2988]{2,1,0:T(1,128)S(1)}, u32[]{:S(2)}, u32[]{:S(2)}) async-start(f32[32,1,2988]{2,1,0:T(1,128)} %copy.298), calls=%async_computation.7 | async-start | bytes 786432 | tf_op jit(solution)/shard_map/all_to_all | solution.py:560
  524.4 35.9 %collective-permute-start.31 = (bf16[2,144,1152]{2,1,0:T(8,128)(2,1)}, bf16[2,144,1152]{2,1,0:T(8,128)(2,1)}, u32[]{:S(2)}, u32[]{:S(2)}) collective-permute-start(bf16[2,144,1152]{2,1,0:T(8,128)(2,1)} %slice.481), channel_id=1, source_target_pairs={{0,16},{1,17},{2,18},{3,19},{4,20},{5,21},{6,22},{7,23},{8,24},{9,... | collective-permute-start | bytes 1990664 | tf_op jit(solution)/shard_map/ppermute | solution.py:555
  526.4 19.8 %collective-permute-start.28 = (f32[36,1152]{1,0:T(8,128)S(1)}, f32[36,1152]{1,0:T(8,128)S(1)}, u32[]{:S(2)}, u32[]{:S(2)}) collective-permute-start(f32[36,1152]{1,0:T(8,128)S(1)} %get-tuple-element.423), channel_id=1, source_target_pairs={{28,0},{0,1},{4,2},{1,3},{5,4},{10,5},{6,6},{14,7},{15,8},{11,9},{... | collective-permute-start | bytes 497672 | tf_op jit(solution)/shard_map/ppermute | solution.py:983
  (177 other events, 1237.3 us)
Sparse Core Ops, SparseCore 0:
  91.8 161.3 all-gather.2
